TPU v7x, 128 devices: a whole 4x4x4 slice. The times are simulated.
128 devices in a mesh: band: 8 (over z, core), patch: 16 (over y, x).
Axes of the slice: x: 4, y: 4, z: 4, core: 2. Of those that a mesh axis runs over, the one named last changes fastest.
Arguments:
- grid_latent: bfloat16 [16384, 512], P(('band', 'patch')), may hold values from -6 to 6
- mesh_latent: bfloat16 [16384, 512], P(('band', 'patch')), may hold values from -6 to 6
- weights: bfloat16 [20, 512, 512], replicated, may hold values from -0.25 to 0.25
- enc_dev: int32 [49152, 1], P(('band', 'patch')), may hold values from 0 to 127; in each aligned block of 384 rows (0 to 383, 384 to 767, ...) at most 6 rows name the same one
- enc_row: int32 [49152], P(('band', 'patch')), may hold values from 0 to 127
- enc_dst: int32 [49152], P(('band', 'patch')), may hold values from 0 to 127
- proc_dev: int32 [49152, 1], P(('band', 'patch')), may hold values from 0 to 127; in each aligned block of 384 rows (0 to 383, 384 to 767, ...) at most 6 rows name the same one
- proc_row: int32 [49152], P(('band', 'patch')), may hold values from 0 to 127
- proc_dst: int32 [49152], P(('band', 'patch')), may hold values from 0 to 127
- loc_src: int32 [32768], P(('band', 'patch')), may hold values from 0 to 127
- loc_dst: int32 [32768], P(('band', 'patch')), may hold values from 0 to 127
- dec_dev: int32 [49152, 1], P(('band', 'patch')), may hold values from 0 to 127; in each aligned block of 384 rows (0 to 383, 384 to 767, ...) at most 6 rows name the same one
- dec_row: int32 [49152], P(('band', 'patch')), may hold values from 0 to 127
Outputs:
- decoded: bfloat16 [16384, 512], P(('band', 'patch'))
Inputs may be any that keep to these rules, and one draw needn't show every extreme that they name: `enc_dev`: among the rows of one device, no device number appears more than 6 times. `proc_dev`: among the rows of one device, no device number appears more than 6 times. `dec_dev`: among the rows of one device, no device number appears more than 6 times.
All inputs are finite; a program needn't handle non-finite values.
Results may differ from a plain program's by a relative error of at most 0.013.
Values may be sent and summed in bfloat16 or wider, within the bound.
No kernel may reach another device: no remote copies, remote signals or barrier semaphores. Data moves between devices by JAX's collectives and lax.ppermute only.
A program may use at most 128 MiB of HBM per device.

v0:
```python
import jax
import jax.numpy as jnp
from jax import lax
from jax.sharding import PartitionSpec as P

epsilon = 1e-05


def layer_norm(values):
    average = jnp.mean(values, axis=-1, keepdims=True)
    centred = values - average
    spread = jnp.mean(centred * centred, axis=-1, keepdims=True)
    return centred * lax.rsqrt(spread + epsilon)


def perceptron(pieces, first_mats, second):
    summed = jnp.dot(pieces[0], first_mats[0], preferred_element_type=jnp.float32)
    for piece, matrix in zip(pieces[1:], first_mats[1:]):
        summed = summed + jnp.dot(piece, matrix, preferred_element_type=jnp.float32)
    hidden = jax.nn.silu(summed).astype(jnp.bfloat16)
    return layer_norm(jnp.dot(hidden, second, preferred_element_type=jnp.float32))


def residual_add(base, update):
    return (base.astype(jnp.float32) + update).astype(jnp.bfloat16)


def node_sums(messages, targets, node_count):
    matches = (jnp.arange(node_count, dtype=jnp.int32)[:, None] == targets[None, :]).astype(
        jnp.bfloat16
    )
    return jnp.dot(matches, messages, preferred_element_type=jnp.float32).astype(jnp.bfloat16)


def make_request(source_dev, src_row, capacity, devices):
    source_ids = source_dev[:, 0]
    matches = (source_ids[:, None] == jnp.arange(devices, dtype=jnp.int32)[None, :]).astype(
        jnp.int32
    )
    position = jnp.sum(jnp.cumsum(matches, axis=0) * matches, axis=1) - 1
    slot_index = source_ids * capacity + position
    request = jnp.zeros((devices * capacity,), jnp.int32).at[slot_index].set(src_row)
    return (slot_index, request.reshape(devices, capacity))


def send_back(rows_table, wanted):
    picked = jnp.take(rows_table, wanted, axis=0)
    received = lax.all_to_all(picked, ("band", "patch"), split_axis=0, concat_axis=0, tiled=True)
    return received


def pull_rows(rows_table, slot_index, request):
    devices = request.shape[0]
    capacity = request.shape[1]
    width = rows_table.shape[1]
    received = send_back(
        rows_table,
        lax.all_to_all(request, ("band", "patch"), split_axis=0, concat_axis=0, tiled=True),
    )
    return jnp.take(received.reshape(devices * capacity, width), slot_index, axis=0)


def body(
    grid_latent,
    mesh_latent,
    weights,
    enc_dev,
    enc_row,
    enc_dst,
    proc_dev,
    proc_row,
    proc_dst,
    loc_src,
    loc_dst,
    dec_dev,
    dec_row,
):
    devices = lax.axis_size("band") * lax.axis_size("patch")
    edge_count = enc_dev.shape[0]
    capacity = max(2, 2 * edge_count // devices)
    mesh_count = mesh_latent.shape[0]
    grid_count = grid_latent.shape[0]
    width = grid_latent.shape[1]
    sections = [make_request(enc_dev, enc_row, capacity, devices)]
    sections.append(make_request(proc_dev, proc_row, capacity, devices))
    sections.append(make_request(dec_dev, dec_row, capacity, devices))

    def mesh_sources(rows_table, index):
        return pull_rows(rows_table, sections[index][0], sections[index][1])

    enc_sources = pull_rows(grid_latent, sections[0][0], sections[0][1])
    enc_targets = jnp.take(mesh_latent, enc_dst, axis=0)
    enc_msg = perceptron((enc_sources, enc_targets), (weights[0], weights[1]), weights[2]).astype(
        jnp.bfloat16
    )
    enc_sum = node_sums(enc_msg, enc_dst, mesh_count)
    mesh_one = residual_add(
        mesh_latent, perceptron((mesh_latent, enc_sum), (weights[3], weights[4]), weights[5])
    )
    grid_one = residual_add(grid_latent, perceptron((grid_latent,), (weights[6],), weights[7]))
    far_sources = mesh_sources(mesh_one, 1)
    all_sources = jnp.concatenate([far_sources, jnp.take(mesh_one, loc_src, axis=0)], axis=0)
    all_targets = jnp.concatenate([proc_dst, loc_dst], axis=0)
    proc_msg = perceptron(
        (all_sources, jnp.take(mesh_one, all_targets, axis=0)),
        (weights[8], weights[9]),
        weights[10],
    ).astype(jnp.bfloat16)
    proc_sum = node_sums(proc_msg, all_targets, mesh_count)
    mesh_two = residual_add(
        mesh_one, perceptron((mesh_one, proc_sum), (weights[11], weights[12]), weights[13])
    )
    dec_sources = mesh_sources(mesh_two, 2)
    dec_targets = jnp.repeat(grid_one, 3, axis=0)
    dec_msg = perceptron(
        (dec_sources, dec_targets), (weights[14], weights[15]), weights[16]
    ).astype(jnp.bfloat16)
    dec_sum = jnp.sum(dec_msg.astype(jnp.float32).reshape(grid_count, 3, width), axis=1).astype(
        jnp.bfloat16
    )
    return residual_add(
        grid_one, perceptron((grid_one, dec_sum), (weights[17], weights[18]), weights[19])
    )


def solution(mesh):
    in_specs = (
        P(("band", "patch"), None),
        P(("band", "patch"), None),
        P(),
        P(("band", "patch"), None),
        P(("band", "patch")),
        P(("band", "patch")),
        P(("band", "patch"), None),
        P(("band", "patch")),
        P(("band", "patch")),
        P(("band", "patch")),
        P(("band", "patch")),
        P(("band", "patch"), None),
        P(("band", "patch")),
    )
    out_specs = P(("band", "patch"), None)
    return jax.shard_map(body, mesh=mesh, in_specs=in_specs, out_specs=out_specs, check_vma=False)
```

profile of v0, /device:TPU:1, one launch (start us, length us, event | category | flops | bytes accessed | tf_op | source)
XLA Modules:
  0.0 183.4 jit_solution(9420890933884074910)
XLA Ops:
  2.1 3.1 %scatter_custom_fusion = s32[768]{0:T(1024)S(1)} fusion(s32[384]{0:T(512)S(1)} %fusion.129, s32[384]{0:T(512)} %param.21, s32[]{:T(128)} %constant.108.clone.1), kind=kCustom, calls=%fused_computation.192 | custom fusion | bytes 3584 | tf_op jit(solution)/shard_map/scatter | solution.py:42
  6.0 11.5 %all-to-all-start = ((s32[128,1,6]{2,1,0:T(1,128)}), s32[128,1,6]{2,1,0:T(1,128)S(1)}, u32[]{:S(2)}, u32[]{:S(2)}) async-start(s32[128,1,6]{2,1,0:T(1,128)} %bitcast.12), calls=%async_computation | async-start | bytes 131072 | tf_op jit(solution)/shard_map/all_to_all | solution.py:58
  27.9 1.8 fusion.144
  30.6 2.1 %gather_fusion = bf16[384,512]{1,0:T(8,128)(2,1)S(1)} fusion(bf16[128,512]{1,0:T(8,128)(2,1)S(1)} %copy-done.1, s32[1024]{0:T(1024)S(1)} %pad_clamp_fusion.6), kind=kCustom, calls=%fused_computation.6 | custom fusion | bytes 787968 | tf_op jit(solution)/shard_map/jit(_take)/gather | solution.py:92
  32.7 3.1 %scatter_custom_fusion.1 = s32[768]{0:T(1024)S(1)} fusion(s32[384]{0:T(512)S(1)} %fusion.130, s32[384]{0:T(512)} %param.24, s32[]{:T(128)} %constant.108.clone.1), kind=kCustom, calls=%fused_computation.190 | custom fusion | bytes 3584 | tf_op jit(solution)/shard_map/scatter | solution.py:42
  36.5 3.1 %scatter_custom_fusion.2 = s32[768]{0:T(1024)S(1)} fusion(s32[384]{0:T(512)S(1)} %fusion.131, s32[384]{0:T(512)} %param.29, s32[]{:T(128)} %constant.108.clone.1), kind=kCustom, calls=%fused_computation.188 | custom fusion | bytes 3584 | tf_op jit(solution)/shard_map/scatter | solution.py:42
  40.4 9.8 %all-to-all-start.2 = ((s32[128,1,6]{2,1,0:T(1,128)}), s32[128,1,6]{2,1,0:T(1,128)S(1)}, u32[]{:S(2)}, u32[]{:S(2)}) async-start(s32[128,1,6]{2,1,0:T(1,128)} %bitcast.23), calls=%async_computation.2 | async-start | bytes 131072 | tf_op jit(solution)/shard_map/all_to_all | solution.py:58
  50.3 2.7 %gather_fusion.3 = bf16[768,512]{1,0:T(8,128)(2,1)S(1)} fusion(bf16[128,512]{1,0:T(8,128)(2,1)S(1)} %copy-done, s32[1024]{0:T(1024)S(1)} %pad_clamp_fusion.8), kind=kCustom, calls=%fused_computation.clone | custom fusion | bytes 1575936 | tf_op jit(solution)/shard_map/jit(_take)/gather | solution.py:47
  53.3 6.4 %all-to-all-done.2 = s32[128,1,6]{2,1,0:T(1,128)S(1)} async-done(((s32[128,1,6]{2,1,0:T(1,128)}), s32[128,1,6]{2,1,0:T(1,128)S(1)}, u32[]{:S(2)}, u32[]{:S(2)}) %all-to-all-start.2) | async-done | bytes 3104 | tf_op jit(solution)/shard_map/all_to_all | solution.py:58
  59.7 4.5 %all-to-all-start.4 = ((s32[128,1,6]{2,1,0:T(1,128)}), s32[128,1,6]{2,1,0:T(1,128)S(1)}, u32[]{:S(2)}, u32[]{:S(2)}) async-start(s32[128,1,6]{2,1,0:T(1,128)} %bitcast.6), calls=%async_computation.4 | async-start | bytes 131072 | tf_op jit(solution)/shard_map/all_to_all | solution.py:58
  65.4 8.4 %all-to-all-done.4 = s32[128,1,6]{2,1,0:T(1,128)S(1)} async-done(((s32[128,1,6]{2,1,0:T(1,128)}), s32[128,1,6]{2,1,0:T(1,128)S(1)}, u32[]{:S(2)}, u32[]{:S(2)}) %all-to-all-start.4) | async-done | bytes 3104 | tf_op jit(solution)/shard_map/all_to_all | solution.py:58
  73.8 4.5 %all-to-all-start.1 = ((bf16[128,6,512]{2,1,0:T(8,128)(2,1)}), bf16[128,6,512]{2,1,0:T(8,128)(2,1)S(1)}, u32[]{:S(2)}, u32[]{:S(2)}) async-start(bf16[128,6,512]{2,1,0:T(8,128)(2,1)} %broadcast_select_fusion.2), calls=%async_computation.1 | async-start | bytes 2097152 | tf_op jit(solution)/shard_map/all_to_all | solution.py:48
  78.6 18.5 %all-to-all-done.1 = bf16[128,6,512]{2,1,0:T(8,128)(2,1)S(1)} async-done(((bf16[128,6,512]{2,1,0:T(8,128)(2,1)}), bf16[128,6,512]{2,1,0:T(8,128)(2,1)S(1)}, u32[]{:S(2)}, u32[]{:S(2)}) %all-to-all-start.1) | async-done | bytes 786464 | tf_op jit(solution)/shard_map/all_to_all | solution.py:48
  97.4 2.1 %gather_fusion.4 = bf16[384,512]{1,0:T(8,128)(2,1)S(1)} fusion(bf16[768,512]{1,0:T(8,128)(2,1)S(1)} %reshape.305, s32[1024]{0:T(1024)S(1)} %pad_clamp_fusion.7), kind=kCustom, calls=%fused_computation.1.clone | custom fusion | bytes 787968 | tf_op jit(solution)/shard_map/jit(_take)/gather | solution.py:60
  99.4 1.5 fusion.39
  100.9 2.1 %fusion.147 = (f32[384]{0:T(512)S(1)}, f32[384,512]{1,0:T(8,128)S(1)}) fusion(bf16[20,512,512]{2,1,0:T(8,128)(2,1)} %param.19, f32[384,512]{1,0:T(8,128)S(1)} %fusion.39, bf16[384,512]{1,0:T(8,128)(2,1)S(1)} %gather_fusion, pred[384]{0:T(512)(128)(4,1)S(1)} %compare_and_fusion.8), kind=kOutput, calls=%fused_computation.226 | convolution fusion | flops 404225664 | bytes 3016576 | tf_op jit(solution)/shard_map/dot_general | solution.py:21
  103.2 1.6 multiply_convert_fusion.14
  106.6 2.7 %gather_fusion.5 = bf16[768,512]{1,0:T(8,128)(2,1)S(1)} fusion(bf16[128,512]{1,0:T(8,128)(2,1)S(1)} %add_convert_fusion.2, s32[1024]{0:T(1024)S(1)} %pad_clamp_fusion.5), kind=kCustom, calls=%fused_computation.2.clone | custom fusion | bytes 1575936 | tf_op jit(solution)/shard_map/jit(_take)/gather | solution.py:47
  110.7 4.7 %all-to-all-start.3 = ((bf16[128,6,512]{2,1,0:T(8,128)(2,1)}), bf16[128,6,512]{2,1,0:T(8,128)(2,1)S(1)}, u32[]{:S(2)}, u32[]{:S(2)}) async-start(bf16[128,6,512]{2,1,0:T(8,128)(2,1)} %broadcast_select_fusion.1), calls=%async_computation.3 | async-start | bytes 2097152 | tf_op jit(solution)/shard_map/all_to_all | solution.py:48
  116.7 2.8 %gather_fusion.2 = bf16[640,512]{1,0:T(8,128)(2,1)S(1)} fusion(bf16[128,512]{1,0:T(8,128)(2,1)S(1)} %add_convert_fusion.2, s32[1024]{0:T(1024)S(1)} %pad_clamp_fusion.2), kind=kCustom, calls=%fused_computation.8 | custom fusion | bytes 1313280 | tf_op jit(solution)/shard_map/jit(_take)/gather | solution.py:105
  121.6 12.8 %all-to-all-done.3 = bf16[128,6,512]{2,1,0:T(8,128)(2,1)S(1)} async-done(((bf16[128,6,512]{2,1,0:T(8,128)(2,1)}), bf16[128,6,512]{2,1,0:T(8,128)(2,1)S(1)}, u32[]{:S(2)}, u32[]{:S(2)}) %all-to-all-start.3) | async-done | bytes 786464 | tf_op jit(solution)/shard_map/all_to_all | solution.py:48
  134.7 2.1 %gather_fusion.6 = bf16[384,512]{1,0:T(8,128)(2,1)S(1)} fusion(bf16[768,512]{1,0:T(8,128)(2,1)S(1)} %reshape.307, s32[1024]{0:T(1024)S(1)} %pad_clamp_fusion.4), kind=kCustom, calls=%fused_computation.4.clone | custom fusion | bytes 787968 | tf_op jit(solution)/shard_map/jit(_take)/gather | solution.py:60
  136.9 2.7 %fusion.3 = f32[640,512]{1,0:T(8,128)} fusion(bf16[256,512]{1,0:T(8,128)(2,1)} %broadcast_select_fusion.4, bf16[384,512]{1,0:T(8,128)(2,1)S(1)} %broadcast_select_fusion.3, bf16[20,512,512]{2,1,0:T(8,128)(2,1)} %param.19), kind=kOutput, calls=%fused_computation.35 | convolution fusion | flops 336855040 | bytes 2490368 | tf_op jit(solution)/shard_map/dot_general | solution.py:17
  139.6 2.6 %fusion.153 = (f32[640]{0:T(1024)S(1)}, f32[640,512]{0,1:T(8,128)S(1)}) fusion(bf16[20,512,512]{2,1,0:T(8,128)(2,1)} %param.19, f32[640,512]{1,0:T(8,128)} %fusion.3, bf16[640,512]{1,0:T(8,128)(2,1)S(1)} %gather_fusion.2, pred[640]{0:T(1024)(128)(4,1)S(1)} %compare_and_fusion.3), kind=kOutput, calls=%fused_computation.228 | convolution fusion | flops 673709440 | bytes 4328576 | tf_op jit(solution)/shard_map/dot_general | solution.py:21
  142.4 1.6 multiply_convert_fusion.11
  145.7 2.7 %gather_fusion.7 = bf16[768,512]{1,0:T(8,128)(2,1)S(1)} fusion(bf16[128,512]{1,0:T(8,128)(2,1)S(1)} %add_convert_fusion.1, s32[1024]{0:T(1024)S(1)} %pad_clamp_fusion.1), kind=kCustom, calls=%fused_computation.3.clone | custom fusion | bytes 1575936 | tf_op jit(solution)/shard_map/jit(_take)/gather | solution.py:47
  149.9 4.7 %all-to-all-start.5 = ((bf16[128,6,512]{2,1,0:T(8,128)(2,1)}), bf16[128,6,512]{2,1,0:T(8,128)(2,1)S(1)}, u32[]{:S(2)}, u32[]{:S(2)}) async-start(bf16[128,6,512]{2,1,0:T(8,128)(2,1)} %broadcast_select_fusion), calls=%async_computation.5 | async-start | bytes 2097152 | tf_op jit(solution)/shard_map/all_to_all | solution.py:48
  156.5 17.0 %all-to-all-done.5 = bf16[128,6,512]{2,1,0:T(8,128)(2,1)S(1)} async-done(((bf16[128,6,512]{2,1,0:T(8,128)(2,1)}), bf16[128,6,512]{2,1,0:T(8,128)(2,1)S(1)}, u32[]{:S(2)}, u32[]{:S(2)}) %all-to-all-start.5) | async-done | bytes 786464 | tf_op jit(solution)/shard_map/all_to_all | solution.py:48
  173.8 2.1 %gather_fusion.8 = bf16[384,512]{1,0:T(8,128)(2,1)S(1)} fusion(bf16[768,512]{1,0:T(8,128)(2,1)S(1)} %reshape.309, s32[1024]{0:T(1024)S(1)} %pad_clamp_fusion), kind=kCustom, calls=%fused_computation.5.clone | custom fusion | bytes 787968 | tf_op jit(solution)/shard_map/jit(_take)/gather | solution.py:60
  175.9 1.5 fusion.22
  177.4 2.0 %fusion.159 = (f32[384]{0:T(512)S(1)}, f32[384,512]{1,0:T(8,128)S(1)}) fusion(bf16[20,512,512]{2,1,0:T(8,128)(2,1)} %param.19, f32[384,512]{1,0:T(8,128)S(1)} %fusion.22, bf16[384,512]{1,0:T(8,128)(2,1)S(1)} %reshape.310), kind=kOutput, calls=%fused_computation.230 | convolution fusion | flops 404029056 | bytes 3016192 | tf_op jit(solution)/shard_map/dot_general | solution.py:21
  180.7 1.7 fusion.162
  (118 shorter events, 32.6 us)
Async XLA Ops:
  0.0 30.6 %copy-start.1 = (bf16[128,512]{1,0:T(8,128)(2,1)S(1)}, bf16[128,512]{1,0:T(8,128)(2,1)}, u32[]{:S(2)}) copy-start(bf16[128,512]{1,0:T(8,128)(2,1)} %param.18) | copy-start | bytes 393220
  0.0 50.3 %copy-start = (bf16[128,512]{1,0:T(8,128)(2,1)S(1)}, bf16[128,512]{1,0:T(8,128)(2,1)}, u32[]{:S(2)}) copy-start(bf16[128,512]{1,0:T(8,128)(2,1)} %param.17) | copy-start | bytes 393220
  6.0 34.4 %all-to-all-start = ((s32[128,1,6]{2,1,0:T(1,128)}), s32[128,1,6]{2,1,0:T(1,128)S(1)}, u32[]{:S(2)}, u32[]{:S(2)}) async-start(s32[128,1,6]{2,1,0:T(1,128)} %bitcast.12), calls=%async_computation | async-start | bytes 131072 | tf_op jit(solution)/shard_map/all_to_all | solution.py:58
  40.4 19.4 %all-to-all-start.2 = ((s32[128,1,6]{2,1,0:T(1,128)}), s32[128,1,6]{2,1,0:T(1,128)S(1)}, u32[]{:S(2)}, u32[]{:S(2)}) async-start(s32[128,1,6]{2,1,0:T(1,128)} %bitcast.23), calls=%async_computation.2 | async-start | bytes 131072 | tf_op jit(solution)/shard_map/all_to_all | solution.py:58
  53.0 50.2 %copy-start.2 = (s32[384]{0:T(512)S(1)}, s32[384]{0:T(512)}, u32[]{:S(2)}) copy-start(s32[384]{0:T(512)} %param.22) | copy-start | bytes 4612
  59.7 14.1 %all-to-all-start.4 = ((s32[128,1,6]{2,1,0:T(1,128)}), s32[128,1,6]{2,1,0:T(1,128)S(1)}, u32[]{:S(2)}, u32[]{:S(2)}) async-start(s32[128,1,6]{2,1,0:T(1,128)} %bitcast.6), calls=%async_computation.4 | async-start | bytes 131072 | tf_op jit(solution)/shard_map/all_to_all | solution.py:58
  73.8 23.3 %all-to-all-start.1 = ((bf16[128,6,512]{2,1,0:T(8,128)(2,1)}), bf16[128,6,512]{2,1,0:T(8,128)(2,1)S(1)}, u32[]{:S(2)}, u32[]{:S(2)}) async-start(bf16[128,6,512]{2,1,0:T(8,128)(2,1)} %broadcast_select_fusion.2), calls=%async_computation.1 | async-start | bytes 2097152 | tf_op jit(solution)/shard_map/all_to_all | solution.py:48
  110.7 23.7 %all-to-all-start.3 = ((bf16[128,6,512]{2,1,0:T(8,128)(2,1)}), bf16[128,6,512]{2,1,0:T(8,128)(2,1)S(1)}, u32[]{:S(2)}, u32[]{:S(2)}) async-start(bf16[128,6,512]{2,1,0:T(8,128)(2,1)} %broadcast_select_fusion.1), calls=%async_computation.3 | async-start | bytes 2097152 | tf_op jit(solution)/shard_map/all_to_all | solution.py:48
  149.9 23.7 %all-to-all-start.5 = ((bf16[128,6,512]{2,1,0:T(8,128)(2,1)}), bf16[128,6,512]{2,1,0:T(8,128)(2,1)S(1)}, u32[]{:S(2)}, u32[]{:S(2)}) async-start(bf16[128,6,512]{2,1,0:T(8,128)(2,1)} %broadcast_select_fusion), calls=%async_computation.5 | async-start | bytes 2097152 | tf_op jit(solution)/shard_map/all_to_all | solution.py:48
where the time goes:
time: 185 us; the launch traced here: 183 us
  waiting for transfers between devices  63.1 us (34%)
  starting transfers between devices  39.7 us (21%)
  local copies, waits for them, and re-layouts  36.9 us (20%)
  matrix products  25.6 us (14%)
  other arithmetic  17.5 us (9%)
    all_to_all x3, waiting for transfers between devices, send_back(): lax.all_to_all(picked, ('band', 'patch'), split_axis=0, concat_axis=0, ti...  48.3 us
    all_to_all x3, starting transfers between devices, pull_rows(): lax.all_to_all(request, ('band', 'patch'), split_axis=0, concat_axis=0, t...  25.7 us
    all_to_all x3, waiting for transfers between devices, pull_rows(): lax.all_to_all(request, ('band', 'patch'), split_axis=0, concat_axis=0, t...  14.8 us
    all_to_all x3, starting transfers between devices, send_back(): lax.all_to_all(picked, ('band', 'patch'), split_axis=0, concat_axis=0, ti...  14 us
    dot_general x7, matrix products, perceptron(): jnp.dot(hidden, second, preferred_element_type=jnp.float32)  12.9 us
    dot_general x6, matrix products, perceptron(): jnp.dot(pieces[0], first_mats[0], preferred_element_type=jnp.float32)  9.48 us
    scatter x3, local copies, waits for them, and re-layouts, make_request(): jnp.zeros((devices * capacity,), jnp.int32).at[slot_index].set(src_row)  9.24 us
    gather x6, local copies, waits for them, and re-layouts, send_back(): picked = jnp.take(rows_table, wanted, axis=0)  8.82 us
  transfers between devices with their start and end apart: 6, of which 5 were waited for; matrix products, arithmetic and copies ran while one was open for 18% of the time, Pallas kernels for 0%

commit v1 on v0

v1 whole, which is shorter than its diff:
```python
import functools

import jax
import jax.numpy as jnp
from jax import lax
from jax.experimental import pallas as pl
from jax.experimental.pallas import tpu as pltpu
from jax.sharding import PartitionSpec as P

AXES = ("band", "patch")
EPSILON = 1e-05
BF = jnp.bfloat16
F32 = jnp.float32
I32 = jnp.int32


def dot(a, b):
    return jnp.dot(a, b, preferred_element_type=F32)


def dot_rows(a, b):
    return lax.dot_general(a, b, (((0,), (0,)), ((), ())), preferred_element_type=F32)


def dot_lanes(a, b):
    return lax.dot_general(a, b, (((1,), (1,)), ((), ())), preferred_element_type=F32)


def iota(shape, axis):
    return lax.broadcasted_iota(I32, shape, axis)


def flag(condition):
    return jnp.where(condition, 1.0, 0.0).astype(BF)


def column(row):
    count = row.shape[1]
    same = iota((count, count), 0) == iota((count, count), 1)
    return jnp.sum(jnp.where(same, row.astype(F32), 0.0), axis=1, keepdims=True).astype(I32)


def choose(row, count):
    edges = row.shape[1]
    return flag(iota((edges, count), 1) == column(row))


def choose_t(row, count):
    return flag(iota((count, row.shape[1]), 0) == row)


def silu(v):
    return 0.5 * v * (1.0 + jnp.tanh(0.5 * v))


def finish(summed, second):
    out = dot(silu(summed).astype(BF), second)
    centred = out - jnp.mean(out, axis=-1, keepdims=True)
    spread = jnp.mean(centred * centred, axis=-1, keepdims=True)
    return centred * lax.rsqrt(spread + EPSILON)


def residual(base, update):
    return (base.astype(F32) + update).astype(BF)


def spread_rows(chosen, values):
    high = values.astype(BF)
    low = (values - high.astype(F32)).astype(BF)
    return dot(jnp.concatenate([chosen, chosen], axis=1), jnp.concatenate([high, low], axis=0))


def wanted_rows(wanted, kind, cap):
    devices, lanes = wanted.shape
    total = devices * cap
    row = iota((total, 1), 0)
    owner = jnp.floor((row.astype(F32) + 0.5) * (1.0 / cap)).astype(I32)
    slot = row - owner * cap
    expand = flag(iota((total, devices), 1) == owner)
    values = dot(expand, wanted.astype(F32).astype(BF))
    own = jnp.where(iota((total, lanes), 1) == slot + kind * cap, values, 0.0).astype(BF)
    index = dot(own, jnp.ones((lanes, lanes), BF))
    return flag(iota((total, lanes), 1).astype(F32) == index)


def ask_kernel(cap, devices, dev0, row0, dev1, row1, dev2, row2, request, slots):
    edges = dev0.shape[1]
    earlier = flag(iota((edges, edges), 0) < iota((edges, edges), 1))
    total = jnp.zeros(request.shape, F32)
    for kind, (dev, row) in enumerate(((dev0, row0), (dev1, row1), (dev2, row2))):
        source = dev[...]
        hit = iota((devices, edges), 0) == source
        hits = flag(hit)
        before = dot(hits, earlier)
        place = jnp.sum(jnp.where(hit, before, 0.0), axis=0, keepdims=True).astype(I32)
        mine = iota((request.shape[1], edges), 0) == place + kind * cap
        total = total + dot_lanes(hits, jnp.where(mine, row[...].astype(F32), 0.0).astype(BF))
        slots[kind : kind + 1, :] = source * cap + place
    request[...] = total.astype(I32)


def first_kernel(cap, devices, grid, mesh, w1, w3, w6, w7, slots, enc_dst, grid_one, target, base, pick):
    grid_one[...] = residual(grid[...], finish(dot(grid[...], w6[...]), w7[...]))
    target[...] = spread_rows(choose(enc_dst[...], mesh.shape[0]), dot(mesh[...], w1[...]))
    base[...] = dot(mesh[...], w3[...])
    pick[...] = choose(slots[0:1, :], devices * cap)


def serve_kernel(cap, wanted, table, out):
    out[...] = dot(wanted_rows(wanted[...], 0, cap), table[...]).astype(BF)


def plan_kernel(cap, devices, wanted, slots, hot1, hot2, pick1, pick2):
    hot1[...] = wanted_rows(wanted[...], 1, cap)
    hot2[...] = wanted_rows(wanted[...], 2, cap)
    pick1[...] = choose(slots[1:2, :], devices * cap)
    pick2[...] = choose(slots[2:3, :], devices * cap)


def enc_kernel(received, pick, target, base, mesh, dst, hot, w0, w2, w4, w5, mesh_one, out):
    source = dot(pick[...], received[...]).astype(BF)
    message = finish(dot(source, w0[...]) + target[...], w2[...]).astype(BF)
    summed = dot(choose_t(dst[...], mesh.shape[0]), message).astype(BF)
    update = finish(base[...] + dot(summed, w4[...]), w5[...])
    one = residual(mesh[...], update)
    mesh_one[...] = one
    out[...] = dot(hot[...], one).astype(BF)


def local_kernel(mesh_one, w8, w9, w10, w11, loc_src, loc_dst, proc_dst, target, base, partial):
    one = mesh_one[...]
    count = one.shape[0]
    ends = dot(one, w9[...])
    target[...] = spread_rows(choose(proc_dst[...], count), ends)
    base[...] = dot(one, w11[...])
    start = spread_rows(choose(loc_src[...], count), dot(one, w8[...]))
    both = start + spread_rows(choose(loc_dst[...], count), ends)
    message = finish(both, w10[...]).astype(BF)
    partial[...] = dot(choose_t(loc_dst[...], count), message)


def proc_kernel(received, pick, target, base, partial, mesh_one, dst, hot, w8, w10, w12, w13, out):
    source = dot(pick[...], received[...]).astype(BF)
    message = finish(dot(source, w8[...]) + target[...], w10[...]).astype(BF)
    summed = (partial[...] + dot(choose_t(dst[...], mesh_one.shape[0]), message)).astype(BF)
    update = finish(base[...] + dot(summed, w12[...]), w13[...])
    two = residual(mesh_one[...], update)
    out[...] = dot(hot[...], two).astype(BF)


def last_kernel(grid_one, w15, w17, target, base):
    one = grid_one[...]
    rows = target.shape[0]
    near = iota((rows, one.shape[0]), 0) - 3 * iota((rows, one.shape[0]), 1)
    target[...] = spread_rows(flag((near >= 0) & (near < 3)), dot(one, w15[...]))
    base[...] = dot(one, w17[...])


def dec_kernel(received, pick, target, base, grid_one, w14, w16, w18, w19, out):
    source = dot(pick[...], received[...]).astype(BF)
    message = finish(dot(source, w14[...]) + target[...], w16[...]).astype(BF)
    shape = (grid_one.shape[0], target.shape[0])
    near = iota(shape, 1) - 3 * iota(shape, 0)
    summed = dot(flag((near >= 0) & (near < 3)), message).astype(BF)
    update = finish(base[...] + dot(summed, w18[...]), w19[...])
    out[...] = residual(grid_one[...], update)


def run(kernel, outs, *args, macs=0):
    spec = pl.BlockSpec(memory_space=pltpu.VMEM)
    moved = sum(a.size * a.dtype.itemsize for a in list(args) + list(outs))
    result = pl.pallas_call(
        kernel,
        out_shape=tuple(outs),
        in_specs=[spec] * len(args),
        out_specs=tuple(spec for _ in outs),
        compiler_params=pltpu.CompilerParams(vmem_limit_bytes=32 * 2**20),
        cost_estimate=pl.CostEstimate(flops=2 * macs, bytes_accessed=moved, transcendentals=0),
    )(*args)
    return result


def exchange(rows, cap):
    total, width = rows.shape
    parts = rows.reshape(total // cap, cap * width // 128, 128)
    moved = lax.all_to_all(parts, AXES, split_axis=0, concat_axis=0, tiled=True)
    return moved.reshape(total, width)


def body(
    grid_latent,
    mesh_latent,
    weights,
    enc_dev,
    enc_row,
    enc_dst,
    proc_dev,
    proc_row,
    proc_dst,
    loc_src,
    loc_dst,
    dec_dev,
    dec_row,
):
    devices = lax.axis_size("band") * lax.axis_size("patch")
    edges = enc_dev.shape[0]
    cap = max(2, 2 * edges // devices)
    count, width = mesh_latent.shape
    w = [weights[k] for k in range(weights.shape[0])]

    def line(values):
        return values.reshape(1, values.size)

    def arr(shape, dtype):
        return jax.ShapeDtypeStruct(shape, dtype)

    lanes = 128
    total = devices * cap
    request, slots = run(
        functools.partial(ask_kernel, cap, devices),
        (arr((devices, lanes), I32), arr((8, edges), I32)),
        line(enc_dev), line(enc_row), line(proc_dev), line(proc_row), line(dec_dev), line(dec_row),
        macs=3 * devices * edges * (edges + lanes),
    )
    asked = request.reshape(devices, 1, lanes)
    wanted = lax.all_to_all(asked, AXES, split_axis=0, concat_axis=0, tiled=True).reshape(devices, lanes)
    grid_one, enc_target, enc_base, enc_pick = run(
        functools.partial(first_kernel, cap, devices),
        (arr(grid_latent.shape, BF), arr((edges, width), F32), arr((count, width), F32), arr((edges, total), BF)),
        grid_latent, mesh_latent, w[1], w[3], w[6], w[7], slots, line(enc_dst),
        macs=7 * count * width * width,
    )
    (served,) = run(
        functools.partial(serve_kernel, cap),
        (arr((total, width), BF),),
        wanted, grid_latent,
        macs=total * count * (width + 2 * count),
    )
    enc_rows = exchange(served, cap)
    hot1, hot2, proc_pick, dec_pick = run(
        functools.partial(plan_kernel, cap, devices),
        (arr((total, count), BF), arr((total, count), BF), arr((edges, total), BF), arr((edges, total), BF)),
        wanted, slots,
        macs=4 * total * count * count,
    )
    mesh_one, served = run(
        enc_kernel,
        (arr(mesh_latent.shape, BF), arr((total, width), BF)),
        enc_rows, enc_pick, enc_target, enc_base, mesh_latent, line(enc_dst), hot1, w[0], w[2], w[4], w[5],
        macs=edges * width * (total + 3 * width),
    )
    proc_rows = exchange(served, cap)
    proc_target, proc_base, partial = run(
        local_kernel,
        (arr((edges, width), F32), arr((count, width), F32), arr((count, width), F32)),
        mesh_one, w[8], w[9], w[10], w[11], line(loc_src), line(loc_dst), line(proc_dst),
        macs=7 * count * width * width,
    )
    (served,) = run(
        proc_kernel,
        (arr((total, width), BF),),
        proc_rows, proc_pick, proc_target, proc_base, partial, mesh_one, line(proc_dst), hot2, w[8], w[10], w[12], w[13],
        macs=edges * width * (total + 3 * width),
    )
    dec_rows = exchange(served, cap)
    dec_target, dec_base = run(
        last_kernel,
        (arr((edges, width), F32), arr((count, width), F32)),
        grid_one, w[15], w[17],
        macs=4 * count * width * width,
    )
    (decoded,) = run(
        dec_kernel,
        (arr(grid_latent.shape, BF),),
        dec_rows, dec_pick, dec_target, dec_base, grid_one, w[14], w[16], w[18], w[19],
        macs=edges * width * (total + 3 * width),
    )
    return decoded


def solution(mesh):
    rows = P(AXES, None)
    edge = P(AXES)
    in_specs = (rows, rows, P(), rows, edge, edge, rows, edge, edge, edge, edge, rows, edge)
    return jax.shard_map(body, mesh=mesh, in_specs=in_specs, out_specs=rows, check_vma=False)
```

time: 185 us -> 132 us (0.71)
  waiting for transfers between devices: 63.1 us -> 26.6 us
  matrix products: 25.6 us -> 0 us
  starting transfers between devices: 39.7 us -> 18.5 us
  blocking collectives: 0 us -> 20.9 us
  other arithmetic: 17.5 us -> 0 us
  local copies, waits for them, and re-layouts: 36.9 us -> 52.5 us
  Pallas kernels: 0 us -> 11.7 us
    all_to_all x6 -> x3, waiting for transfers between devices: 63.1 us -> 26.6 us  [exchange(): moved = lax.all_to_all(parts, AXES, split_axis=0, concat_axis=0, tiled=True)]
    unnamed x7 -> x86, local copies, waits for them, and re-layouts: 0.7 us -> 33.6 us
    dot_general x15 -> x0, matrix products: 25.6 us -> none  [the longest x7 12.9 us: perceptron(): jnp.dot(hidden, second, preferred_element_type=jnp.float32)]
    all_to_all x6 -> x3, starting transfers between devices: 39.7 us -> 18.5 us  [exchange(): moved = lax.all_to_all(parts, AXES, split_axis=0, concat_axis=0, tiled=True)]
    gather x12 -> x0, local copies, waits for them, and re-layouts: 21 us -> none  [the longest x6 8.82 us: send_back(): picked = jnp.take(rows_table, wanted, axis=0)]
    all_to_all x0 -> x1, blocking collectives: none -> 20.9 us  [body(): lax.all_to_all(asked, AXES, split_axis=0, concat_axis=0, tiled=True)]
    pallas_call x0 -> x9, Pallas kernels: none -> 11.7 us  [run(): pl.pallas_call(kernel, out_shape=tuple(outs), in_specs=[spec] * len(args)...]
    reshape x5 -> x11, local copies, waits for them, and re-layouts: 1.33 us -> 11.3 us  [the longest x3 5.01 us: exchange(): parts = rows.reshape(total // cap, cap * width // 128, 128)]
  transfers between devices with their start and end apart: 6 -> 3, of which waited for: 5 -> 3; matrix products, arithmetic and copies ran while one was open for 18% -> 6% of each run, Pallas kernels for 0% -> 3%
where the time goes in v1:
time: 132 us; the launch traced here: 131 us
  local copies, waits for them, and re-layouts  52.5 us (40%)
  waiting for transfers between devices  26.6 us (20%)
  blocking collectives  20.9 us (16%)
  starting transfers between devices  18.5 us (14%)
  Pallas kernels  11.7 us (9%)
    unnamed x86, local copies, waits for them, and re-layouts  33.6 us
    all_to_all x3, waiting for transfers between devices, exchange(): moved = lax.all_to_all(parts, AXES, split_axis=0, concat_axis=0, tiled=True)  26.6 us
    all_to_all x1, blocking collectives, body(): lax.all_to_all(asked, AXES, split_axis=0, concat_axis=0, tiled=True)  20.9 us
    all_to_all x3, starting transfers between devices, exchange(): moved = lax.all_to_all(parts, AXES, split_axis=0, concat_axis=0, tiled=True)  18.5 us
    pallas_call x9, Pallas kernels, run(): pl.pallas_call(kernel, out_shape=tuple(outs), in_specs=[spec] * len(args)...  11.7 us
    squeeze x2, local copies, waits for them, and re-layouts, body(): w = [weights[k] for k in range(weights.shape[0])]  7.58 us
    reshape x3, local copies, waits for them, and re-layouts, exchange(): parts = rows.reshape(total // cap, cap * width // 128, 128)  5.01 us
    reshape x3, local copies, waits for them, and re-layouts, exchange(): return moved.reshape(total, width)  3.59 us
  transfers between devices with their start and end apart: 3, of which 3 were waited for; matrix products, arithmetic and copies ran while one was open for 6% of the time, Pallas kernels for 3%

profile of v1, /device:TPU:1, one launch (start us, length us, event | category | flops | bytes accessed | tf_op | source)
XLA Modules:
  0.0 130.5 jit_solution(12480475151538853462)
XLA Ops:
  4.8 20.9 %all_to_all.20 = s32[128,1,128]{2,1,0:T(1,128)S(1)} all-to-all(s32[128,1,128]{2,1,0:T(1,128)S(1)} %bitcast.51), channel_id=1, replica_groups=mesh['band'=8,'patch'=16] {'band','patch'}, dimensions={0} | all-to-all | bytes 131072 | tf_op jit(solution)/shard_map/all_to_all | solution.py:226
  27.2 1.4 %reshape.64 = bf16[128,24,128]{2,1,0:T(8,128)(2,1)} reshape(bf16[768,512]{1,0:T(8,128)(2,1)S(1)} %shard_map.128) | data formatting | bytes 1572864 | tf_op jit(solution)/shard_map/reshape | solution.py:185
  28.6 5.5 %all-to-all-start.1 = ((bf16[128,24,128]{2,1,0:T(8,128)(2,1)}), bf16[128,24,128]{2,1,0:T(8,128)(2,1)}, u32[]{:S(2)}, u32[]{:S(2)}) async-start(bf16[128,24,128]{2,1,0:T(8,128)(2,1)} %reshape.64), calls=%async_computation.1 | async-start | bytes 1572864 | tf_op jit(solution)/shard_map/all_to_all | solution.py:186
  34.8 6.5 %slice_bitcast_fusion = (bf16[512,512]{1,0:T(8,128)(2,1)S(1)}, bf16[512,512]{1,0:T(8,128)(2,1)}, bf16[512,512]{1,0:T(8,128)(2,1)}, bf16[512,512]{1,0:T(8,128)(2,...) fusion(bf16[20,512,512]{2,1,0:T(8,128)(2,1)} %param.15), kind=kLoop, calls=%fused_computation | loop fusion | bytes 19922944 | tf_op jit(solution)/shard_map/squeeze | solution.py:209
  48.1 2.3 %all-to-all-done.1 = bf16[128,24,128]{2,1,0:T(8,128)(2,1)} async-done(((bf16[128,24,128]{2,1,0:T(8,128)(2,1)}), bf16[128,24,128]{2,1,0:T(8,128)(2,1)}, u32[]{:S(2)}, u32[]{:S(2)}) %all-to-all-start.1) | async-done | bytes 786464 | tf_op jit(solution)/shard_map/all_to_all | solution.py:186
  50.5 1.6 %reshape.65.received = bf16[768,512]{1,0:T(8,128)(2,1)S(1)} reshape(bf16[128,24,128]{2,1,0:T(8,128)(2,1)} %all-to-all-done.1) | data formatting | bytes 1572864 | tf_op jit(solution)/shard_map/reshape | solution.py:187
  52.1 1.0 copy-done.7
  53.1 1.0 copy-done.8
  54.1 1.0 copy-done.9
  55.2 1.0 copy-done.10
  56.2 1.1 copy-done.15
  60.1 2.2 %shard_map.131 = (bf16[128,512]{1,0:T(8,128)(2,1)S(1)}, bf16[768,512]{1,0:T(8,128)(2,1)S(1)}) custom-call(bf16[768,512]{1,0:T(8,128)(2,1)S(1)} %reshape.65.received, bf16[384,768]{1,0:T(8,128)(2,1)S(1)} %get-tuple-element.24.pick, f32[384,512]{1,0:T(8,128)S(1)} %copy-done.15, f32[128,512]{1,0:T(8,128)S(1)} %copy-done.30, bf16[128,512]{1,0:T(8,128)(2,1)S(1)} %copy-done.23, ...), custom_call_target="tpu_custom_call" | custom-call | flops 905969664 | bytes 5768704 | tf_op jit(solution)/shard_map/pallas_call | solution.py:172
  63.9 2.3 %reshape.67 = bf16[128,24,128]{2,1,0:T(8,128)(2,1)} reshape(bf16[768,512]{1,0:T(8,128)(2,1)} %copy-done.13) | data formatting | bytes 1572864 | tf_op jit(solution)/shard_map/reshape | solution.py:185
  66.2 7.6 %all-to-all-start.2 = ((bf16[128,24,128]{2,1,0:T(8,128)(2,1)}), bf16[128,24,128]{2,1,0:T(8,128)(2,1)S(1)}, u32[]{:S(2)}, u32[]{:S(2)}) async-start(bf16[128,24,128]{2,1,0:T(8,128)(2,1)} %reshape.67), calls=%async_computation.2 | async-start | bytes 1572864 | tf_op jit(solution)/shard_map/all_to_all | solution.py:186
  73.8 1.0 copy-done.6
  75.8 1.4 %shard_map.132 = (f32[384,512]{1,0:T(8,128)S(1)}, f32[128,512]{1,0:T(8,128)S(1)}, f32[128,512]{1,0:T(8,128)S(1)}) custom-call(bf16[128,512]{1,0:T(8,128)(2,1)S(1)} %copy-done.27, bf16[512,512]{1,0:T(8,128)(2,1)S(1)} %get-tuple-element.49.w8, bf16[512,512]{1,0:T(8,128)(2,1)S(1)} %copy-done.6, bf16[512,512]{1,0:T(8,128)(2,1)S(1)} %get-tuple-element.47.w10, ...), custom_call_target="tpu_custom_call" | custom-call | flops 469762048 | bytes 3542528 | tf_op jit(solution)/shard_map/pallas_call | solution.py:172
  78.8 11.6 %all-to-all-done.2 = bf16[128,24,128]{2,1,0:T(8,128)(2,1)S(1)} async-done(((bf16[128,24,128]{2,1,0:T(8,128)(2,1)}), bf16[128,24,128]{2,1,0:T(8,128)(2,1)S(1)}, u32[]{:S(2)}, u32[]{:S(2)}) %all-to-all-start.2) | async-done | bytes 786464 | tf_op jit(solution)/shard_map/all_to_all | solution.py:186
  90.8 1.0 copy-done.2
  91.9 1.0 copy-done.3
  92.9 1.1 copy-done.12
  94.0 1.1 copy-done.19
  97.9 2.2 %shard_map.133 = bf16[768,512]{1,0:T(8,128)(2,1)S(1)} custom-call(bf16[768,512]{1,0:T(8,128)(2,1)S(1)} %reshape.68.received, bf16[384,768]{1,0:T(8,128)(2,1)S(1)} %copy-done.19, f32[384,512]{1,0:T(8,128)S(1)} %copy-done.12, f32[128,512]{1,0:T(8,128)S(1)} %get-tuple-element.32.base, f32[128,512]{1,0:T(8,128)S(1)} %copy-done.32, ...), custom_call_target="tpu_custom_call" | custom-call | flops 905969664 | bytes 5899776 | tf_op jit(solution)/shard_map/pallas_call | solution.py:172
  100.1 1.4 %reshape.72 = bf16[128,24,128]{2,1,0:T(8,128)(2,1)} reshape(bf16[768,512]{1,0:T(8,128)(2,1)S(1)} %shard_map.133) | data formatting | bytes 1572864 | tf_op jit(solution)/shard_map/reshape | solution.py:185
  101.4 5.4 %all-to-all-start.3 = ((bf16[128,24,128]{2,1,0:T(8,128)(2,1)}), bf16[128,24,128]{2,1,0:T(8,128)(2,1)}, u32[]{:S(2)}, u32[]{:S(2)}) async-start(bf16[128,24,128]{2,1,0:T(8,128)(2,1)} %reshape.72), calls=%async_computation.3 | async-start | bytes 1572864 | tf_op jit(solution)/shard_map/all_to_all | solution.py:186
  107.9 1.0 copy-done.5
  109.5 1.1 slice_bitcast_fusion.1.w18
  110.6 12.7 %all-to-all-done.3 = bf16[128,24,128]{2,1,0:T(8,128)(2,1)} async-done(((bf16[128,24,128]{2,1,0:T(8,128)(2,1)}), bf16[128,24,128]{2,1,0:T(8,128)(2,1)}, u32[]{:S(2)}, u32[]{:S(2)}) %all-to-all-start.3) | async-done | bytes 786464 | tf_op jit(solution)/shard_map/all_to_all | solution.py:186
  123.3 1.6 %reshape.73.received = bf16[768,512]{1,0:T(8,128)(2,1)S(1)} reshape(bf16[128,24,128]{2,1,0:T(8,128)(2,1)} %all-to-all-done.3) | data formatting | bytes 1572864 | tf_op jit(solution)/shard_map/reshape | solution.py:187
  124.9 1.0 copy-done
  125.9 1.0 copy-done.1
  126.9 1.1 copy-done.17
  128.0 2.5 %shard_map.135 = bf16[128,512]{1,0:T(8,128)(2,1)} custom-call(bf16[768,512]{1,0:T(8,128)(2,1)S(1)} %reshape.73.received, bf16[384,768]{1,0:T(8,128)(2,1)S(1)} %copy-done.17, f32[384,512]{1,0:T(8,128)S(1)} %get-tuple-element.37.target, f32[128,512]{1,0:T(8,128)S(1)} %get-tuple-element.38.base, bf16[128,512]{1,0:T(8,128)(2,1)S(1)} %copy-done.25, ...), custom_call_target="tpu_custom_call" | custom-call | flops 905969664 | bytes 4784128 | tf_op jit(solution)/shard_map/pallas_call | solution.py:172
  (83 shorter events, 25.5 us)
Async XLA Ops:
  25.7 0.9 copy-start.20
  28.6 12.8 %copy-start.21 = (bf16[128,512]{1,0:T(8,128)(2,1)S(1)}, bf16[128,512]{1,0:T(8,128)(2,1)}, u32[]{:S(2)}) copy-start(bf16[128,512]{1,0:T(8,128)(2,1)} %grid.1) | copy-start | bytes 393220
  28.6 12.8 %copy-start.22 = (bf16[128,512]{1,0:T(8,128)(2,1)S(1)}, bf16[128,512]{1,0:T(8,128)(2,1)}, u32[]{:S(2)}) copy-start(bf16[128,512]{1,0:T(8,128)(2,1)} %mesh.3) | copy-start | bytes 393220
  28.6 21.9 %all-to-all-start.1 = ((bf16[128,24,128]{2,1,0:T(8,128)(2,1)}), bf16[128,24,128]{2,1,0:T(8,128)(2,1)}, u32[]{:S(2)}, u32[]{:S(2)}) async-start(bf16[128,24,128]{2,1,0:T(8,128)(2,1)} %reshape.64), calls=%async_computation.1 | async-start | bytes 1572864 | tf_op jit(solution)/shard_map/all_to_all | solution.py:186
  41.3 32.5 %copy-start.42 = (s32[384]{0:T(512)S(1)}, s32[384]{0:T(512)}, u32[]{:S(2)}) copy-start(s32[384]{0:T(512)} %param.21) | copy-start | bytes 4612
  41.3 32.5 %copy-start.37 = (s32[256]{0:T(256)S(1)}, s32[256]{0:T(256)}, u32[]{:S(2)}) copy-start(s32[256]{0:T(256)} %param.22) | copy-start | bytes 3076
  41.3 32.5 %copy-start.38 = (s32[256]{0:T(256)S(1)}, s32[256]{0:T(256)}, u32[]{:S(2)}) copy-start(s32[256]{0:T(256)} %param.23) | copy-start | bytes 3076
  52.1 1.0 copy-start.7
  53.1 1.0 copy-start.8
  54.1 1.0 copy-start.9
  55.2 1.0 copy-start.10
  56.2 1.1 copy-start.15
  57.4 0.9 copy-start.23
  58.3 0.9 copy-start.30
  59.2 0.9 copy-start.36
  63.9 43.0 %copy-start.25 = (bf16[128,512]{1,0:T(8,128)(2,1)S(1)}, bf16[128,512]{1,0:T(8,128)(2,1)}, u32[]{:S(2)}) copy-start(bf16[128,512]{1,0:T(8,128)(2,1)} %copy-done.24) | copy-start | bytes 393220
  66.2 24.1 %all-to-all-start.2 = ((bf16[128,24,128]{2,1,0:T(8,128)(2,1)}), bf16[128,24,128]{2,1,0:T(8,128)(2,1)S(1)}, u32[]{:S(2)}, u32[]{:S(2)}) async-start(bf16[128,24,128]{2,1,0:T(8,128)(2,1)} %reshape.67), calls=%async_computation.2 | async-start | bytes 1572864 | tf_op jit(solution)/shard_map/all_to_all | solution.py:186
  73.8 1.0 copy-start.6
  74.9 0.9 copy-start.27
  90.8 1.0 copy-start.2
  91.9 1.0 copy-start.3
  92.9 1.1 copy-start.12
  94.0 1.1 copy-start.19
  95.1 0.9 copy-start.28
  96.0 0.9 copy-start.32
  97.0 0.9 copy-start.34
  101.4 21.8 %all-to-all-start.3 = ((bf16[128,24,128]{2,1,0:T(8,128)(2,1)}), bf16[128,24,128]{2,1,0:T(8,128)(2,1)}, u32[]{:S(2)}, u32[]{:S(2)}) async-start(bf16[128,24,128]{2,1,0:T(8,128)(2,1)} %reshape.72), calls=%async_computation.3 | async-start | bytes 1572864 | tf_op jit(solution)/shard_map/all_to_all | solution.py:186
  106.9 1.0 copy-start.4
  107.9 1.0 copy-start.5
  124.8 1.0 copy-start
  125.9 1.0 copy-start.1
  126.9 1.1 copy-start.17
  (14 other events, 10.4 us)

commit v2 on v1

v2 whole, which is shorter than its diff:
```python
import functools

import jax
import jax.numpy as jnp
from jax import lax
from jax.experimental import pallas as pl
from jax.experimental.pallas import tpu as pltpu
from jax.sharding import PartitionSpec as P

AXES = ("band", "patch")
EPSILON = 1e-05
BF = jnp.bfloat16
F32 = jnp.float32
I32 = jnp.int32


def dot(a, b):
    return jnp.dot(a, b, preferred_element_type=F32)


def dot_rows(a, b):
    return lax.dot_general(a, b, (((0,), (0,)), ((), ())), preferred_element_type=F32)


def dot_lanes(a, b):
    return lax.dot_general(a, b, (((1,), (1,)), ((), ())), preferred_element_type=F32)


def iota(shape, axis):
    return lax.broadcasted_iota(I32, shape, axis)


def flag(condition):
    return jnp.where(condition, 1.0, 0.0).astype(BF)


def column(row):
    count = row.shape[1]
    same = iota((count, count), 0) == iota((count, count), 1)
    return jnp.sum(jnp.where(same, row.astype(F32), 0.0), axis=1, keepdims=True).astype(I32)


def choose(row, count):
    edges = row.shape[1]
    return flag(iota((edges, count), 1) == column(row))


def choose_t(row, count):
    return flag(iota((count, row.shape[1]), 0) == row)


def silu(v):
    return 0.5 * v * (1.0 + jnp.tanh(0.5 * v))


def finish(summed, second):
    out = dot(silu(summed).astype(BF), second)
    centred = out - jnp.mean(out, axis=-1, keepdims=True)
    spread = jnp.mean(centred * centred, axis=-1, keepdims=True)
    return centred * lax.rsqrt(spread + EPSILON)


def residual(base, update):
    return (base.astype(F32) + update).astype(BF)


def spread_rows(chosen, values):
    high = values.astype(BF)
    low = (values - high.astype(F32)).astype(BF)
    return dot(jnp.concatenate([chosen, chosen], axis=1), jnp.concatenate([high, low], axis=0))


def wanted_rows(wanted, kind, cap):
    devices, lanes = wanted.shape
    total = devices * cap
    row = iota((total, 1), 0)
    owner = jnp.floor((row.astype(F32) + 0.5) * (1.0 / cap)).astype(I32)
    slot = row - owner * cap
    expand = flag(iota((total, devices), 1) == owner)
    values = dot(expand, wanted.astype(F32).astype(BF))
    own = jnp.where(iota((total, lanes), 1) == slot + kind * cap, values, 0.0).astype(BF)
    index = dot(own, jnp.ones((lanes, lanes), BF))
    return flag(iota((total, lanes), 1).astype(F32) == index)


def start(sems, *pairs):
    copies = [pltpu.make_async_copy(src, dst, sems.at[n]) for n, (src, dst) in enumerate(pairs)]
    for copy in copies:
        copy.start()
    return copies


def ask_kernel(cap, devices, dev0, dev1, dev2, row0, row1, row2, request, slots, *scratch):
    lines, sems = scratch[:6], scratch[6]
    copies = start(sems, *zip((dev0, dev1, dev2, row0, row1, row2), lines))
    edges = row0.shape[0]
    earlier = flag(iota((edges, edges), 0) < iota((edges, edges), 1))
    for copy in copies:
        copy.wait()
    total = jnp.zeros(request.shape, F32)
    for kind in range(3):
        source = lines[kind][...]
        row = lines[3 + kind][...].reshape(1, edges)
        hit = iota((devices, edges), 0) == source
        hits = flag(hit)
        before = dot(hits, earlier)
        place = jnp.sum(jnp.where(hit, before, 0.0), axis=0, keepdims=True).astype(I32)
        mine = iota((request.shape[1], edges), 0) == place + kind * cap
        total = total + dot_lanes(hits, jnp.where(mine, row.astype(F32), 0.0).astype(BF))
        slots[kind : kind + 1, :] = source * cap + place
    request[...] = total.astype(I32)


def first_kernel(cap, devices, slots, grid, mesh, enc_dst, w, grid_one, target, base, pick, g, m, d, w6, w7, w1, w3, sems):
    copies = start(sems, (grid, g), (w.at[6], w6), (w.at[7], w7), (mesh, m), (w.at[1], w1), (enc_dst, d), (w.at[3], w3))
    pick[...] = choose(slots[0:1, :], devices * cap)
    for copy in copies:
        copy.wait()
    grid_one[...] = residual(g[...], finish(dot(g[...], w6[...]), w7[...]))
    dst = d[...].reshape(1, d.shape[0])
    target[...] = spread_rows(choose(dst, m.shape[0]), dot(m[...], w1[...]))
    base[...] = dot(m[...], w3[...])


def serve_kernel(cap, wanted, table, out, held, sems):
    (copy,) = start(sems, (table, held))
    hot = wanted_rows(wanted[...], 0, cap)
    copy.wait()
    out[...] = dot(hot, held[...]).astype(BF)


def plan_kernel(cap, devices, wanted, slots, hot1, hot2, pick1, pick2):
    hot1[...] = wanted_rows(wanted[...], 1, cap)
    hot2[...] = wanted_rows(wanted[...], 2, cap)
    pick1[...] = choose(slots[1:2, :], devices * cap)
    pick2[...] = choose(slots[2:3, :], devices * cap)


def enc_kernel(received, pick, target, base, hot, mesh, dst, w, mesh_one, out, w0, w2, w4, w5, m, d, sems):
    copies = start(sems, (w.at[0], w0), (w.at[2], w2), (w.at[4], w4), (w.at[5], w5), (mesh, m), (dst, d))
    source = dot(pick[...], received[...]).astype(BF)
    copies[0].wait()
    summed = dot(source, w0[...]) + target[...]
    copies[1].wait()
    message = finish(summed, w2[...]).astype(BF)
    copies[5].wait()
    summed = dot(choose_t(d[...].reshape(1, d.shape[0]), m.shape[0]), message).astype(BF)
    copies[2].wait()
    summed = base[...] + dot(summed, w4[...])
    copies[3].wait()
    copies[4].wait()
    one = residual(m[...], finish(summed, w5[...]))
    mesh_one[...] = one
    out[...] = dot(hot[...], one).astype(BF)


def local_kernel(
    mesh_one, loc_src, loc_dst, proc_dst, w, target, base, partial, w9, w8, w10, w11, s, d, p, sems
):
    copies = start(
        sems, (w.at[9], w9), (w.at[8], w8), (w.at[10], w10), (w.at[11], w11), (loc_src, s), (loc_dst, d), (proc_dst, p)
    )
    for copy in copies:
        copy.wait()
    one = mesh_one[...]
    count = one.shape[0]
    local = s.shape[0]
    ends = dot(one, w9[...])
    target[...] = spread_rows(choose(p[...].reshape(1, p.shape[0]), count), ends)
    base[...] = dot(one, w11[...])
    begin = spread_rows(choose(s[...].reshape(1, local), count), dot(one, w8[...]))
    stop = d[...].reshape(1, local)
    message = finish(begin + spread_rows(choose(stop, count), ends), w10[...]).astype(BF)
    partial[...] = dot(choose_t(stop, count), message)


def proc_kernel(
    received, pick, target, base, partial, mesh_one, hot, dst, w, out, w8, w10, w12, w13, d, sems
):
    copies = start(sems, (w.at[8], w8), (w.at[10], w10), (w.at[12], w12), (w.at[13], w13), (dst, d))
    source = dot(pick[...], received[...]).astype(BF)
    copies[0].wait()
    summed = dot(source, w8[...]) + target[...]
    copies[1].wait()
    message = finish(summed, w10[...]).astype(BF)
    copies[4].wait()
    summed = dot(choose_t(d[...].reshape(1, d.shape[0]), mesh_one.shape[0]), message)
    copies[2].wait()
    summed = base[...] + dot((partial[...] + summed).astype(BF), w12[...])
    copies[3].wait()
    two = residual(mesh_one[...], finish(summed, w13[...]))
    out[...] = dot(hot[...], two).astype(BF)


def last_kernel(grid_one, w, target, base, w15, w17, sems):
    copies = start(sems, (w.at[15], w15), (w.at[17], w17))
    one = grid_one[...]
    rows = target.shape[0]
    near = iota((rows, one.shape[0]), 0) - 3 * iota((rows, one.shape[0]), 1)
    copies[0].wait()
    target[...] = spread_rows(flag((near >= 0) & (near < 3)), dot(one, w15[...]))
    copies[1].wait()
    base[...] = dot(one, w17[...])


def dec_kernel(received, pick, target, base, grid_one, w, out, w14, w16, w18, w19, sems):
    copies = start(sems, (w.at[14], w14), (w.at[16], w16), (w.at[18], w18), (w.at[19], w19))
    source = dot(pick[...], received[...]).astype(BF)
    copies[0].wait()
    summed = dot(source, w14[...]) + target[...]
    copies[1].wait()
    message = finish(summed, w16[...]).astype(BF)
    shape = (grid_one.shape[0], target.shape[0])
    near = iota(shape, 1) - 3 * iota(shape, 0)
    summed = dot(flag((near >= 0) & (near < 3)), message).astype(BF)
    copies[2].wait()
    summed = base[...] + dot(summed, w18[...])
    copies[3].wait()
    out[...] = residual(grid_one[...], finish(summed, w19[...]))


def run(kernel, outs, near, far=(), held=(), macs=0, grant=16):
    inside = pl.BlockSpec(memory_space=pltpu.VMEM)
    outside = pl.BlockSpec(memory_space=pltpu.HBM)
    moved = sum(a.size * a.dtype.itemsize for a in list(near) + list(held) + list(outs))
    scratch = [pltpu.VMEM(a.shape, a.dtype) for a in held]
    if held:
        scratch.append(pltpu.SemaphoreType.DMA((len(held),)))
    return pl.pallas_call(
        kernel,
        out_shape=tuple(outs),
        in_specs=[inside] * len(near) + [outside] * len(far),
        out_specs=tuple(inside for _ in outs),
        scratch_shapes=scratch,
        compiler_params=pltpu.CompilerParams(vmem_limit_bytes=grant * 2**20),
        cost_estimate=pl.CostEstimate(flops=2 * macs, bytes_accessed=moved, transcendentals=0),
    )(*near, *far)


def exchange(rows, cap):
    total, width = rows.shape
    parts = rows.reshape(total // cap, cap * width // 128, 128)
    moved = lax.all_to_all(parts, AXES, split_axis=0, concat_axis=0, tiled=True)
    return moved.reshape(total, width)


def body(
    grid_latent,
    mesh_latent,
    weights,
    enc_dev,
    enc_row,
    enc_dst,
    proc_dev,
    proc_row,
    proc_dst,
    loc_src,
    loc_dst,
    dec_dev,
    dec_row,
):
    devices = lax.axis_size("band") * lax.axis_size("patch")
    edges = enc_dev.shape[0]
    cap = max(2, 2 * edges // devices)
    count, width = mesh_latent.shape

    def arr(shape, dtype):
        return jax.ShapeDtypeStruct(shape, dtype)

    lanes = 128
    total = devices * cap
    line = arr((1, edges), I32)
    row = arr((edges,), I32)
    loc = arr(loc_src.shape, I32)
    mat = arr((width, width), BF)
    nodes = arr((count, width), BF)
    nodes32 = arr((count, width), F32)
    edges32 = arr((edges, width), F32)
    pick = arr((edges, total), BF)
    hot = arr((total, count), BF)
    rows = arr((total, width), BF)
    edge_macs = edges * width * (total + 3 * width)
    request, slots = run(
        functools.partial(ask_kernel, cap, devices),
        (arr((devices, lanes), I32), arr((8, edges), I32)),
        (),
        (enc_dev.reshape(1, edges), proc_dev.reshape(1, edges), dec_dev.reshape(1, edges), enc_row, proc_row, dec_row),
        (line, line, line, row, row, row),
        macs=3 * devices * edges * (edges + lanes),
    )
    asked = request.reshape(devices, 1, lanes)
    wanted = lax.all_to_all(asked, AXES, split_axis=0, concat_axis=0, tiled=True).reshape(devices, lanes)
    grid_one, enc_target, enc_base, enc_pick = run(
        functools.partial(first_kernel, cap, devices),
        (nodes, edges32, nodes32, pick),
        (slots,),
        (grid_latent, mesh_latent, enc_dst, weights),
        (nodes, nodes, row, mat, mat, mat, mat),
        macs=7 * count * width * width,
    )
    (served,) = run(
        functools.partial(serve_kernel, cap),
        (rows,),
        (wanted,),
        (grid_latent,),
        (nodes,),
        macs=total * count * (width + 2 * count),
    )
    enc_rows = exchange(served, cap)
    hot1, hot2, proc_pick, dec_pick = run(
        functools.partial(plan_kernel, cap, devices),
        (hot, hot, pick, pick),
        (wanted, slots),
        macs=4 * total * count * count,
    )
    mesh_one, served = run(
        enc_kernel,
        (nodes, rows),
        (enc_rows, enc_pick, enc_target, enc_base, hot1),
        (mesh_latent, enc_dst, weights),
        (mat, mat, mat, mat, nodes, row),
        macs=edge_macs,
    )
    proc_rows = exchange(served, cap)
    proc_target, proc_base, partial = run(
        local_kernel,
        (edges32, nodes32, nodes32),
        (mesh_one,),
        (loc_src, loc_dst, proc_dst, weights),
        (mat, mat, mat, mat, loc, loc, row),
        macs=7 * count * width * width,
    )
    (served,) = run(
        proc_kernel,
        (rows,),
        (proc_rows, proc_pick, proc_target, proc_base, partial, mesh_one, hot2),
        (proc_dst, weights),
        (mat, mat, mat, mat, row),
        macs=edge_macs,
    )
    dec_rows = exchange(served, cap)
    dec_target, dec_base = run(
        last_kernel,
        (edges32, nodes32),
        (grid_one,),
        (weights,),
        (mat, mat),
        macs=4 * count * width * width,
    )
    (decoded,) = run(
        dec_kernel,
        (nodes,),
        (dec_rows, dec_pick, dec_target, dec_base, grid_one),
        (weights,),
        (mat, mat, mat, mat),
        macs=edge_macs,
    )
    return decoded


def solution(mesh):
    rows = P(AXES, None)
    edge = P(AXES)
    in_specs = (rows, rows, P(), rows, edge, edge, rows, edge, edge, edge, edge, rows, edge)
    return jax.shard_map(body, mesh=mesh, in_specs=in_specs, out_specs=rows, check_vma=False)
```

time: 132 us -> 130 us (0.985)
  Pallas kernels: 11.7 us -> 15.1 us
  waiting for transfers between devices: 26.6 us -> 23.5 us
  starting transfers between devices: 18.5 us -> 16.5 us
    unnamed x86 -> x76, local copies, waits for them, and re-layouts: 33.6 us -> 45.2 us
    squeeze x2 -> x0, local copies, waits for them, and re-layouts: 7.58 us -> none  [body(): w = [weights[k] for k in range(weights.shape[0])]]
    pallas_call x9, Pallas kernels: 11.7 us -> 15.1 us  [run(): pl.pallas_call(kernel, out_shape=tuple(outs), in_specs=[inside] * len(nea...]
    all_to_all x3, waiting for transfers between devices: 26.6 us -> 23.5 us  [exchange(): moved = lax.all_to_all(parts, AXES, split_axis=0, concat_axis=0, tiled=True)]
    reshape x5 -> x0, local copies, waits for them, and re-layouts: 2.74 us -> none  [line(): return values.reshape(1, values.size)]
    all_to_all x3, starting transfers between devices: 18.5 us -> 16.5 us  [exchange(): moved = lax.all_to_all(parts, AXES, split_axis=0, concat_axis=0, tiled=True)]
  transfers between devices with their start and end apart: 3 -> 3, of which waited for: 3 -> 3; matrix products, arithmetic and copies ran while one was open for 6% -> 0% of each run, Pallas kernels for 3% -> 4%
where the time goes in v2:
time: 130 us; the launch traced here: 129 us
  local copies, waits for them, and re-layouts  52.9 us (41%)
  waiting for transfers between devices  23.5 us (18%)
  blocking collectives  20.9 us (16%)
  starting transfers between devices  16.5 us (13%)
  Pallas kernels  15.1 us (12%)
    unnamed x76, local copies, waits for them, and re-layouts  45.2 us
    all_to_all x3, waiting for transfers between devices, exchange(): moved = lax.all_to_all(parts, AXES, split_axis=0, concat_axis=0, tiled=True)  23.5 us
    all_to_all x1, blocking collectives, body(): lax.all_to_all(asked, AXES, split_axis=0, concat_axis=0, tiled=True)  20.9 us
    all_to_all x3, starting transfers between devices, exchange(): moved = lax.all_to_all(parts, AXES, split_axis=0, concat_axis=0, tiled=True)  16.5 us
    pallas_call x9, Pallas kernels, run(): pl.pallas_call(kernel, out_shape=tuple(outs), in_specs=[inside] * len(nea...  15.1 us
    reshape x3, local copies, waits for them, and re-layouts, exchange(): parts = rows.reshape(total // cap, cap * width // 128, 128)  4.09 us
    reshape x3, local copies, waits for them, and re-layouts, exchange(): return moved.reshape(total, width)  3.59 us
  transfers between devices with their start and end apart: 3, of which 3 were waited for; matrix products, arithmetic and copies ran while one was open for 0% of the time, Pallas kernels for 4%

profile of v2, /device:TPU:1, one launch (start us, length us, event | category | flops | bytes accessed | tf_op | source)
XLA Modules:
  0.0 129.4 jit_solution(8214760133829298532)
XLA Ops:
  4.9 20.9 %all_to_all.20 = s32[128,1,128]{2,1,0:T(1,128)S(1)} all-to-all(s32[128,1,128]{2,1,0:T(1,128)S(1)} %bitcast.9), channel_id=1, replica_groups=mesh['band'=8,'patch'=16] {'band','patch'}, dimensions={0} | all-to-all | bytes 131072 | tf_op jit(solution)/shard_map/all_to_all | solution.py:292
  25.8 0.9 copy-done.13
  27.6 1.4 %reshape.38 = bf16[128,24,128]{2,1,0:T(8,128)(2,1)} reshape(bf16[768,512]{1,0:T(8,128)(2,1)S(1)} %shard_map.128) | data formatting | bytes 1572864 | tf_op jit(solution)/shard_map/reshape | solution.py:242
  28.9 5.4 %all-to-all-start.1 = ((bf16[128,24,128]{2,1,0:T(8,128)(2,1)}), bf16[128,24,128]{2,1,0:T(8,128)(2,1)}, u32[]{:S(2)}, u32[]{:S(2)}) async-start(bf16[128,24,128]{2,1,0:T(8,128)(2,1)} %reshape.38), calls=%async_computation.1 | async-start | bytes 1572864 | tf_op jit(solution)/shard_map/all_to_all | solution.py:243
  34.3 4.0 %copy-done = bf16[20,512,512]{2,1,0:T(8,128)(2,1)S(1)} copy-done((bf16[20,512,512]{2,1,0:T(8,128)(2,1)S(1)}, bf16[20,512,512]{2,1,0:T(8,128)(2,1)}, u32[]{:S(2)}) %copy-start) | copy-done | bytes 10485784
  38.3 0.9 copy-done.8
  39.2 0.9 copy-done.14
  40.8 1.6 %shard_map.129 = (bf16[128,512]{1,0:T(8,128)(2,1)S(1)}, f32[384,512]{1,0:T(8,128)S(1)}, f32[128,512]{1,0:T(8,128)S(1)}, bf16[384,768]{1,0:T(8,128)(2,1)S(1)}) custom-call(s32[8,384]{1,0:T(8,128)S(1)} %get-tuple-element.23.slots, bf16[128,512]{1,0:T(8,128)(2,1)S(1)} %copy-done.14, bf16[128,512]{1,0:T(8,128)(2,1)S(1)} %copy-done.8, s32[384]{0:T(512)S(1)} %copy-done.27, ...), custom_call_target="tpu_custom_call" | custom-call | flops 469762048 | bytes 4142592 | tf_op jit(solution)/shard_map/pallas_call | solution.py:229
  46.6 4.2 %all-to-all-done.1 = bf16[128,24,128]{2,1,0:T(8,128)(2,1)} async-done(((bf16[128,24,128]{2,1,0:T(8,128)(2,1)}), bf16[128,24,128]{2,1,0:T(8,128)(2,1)}, u32[]{:S(2)}, u32[]{:S(2)}) %all-to-all-start.1) | async-done | bytes 786464 | tf_op jit(solution)/shard_map/all_to_all | solution.py:243
  50.7 1.6 %reshape.39.received = bf16[768,512]{1,0:T(8,128)(2,1)S(1)} reshape(bf16[128,24,128]{2,1,0:T(8,128)(2,1)} %all-to-all-done.1) | data formatting | bytes 1572864 | tf_op jit(solution)/shard_map/reshape | solution.py:244
  52.3 4.0 %copy-done.1 = bf16[20,512,512]{2,1,0:T(8,128)(2,1)S(1)} copy-done((bf16[20,512,512]{2,1,0:T(8,128)(2,1)S(1)}, bf16[20,512,512]{2,1,0:T(8,128)(2,1)}, u32[]{:S(2)}) %copy-start.1) | copy-done | bytes 10485784
  57.2 0.9 copy-done.18
  58.2 0.9 copy-done.26
  59.1 3.0 %shard_map.131 = (bf16[128,512]{1,0:T(8,128)(2,1)S(1)}, bf16[768,512]{1,0:T(8,128)(2,1)S(1)}) custom-call(bf16[768,512]{1,0:T(8,128)(2,1)S(1)} %reshape.39.received, bf16[384,768]{1,0:T(8,128)(2,1)S(1)} %get-tuple-element.24.pick, f32[384,512]{1,0:T(8,128)S(1)} %get-tuple-element.25.target, f32[128,512]{1,0:T(8,128)S(1)} %copy-done.18, ...), custom_call_target="tpu_custom_call" | custom-call | flops 905969664 | bytes 5768704 | tf_op jit(solution)/shard_map/pallas_call | solution.py:229
  62.7 1.4 %reshape.40 = bf16[128,24,128]{2,1,0:T(8,128)(2,1)} reshape(bf16[768,512]{1,0:T(8,128)(2,1)S(1)} %get-tuple-element.28) | data formatting | bytes 1572864 | tf_op jit(solution)/shard_map/reshape | solution.py:242
  64.1 5.7 %all-to-all-start.2 = ((bf16[128,24,128]{2,1,0:T(8,128)(2,1)}), bf16[128,24,128]{2,1,0:T(8,128)(2,1)S(1)}, u32[]{:S(2)}, u32[]{:S(2)}) async-start(bf16[128,24,128]{2,1,0:T(8,128)(2,1)} %reshape.40), calls=%async_computation.2 | async-start | bytes 1572864 | tf_op jit(solution)/shard_map/all_to_all | solution.py:243
  69.9 4.0 %copy-done.2 = bf16[20,512,512]{2,1,0:T(8,128)(2,1)S(1)} copy-done((bf16[20,512,512]{2,1,0:T(8,128)(2,1)S(1)}, bf16[20,512,512]{2,1,0:T(8,128)(2,1)}, u32[]{:S(2)}) %copy-start.2) | copy-done | bytes 10485784
  73.8 0.9 copy-done.11
  74.8 1.6 %shard_map.132 = (f32[384,512]{1,0:T(8,128)S(1)}, f32[128,512]{1,0:T(8,128)S(1)}, f32[128,512]{1,0:T(8,128)S(1)}) custom-call(bf16[128,512]{1,0:T(8,128)(2,1)S(1)} %copy-done.11, s32[256]{0:T(256)S(1)} %copy-done.30, s32[256]{0:T(256)S(1)} %copy-done.31, s32[384]{0:T(512)S(1)} %copy-done.29, bf16[20,512,512]{2,1,0:T(8,128)(2,1)S(1)} %copy-done.2), custom_call_target="tpu_custom_call" | custom-call | flops 469762048 | bytes 3542528 | tf_op jit(solution)/shard_map/pallas_call | solution.py:229
  77.8 8.6 %all-to-all-done.2 = bf16[128,24,128]{2,1,0:T(8,128)(2,1)S(1)} async-done(((bf16[128,24,128]{2,1,0:T(8,128)(2,1)}), bf16[128,24,128]{2,1,0:T(8,128)(2,1)S(1)}, u32[]{:S(2)}, u32[]{:S(2)}) %all-to-all-start.2) | async-done | bytes 786464 | tf_op jit(solution)/shard_map/all_to_all | solution.py:243
  86.9 4.0 %copy-done.3 = bf16[20,512,512]{2,1,0:T(8,128)(2,1)S(1)} copy-done((bf16[20,512,512]{2,1,0:T(8,128)(2,1)S(1)}, bf16[20,512,512]{2,1,0:T(8,128)(2,1)}, u32[]{:S(2)}) %copy-start.3) | copy-done | bytes 10485784
  91.8 0.9 copy-done.20
  92.7 0.9 copy-done.22
  93.7 0.9 copy-done.24
  94.6 2.8 %shard_map.133 = bf16[768,512]{1,0:T(8,128)(2,1)S(1)} custom-call(bf16[768,512]{1,0:T(8,128)(2,1)S(1)} %reshape.41.received, bf16[384,768]{1,0:T(8,128)(2,1)S(1)} %copy-done.7, f32[384,512]{1,0:T(8,128)S(1)} %get-tuple-element.31.target, f32[128,512]{1,0:T(8,128)S(1)} %copy-done.20, f32[128,512]{1,0:T(8,128)S(1)} %copy-done.22, ...), custom_call_target="tpu_custom_call" | custom-call | flops 905969664 | bytes 5899776 | tf_op jit(solution)/shard_map/pallas_call | solution.py:229
  97.4 1.4 %reshape.42 = bf16[128,24,128]{2,1,0:T(8,128)(2,1)} reshape(bf16[768,512]{1,0:T(8,128)(2,1)S(1)} %shard_map.133) | data formatting | bytes 1572864 | tf_op jit(solution)/shard_map/reshape | solution.py:242
  98.8 5.4 %all-to-all-start.3 = ((bf16[128,24,128]{2,1,0:T(8,128)(2,1)}), bf16[128,24,128]{2,1,0:T(8,128)(2,1)}, u32[]{:S(2)}, u32[]{:S(2)}) async-start(bf16[128,24,128]{2,1,0:T(8,128)(2,1)} %reshape.42), calls=%async_computation.3 | async-start | bytes 1572864 | tf_op jit(solution)/shard_map/all_to_all | solution.py:243
  104.2 4.0 %copy-done.4 = bf16[20,512,512]{2,1,0:T(8,128)(2,1)S(1)} copy-done((bf16[20,512,512]{2,1,0:T(8,128)(2,1)S(1)}, bf16[20,512,512]{2,1,0:T(8,128)(2,1)}, u32[]{:S(2)}) %copy-start.4) | copy-done | bytes 10485784
  109.9 10.7 %all-to-all-done.3 = bf16[128,24,128]{2,1,0:T(8,128)(2,1)} async-done(((bf16[128,24,128]{2,1,0:T(8,128)(2,1)}), bf16[128,24,128]{2,1,0:T(8,128)(2,1)}, u32[]{:S(2)}, u32[]{:S(2)}) %all-to-all-start.3) | async-done | bytes 786464 | tf_op jit(solution)/shard_map/all_to_all | solution.py:243
  120.6 1.6 %reshape.43.received = bf16[768,512]{1,0:T(8,128)(2,1)S(1)} reshape(bf16[128,24,128]{2,1,0:T(8,128)(2,1)} %all-to-all-done.3) | data formatting | bytes 1572864 | tf_op jit(solution)/shard_map/reshape | solution.py:244
  122.2 4.0 %copy-done.5 = bf16[20,512,512]{2,1,0:T(8,128)(2,1)S(1)} copy-done((bf16[20,512,512]{2,1,0:T(8,128)(2,1)S(1)}, bf16[20,512,512]{2,1,0:T(8,128)(2,1)}, u32[]{:S(2)}) %copy-start.5) | copy-done | bytes 10485784
  126.2 3.0 %shard_map.135 = bf16[128,512]{1,0:T(8,128)(2,1)} custom-call(bf16[768,512]{1,0:T(8,128)(2,1)S(1)} %reshape.43.received, bf16[384,768]{1,0:T(8,128)(2,1)S(1)} %get-tuple-element.35.pick, f32[384,512]{1,0:T(8,128)S(1)} %get-tuple-element.37.target, f32[128,512]{1,0:T(8,128)S(1)} %get-tuple-element.38.base, bf16[128,512]{1,0:T(8,128)(2,1)S(1)} %copy-done.16, ...), custom_call_target="tpu_custom_call" | custom-call | flops 905969664 | bytes 4784128 | tf_op jit(solution)/shard_map/pallas_call | solution.py:229
  (66 shorter events, 16.7 us)
Async XLA Ops:
  0.0 52.3 %copy-start.28 = (s32[384]{0:T(512)S(1)}, s32[384]{0:T(512)}, u32[]{:S(2)}) copy-start(s32[384]{0:T(512)} %dst.2) | copy-start | bytes 4612
  0.0 0.7 copy-start.32
  25.8 0.9 copy-start.13
  28.9 21.8 %all-to-all-start.1 = ((bf16[128,24,128]{2,1,0:T(8,128)(2,1)}), bf16[128,24,128]{2,1,0:T(8,128)(2,1)}, u32[]{:S(2)}, u32[]{:S(2)}) async-start(bf16[128,24,128]{2,1,0:T(8,128)(2,1)} %reshape.38), calls=%async_computation.1 | async-start | bytes 1572864 | tf_op jit(solution)/shard_map/all_to_all | solution.py:243
  34.3 4.0 %copy-start = (bf16[20,512,512]{2,1,0:T(8,128)(2,1)S(1)}, bf16[20,512,512]{2,1,0:T(8,128)(2,1)}, u32[]{:S(2)}) copy-start(bf16[20,512,512]{2,1,0:T(8,128)(2,1)} %w.11) | copy-start | bytes 31457284
  38.3 0.9 copy-start.8
  39.2 0.9 copy-start.14
  43.0 0.7 copy-start.17
  43.7 26.1 %copy-start.29 = (s32[384]{0:T(512)S(1)}, s32[384]{0:T(512)}, u32[]{:S(2)}) copy-start(s32[384]{0:T(512)} %dst.3) | copy-start | bytes 4612
  43.7 26.1 %copy-start.30 = (s32[256]{0:T(256)S(1)}, s32[256]{0:T(256)}, u32[]{:S(2)}) copy-start(s32[256]{0:T(256)} %loc_src.1) | copy-start | bytes 3076
  43.7 26.1 %copy-start.31 = (s32[256]{0:T(256)S(1)}, s32[256]{0:T(256)}, u32[]{:S(2)}) copy-start(s32[256]{0:T(256)} %loc_dst.1) | copy-start | bytes 3076
  44.4 0.8 copy-start.6
  45.9 0.7 copy-start.25
  52.3 4.0 %copy-start.1 = (bf16[20,512,512]{2,1,0:T(8,128)(2,1)S(1)}, bf16[20,512,512]{2,1,0:T(8,128)(2,1)}, u32[]{:S(2)}) copy-start(bf16[20,512,512]{2,1,0:T(8,128)(2,1)} %w.11) | copy-start | bytes 31457284
  56.3 0.9 copy-start.9
  57.2 0.9 copy-start.18
  58.2 0.9 copy-start.26
  62.7 24.2 %copy-start.7 = (bf16[384,768]{1,0:T(8,128)(2,1)S(1)}, bf16[384,768]{1,0:T(8,128)(2,1)}, u32[]{:S(2)}) copy-start(bf16[384,768]{1,0:T(8,128)(2,1)} %copy-done.6) | copy-start | bytes 1769476
  64.1 22.3 %all-to-all-start.2 = ((bf16[128,24,128]{2,1,0:T(8,128)(2,1)}), bf16[128,24,128]{2,1,0:T(8,128)(2,1)S(1)}, u32[]{:S(2)}, u32[]{:S(2)}) async-start(bf16[128,24,128]{2,1,0:T(8,128)(2,1)} %reshape.40), calls=%async_computation.2 | async-start | bytes 1572864 | tf_op jit(solution)/shard_map/all_to_all | solution.py:243
  69.9 4.0 %copy-start.2 = (bf16[20,512,512]{2,1,0:T(8,128)(2,1)S(1)}, bf16[20,512,512]{2,1,0:T(8,128)(2,1)}, u32[]{:S(2)}) copy-start(bf16[20,512,512]{2,1,0:T(8,128)(2,1)} %w.11) | copy-start | bytes 31457284
  73.8 0.9 copy-start.11
  76.4 0.7 copy-start.19
  77.1 0.7 copy-start.21
  86.9 4.0 %copy-start.3 = (bf16[20,512,512]{2,1,0:T(8,128)(2,1)S(1)}, bf16[20,512,512]{2,1,0:T(8,128)(2,1)}, u32[]{:S(2)}) copy-start(bf16[20,512,512]{2,1,0:T(8,128)(2,1)} %w.11) | copy-start | bytes 31457284
  90.9 0.9 copy-start.12
  91.8 0.9 copy-start.20
  92.7 0.9 copy-start.22
  93.7 0.9 copy-start.24
  98.8 21.8 %all-to-all-start.3 = ((bf16[128,24,128]{2,1,0:T(8,128)(2,1)}), bf16[128,24,128]{2,1,0:T(8,128)(2,1)}, u32[]{:S(2)}, u32[]{:S(2)}) async-start(bf16[128,24,128]{2,1,0:T(8,128)(2,1)} %reshape.42), calls=%async_computation.3 | async-start | bytes 1572864 | tf_op jit(solution)/shard_map/all_to_all | solution.py:243
  104.2 4.0 %copy-start.4 = (bf16[20,512,512]{2,1,0:T(8,128)(2,1)S(1)}, bf16[20,512,512]{2,1,0:T(8,128)(2,1)}, u32[]{:S(2)}) copy-start(bf16[20,512,512]{2,1,0:T(8,128)(2,1)} %w.11) | copy-start | bytes 31457284
  108.2 0.9 copy-start.16
  122.2 4.0 %copy-start.5 = (bf16[20,512,512]{2,1,0:T(8,128)(2,1)S(1)}, bf16[20,512,512]{2,1,0:T(8,128)(2,1)}, u32[]{:S(2)}) copy-start(bf16[20,512,512]{2,1,0:T(8,128)(2,1)} %w.11) | copy-start | bytes 31457284
  (9 other events, 6.1 us)

commit v3 on v0

v3 whole, which is shorter than its diff:
```python
import functools

import jax
import jax.numpy as jnp
from jax import lax
from jax.experimental import pallas as pl
from jax.experimental.pallas import tpu as pltpu
from jax.sharding import PartitionSpec as P

AXES = ("band", "patch")
EPSILON = 1e-05
LANES = 128
PARTS = 4
BF = jnp.bfloat16
F32 = jnp.float32
I32 = jnp.int32


def dot(a, b):
    return jnp.dot(a, b, preferred_element_type=F32)


def dot_lanes(a, b):
    return lax.dot_general(a, b, (((1,), (1,)), ((), ())), preferred_element_type=F32)


def iota(shape, axis):
    return lax.broadcasted_iota(I32, shape, axis)


def flag(condition):
    return jnp.where(condition, 1.0, 0.0).astype(BF)


def column(row):
    count = row.shape[1]
    same = iota((count, count), 0) == iota((count, count), 1)
    return jnp.sum(jnp.where(same, row.astype(F32), 0.0), axis=1, keepdims=True).astype(I32)


def choose(row, count):
    return flag(iota((row.shape[1], count), 1) == column(row))


def choose_t(row, count):
    return flag(iota((count, row.shape[1]), 0) == row)


def line(ref):
    return ref[...].reshape(1, ref.shape[0])


def silu(v):
    return 0.5 * v * (1.0 + jnp.tanh(0.5 * v))


def finish(summed, second):
    out = dot(silu(summed).astype(BF), second)
    centred = out - jnp.mean(out, axis=-1, keepdims=True)
    spread = jnp.mean(centred * centred, axis=-1, keepdims=True)
    return centred * lax.rsqrt(spread + EPSILON)


def residual(base, update):
    return (base.astype(F32) + update).astype(BF)


def halves(values):
    high = values.astype(BF)
    return jnp.concatenate([high, (values - high.astype(F32)).astype(BF)], axis=0)


def twice(chosen):
    return jnp.concatenate([chosen, chosen], axis=1)


def start(sems, first, *pairs):
    copies = [pltpu.make_async_copy(src, dst, sems.at[first + n]) for n, (src, dst) in enumerate(pairs)]
    for copy in copies:
        copy.start()
    return copies


def wait(*copies):
    for copy in copies:
        copy.wait()


def part(ref, n):
    size = ref.shape[0] // PARTS
    return ref.at[pl.ds(n * size, size)]


def places(source, devices):
    edges = source.shape[1]
    earlier = flag(iota((edges, edges), 0) < iota((edges, edges), 1))
    hit = iota((devices, edges), 0) == source
    hits = flag(hit)
    return jnp.sum(jnp.where(hit, dot(hits, earlier), 0.0), axis=0, keepdims=True).astype(I32), hits


def serve(asked, kind, cap, table, wide, packed, out, sems, first):
    devices = asked.shape[0]
    blocks = table.shape[1] // LANES
    for slot in range(cap):
        lane = kind * cap + slot
        rows = dot(flag(asked[:, lane : lane + 1] == iota((devices, table.shape[0]), 1)), table)
        for block in range(blocks):
            target = pl.ds(slot * blocks + block, devices, stride=cap * blocks)
            wide[target, :] = rows[:, block * LANES : (block + 1) * LANES]
    copies = []
    size = wide.shape[0] // PARTS
    for n in range(PARTS):
        packed[pl.ds(n * size, size), :] = wide[pl.ds(n * size, size), :].astype(BF)
        copies += start(sems, first + n, (part(packed, n), part(out, n)))
    return copies


def take_in(cap, packed, wide, rows):
    blocks = rows.shape[1] // LANES
    devices = rows.shape[0] // cap
    size = wide.shape[0] // PARTS
    some = devices // PARTS
    for n in range(PARTS):
        wide[pl.ds(n * size, size), :] = packed[pl.ds(n * size, size), :].astype(F32)
        for slot in range(cap):
            for block in range(blocks):
                source = pl.ds(n * size + slot * blocks + block, some, stride=cap * blocks)
                target = pl.ds(slot * devices + n * some, some)
                rows[target, block * LANES : (block + 1) * LANES] = wide[source, :].astype(BF)


def ask_kernel(cap, devices, dev0, dev1, dev2, row0, row1, row2, request, *scratch):
    lines, sems = scratch[:6], scratch[6]
    copies = start(sems, 0, *zip((dev0, dev1, dev2, row0, row1, row2), lines))
    wait(*copies)
    total = jnp.zeros(request.shape, F32)
    for kind in range(3):
        place, hits = places(lines[kind][...], devices)
        row = line(lines[3 + kind]).astype(F32)
        mine = iota((request.shape[1], row.shape[1]), 0) == place + kind * cap
        total = total + dot_lanes(hits, jnp.where(mine, row, 0.0).astype(BF))
    request[...] = total.astype(I32)


def prepare_kernel(
    devices, grid, mesh, dev0, dev1, dev2, w, one, ends, base, dec_ends, dec_base, slots,
    g, m, d0, d1, d2, w6, w7, w1, w3, w15, w17, one_v, ends_v, base_v, dec_ends_v, dec_base_v, slots_v, sems,
):
    copies = start(
        sems, 0, (dev0, d0), (dev1, d1), (dev2, d2), (mesh, m), (w.at[1], w1), (w.at[3], w3), (grid, g),
        (w.at[6], w6), (w.at[7], w7), (w.at[15], w15), (w.at[17], w17),
    )
    wait(*copies[:3])
    for kind, dev in enumerate((d0, d1, d2)):
        source = dev[...]
        slots_v[kind : kind + 1, :] = places(source, devices)[0] * devices + source
    out = start(sems, 11, (slots_v, slots))
    wait(*copies[3:5])
    ends_v[...] = halves(dot(m[...], w1[...]))
    out += start(sems, 12, (ends_v, ends))
    wait(copies[5])
    base_v[...] = dot(m[...], w3[...])
    out += start(sems, 13, (base_v, base))
    wait(*copies[6:9])
    one_v[...] = residual(g[...], finish(dot(g[...], w6[...]), w7[...]))
    out += start(sems, 14, (one_v, one))
    wait(copies[9])
    dec_ends_v[...] = halves(dot(one_v[...], w15[...]))
    out += start(sems, 15, (dec_ends_v, dec_ends))
    wait(copies[10])
    dec_base_v[...] = dot(one_v[...], w17[...])
    out += start(sems, 16, (dec_base_v, dec_base))
    wait(*out)


def serve_kernel(cap, wanted, table, out, asked, held, wide, packed, sems):
    copies = start(sems, 0, (wanted, asked), (table, held))
    wait(*copies)
    wait(*serve(asked[...], 0, cap, held[...], wide, packed, out, sems, 2))


def enc_kernel(
    cap, received, wanted, slots, dst, ends, base, mesh, w, one, out,
    asked, slot, d, ends_v, base_v, m, w0, w2, w4, w5, one_v, wide, packed, rows, sems,
):
    small = start(sems, 0, (slots, slot), (dst, d))
    copies = start(
        sems, 2, (w.at[0], w0), (ends, ends_v), (w.at[2], w2), (base, base_v), (w.at[4], w4),
        (w.at[5], w5), (mesh, m), (wanted, asked),
    )
    wait(*small)
    pick = choose(slot[0:1, :], rows.shape[0])
    to = twice(choose(line(d), m.shape[0]))
    to_t = choose_t(line(d), m.shape[0])
    take_in(cap, received, wide, rows)
    source = dot(pick, rows[...]).astype(BF)
    wait(*copies[:2])
    summed = dot(source, w0[...]) + dot(to, ends_v[...])
    wait(copies[2])
    message = finish(summed, w2[...]).astype(BF)
    summed = dot(to_t, message).astype(BF)
    wait(*copies[3:5])
    summed = base_v[...] + dot(summed, w4[...])
    wait(*copies[5:])
    one_v[...] = residual(m[...], finish(summed, w5[...]))
    sent = start(sems, 10, (one_v, one))
    sent += serve(asked[...], 1, cap, one_v[...], wide, packed, out, sems, 11)
    wait(*sent)


def local_kernel(
    one, loc_src, loc_dst, w, ends, base, partial,
    one_v, w9, w8, w10, w11, s, d, ends_v, base_v, partial_v, sems,
):
    copies = start(
        sems, 0, (one, one_v), (w.at[9], w9), (loc_src, s), (loc_dst, d), (w.at[8], w8), (w.at[10], w10),
        (w.at[11], w11),
    )
    wait(*copies[:2])
    mine = one_v[...]
    count = mine.shape[0]
    ends_v[...] = halves(dot(mine, w9[...]))
    out = start(sems, 7, (ends_v, ends))
    wait(*copies[2:5])
    begin = dot(twice(choose(line(s), count)), halves(dot(mine, w8[...])))
    stop = line(d)
    wait(copies[5])
    message = finish(begin + dot(twice(choose(stop, count)), ends_v[...]), w10[...]).astype(BF)
    partial_v[...] = dot(choose_t(stop, count), message)
    out += start(sems, 8, (partial_v, partial))
    wait(copies[6])
    base_v[...] = dot(mine, w11[...])
    out += start(sems, 9, (base_v, base))
    wait(*out)


def proc_kernel(
    cap, received, wanted, slots, dst, ends, base, partial, one, w, out,
    asked, slot, d, ends_v, base_v, partial_v, one_v, w8, w10, w12, w13, wide, packed, rows, sems,
):
    small = start(sems, 0, (slots, slot), (dst, d))
    copies = start(
        sems, 2, (w.at[8], w8), (ends, ends_v), (w.at[10], w10), (base, base_v), (w.at[12], w12),
        (partial, partial_v), (w.at[13], w13), (one, one_v), (wanted, asked),
    )
    wait(*small)
    pick = choose(slot[1:2, :], rows.shape[0])
    count = one_v.shape[0]
    to = twice(choose(line(d), count))
    to_t = choose_t(line(d), count)
    take_in(cap, received, wide, rows)
    source = dot(pick, rows[...]).astype(BF)
    wait(*copies[:2])
    summed = dot(source, w8[...]) + dot(to, ends_v[...])
    wait(copies[2])
    message = finish(summed, w10[...]).astype(BF)
    summed = dot(to_t, message)
    wait(*copies[3:6])
    summed = base_v[...] + dot((partial_v[...] + summed).astype(BF), w12[...])
    wait(*copies[6:])
    two = residual(one_v[...], finish(summed, w13[...]))
    wait(*serve(asked[...], 2, cap, two, wide, packed, out, sems, 11))


def dec_kernel(
    cap, received, slots, ends, base, one, w, out,
    slot, ends_v, base_v, one_v, w14, w16, w18, w19, wide, rows, sems,
):
    small = start(sems, 0, (slots, slot))
    copies = start(
        sems, 1, (w.at[14], w14), (ends, ends_v), (w.at[16], w16), (base, base_v), (w.at[18], w18),
        (w.at[19], w19), (one, one_v),
    )
    wait(*small)
    edges = slot.shape[1]
    count = one_v.shape[0]
    pick = choose(slot[2:3, :], rows.shape[0])
    near = iota((edges, count), 0) - 3 * iota((edges, count), 1)
    to = twice(flag((near >= 0) & (near < 3)))
    near = iota((count, edges), 1) - 3 * iota((count, edges), 0)
    to_t = flag((near >= 0) & (near < 3))
    take_in(cap, received, wide, rows)
    source = dot(pick, rows[...]).astype(BF)
    wait(*copies[:2])
    summed = dot(source, w14[...]) + dot(to, ends_v[...])
    wait(copies[2])
    message = finish(summed, w16[...]).astype(BF)
    summed = dot(to_t, message).astype(BF)
    wait(*copies[3:5])
    summed = base_v[...] + dot(summed, w18[...])
    wait(*copies[5:])
    out[...] = residual(one_v[...], finish(summed, w19[...]))


def run(kernel, outs, far, held, copies, macs=0, near_out=0, near=()):
    inside = pl.BlockSpec(memory_space=pltpu.VMEM)
    outside = pl.BlockSpec(memory_space=pltpu.HBM)
    moved = sum(a.size * a.dtype.itemsize for a in list(held) + list(outs))
    kept = len(outs) - near_out
    return pl.pallas_call(
        kernel,
        out_shape=tuple(
            pltpu.HBM(a.shape, a.dtype) if n < kept else a for n, a in enumerate(outs)
        ),
        in_specs=[inside] * len(near) + [outside] * len(far),
        out_specs=tuple(outside if n < kept else inside for n in range(len(outs))),
        scratch_shapes=[pltpu.VMEM(a.shape, a.dtype) for a in held] + [pltpu.SemaphoreType.DMA((copies,))],
        compiler_params=pltpu.CompilerParams(vmem_limit_bytes=24 * 2**20),
        cost_estimate=pl.CostEstimate(flops=2 * macs, bytes_accessed=moved, transcendentals=0),
    )(*near, *(pltpu.with_memory_space_constraint(a, pltpu.HBM) for a in far))


def exchange(rows, devices):
    parts = rows.reshape(devices, rows.shape[0] // devices, LANES)
    moved = lax.all_to_all(parts, AXES, split_axis=0, concat_axis=0, tiled=True)
    return moved.reshape(rows.shape)


def body(
    grid_latent,
    mesh_latent,
    weights,
    enc_dev,
    enc_row,
    enc_dst,
    proc_dev,
    proc_row,
    proc_dst,
    loc_src,
    loc_dst,
    dec_dev,
    dec_row,
):
    devices = lax.axis_size("band") * lax.axis_size("patch")
    edges = enc_dev.shape[0]
    cap = max(2, 2 * edges // devices)
    count, width = mesh_latent.shape
    total = devices * cap

    def arr(shape, dtype):
        return jax.ShapeDtypeStruct(shape, dtype)

    across = arr((1, edges), I32)
    row = arr((edges,), I32)
    loc = arr(loc_src.shape, I32)
    mat = arr((width, width), BF)
    nodes = arr((count, width), BF)
    nodes2 = arr((2 * count, width), BF)
    nodes32 = arr((count, width), F32)
    slot = arr((8, edges), I32)
    ask = arr((devices, LANES), I32)
    flat = arr((total * width // LANES, LANES), BF)
    flat32 = arr(flat.shape, F32)
    rows = arr((total, width), BF)
    edge_macs = edges * width * (total + 3 * width)
    devs = tuple(a.reshape(1, edges) for a in (enc_dev, proc_dev, dec_dev))
    (request,) = run(
        functools.partial(ask_kernel, cap, devices),
        (ask,),
        (*devs, enc_row, proc_row, dec_row),
        (across, across, across, row, row, row),
        6,
        macs=3 * devices * edges * (edges + LANES),
        near_out=1,
    )
    asked = request.reshape(devices, 1, LANES)
    wanted = lax.all_to_all(asked, AXES, split_axis=0, concat_axis=0, tiled=True).reshape(devices, LANES)
    grid_one, enc_ends, enc_base, dec_ends, dec_base, slots = run(
        functools.partial(prepare_kernel, devices),
        (nodes, nodes2, nodes32, nodes2, nodes32, slot),
        (grid_latent, mesh_latent, *devs, weights),
        (nodes, nodes, across, across, across) + (mat,) * 6 + (nodes, nodes2, nodes32, nodes2, nodes32, slot),
        17,
        macs=6 * count * width * width + 3 * devices * edges * edges,
    )
    (sent,) = run(
        functools.partial(serve_kernel, cap),
        (flat,),
        (wanted, grid_latent),
        (ask, nodes, flat32, flat),
        2 + PARTS,
        macs=total * count * width,
    )
    enc_rows = exchange(sent, devices)
    mesh_one, sent = run(
        functools.partial(enc_kernel, cap),
        (nodes, flat),
        (wanted, slots, enc_dst, enc_ends, enc_base, mesh_latent, weights),
        (ask, slot, row, nodes2, nodes32, nodes, mat, mat, mat, mat, nodes, flat32, flat, rows),
        11 + PARTS,
        macs=edge_macs,
        near=(enc_rows,),
    )
    proc_rows = exchange(sent, devices)
    proc_ends, proc_base, partial = run(
        local_kernel,
        (nodes2, nodes32, nodes32),
        (mesh_one, loc_src, loc_dst, weights),
        (nodes, mat, mat, mat, mat, loc, loc, nodes2, nodes32, nodes32),
        10,
        macs=7 * count * width * width,
    )
    (sent,) = run(
        functools.partial(proc_kernel, cap),
        (flat,),
        (wanted, slots, proc_dst, proc_ends, proc_base, partial, mesh_one, weights),
        (ask, slot, row, nodes2, nodes32, nodes32, nodes, mat, mat, mat, mat, flat32, flat, rows),
        11 + PARTS,
        macs=edge_macs,
        near=(proc_rows,),
    )
    dec_rows = exchange(sent, devices)
    (decoded,) = run(
        functools.partial(dec_kernel, cap),
        (nodes,),
        (slots, dec_ends, dec_base, grid_one, weights),
        (slot, nodes2, nodes32, nodes, mat, mat, mat, mat, flat32, rows),
        8,
        macs=edge_macs,
        near=(dec_rows,),
        near_out=1,
    )
    return decoded


def solution(mesh):
    rows = P(AXES, None)
    edge = P(AXES)
    in_specs = (rows, rows, P(), rows, edge, edge, rows, edge, edge, edge, edge, rows, edge)
    return jax.shard_map(body, mesh=mesh, in_specs=in_specs, out_specs=rows, check_vma=False)
```

time: 185 us -> 103 us (0.56)
  blocking collectives: 0 us -> 42.5 us
  waiting for transfers between devices: 63.1 us -> 26.2 us
  local copies, waits for them, and re-layouts: 36.9 us -> 0 us
  starting transfers between devices: 39.7 us -> 8.69 us
  matrix products: 25.6 us -> 0 us
  Pallas kernels: 0 us -> 24.7 us
  other arithmetic: 17.5 us -> 0 us
    all_to_all x0 -> x2, blocking collectives: none -> 42.5 us  [the longest x1 21.3 us: body(): lax.all_to_all(asked, AXES, split_axis=0, concat_axis=0, tiled=True)]
    all_to_all x6 -> x2, waiting for transfers between devices: 63.1 us -> 26.2 us  [exchange(): moved = lax.all_to_all(parts, AXES, split_axis=0, concat_axis=0, tiled=True)]
    all_to_all x6 -> x2, starting transfers between devices: 39.7 us -> 8.69 us  [exchange(): moved = lax.all_to_all(parts, AXES, split_axis=0, concat_axis=0, tiled=True)]
    dot_general x15 -> x0, matrix products: 25.6 us -> none  [the longest x7 12.9 us: perceptron(): jnp.dot(hidden, second, preferred_element_type=jnp.float32)]
    pallas_call x0 -> x7, Pallas kernels: none -> 24.7 us  [run(): pl.pallas_call(kernel, out_shape=tuple((pltpu.HBM(a.shape, a.dtype) if n...]
    gather x12 -> x0, local copies, waits for them, and re-layouts: 21 us -> none  [the longest x6 8.82 us: send_back(): picked = jnp.take(rows_table, wanted, axis=0)]
    scatter x3 -> x0, local copies, waits for them, and re-layouts: 9.24 us -> none  [make_request(): jnp.zeros((devices * capacity,), jnp.int32).at[slot_index].set(src_row)]
    select_n x14 -> x0, other arithmetic: 8.78 us -> none  [the longest x6 3.64 us: send_back(): picked = jnp.take(rows_table, wanted, axis=0)]
  transfers between devices with their start and end apart: 6 -> 2, of which waited for: 5 -> 2; matrix products, arithmetic and copies ran while one was open for 18% -> 0% of each run, Pallas kernels for 0% -> 7%
where the time goes in v3:
time: 103 us; the launch traced here: 102 us
  blocking collectives  42.5 us (41%)
  waiting for transfers between devices  26.2 us (25%)
  Pallas kernels  24.7 us (24%)
  starting transfers between devices  8.69 us (8%)
    all_to_all x2, waiting for transfers between devices, exchange(): moved = lax.all_to_all(parts, AXES, split_axis=0, concat_axis=0, tiled=True)  26.2 us
    pallas_call x7, Pallas kernels, run(): pl.pallas_call(kernel, out_shape=tuple((pltpu.HBM(a.shape, a.dtype) if n...  24.7 us
    all_to_all x1, blocking collectives, body(): lax.all_to_all(asked, AXES, split_axis=0, concat_axis=0, tiled=True)  21.3 us
    all_to_all x1, blocking collectives, exchange(): moved = lax.all_to_all(parts, AXES, split_axis=0, concat_axis=0, tiled=True)  21.2 us
    all_to_all x2, starting transfers between devices, exchange(): moved = lax.all_to_all(parts, AXES, split_axis=0, concat_axis=0, tiled=True)  8.69 us
  transfers between devices with their start and end apart: 2, of which 2 were waited for; matrix products, arithmetic and copies ran while one was open for 0% of the time, Pallas kernels for 7%

profile of v3, /device:TPU:1, one launch (start us, length us, event | category | flops | bytes accessed | tf_op | source)
XLA Modules:
  0.0 102.2 jit_solution(5048424806849089848)
XLA Ops:
  0.0 1.5 %shard_map.127 = s32[128,128]{1,0:T(8,128)S(1)} custom-call(s32[1,384]{1,0:T(1,128)} %bitcast.23, s32[1,384]{1,0:T(1,128)} %bitcast.25, s32[1,384]{1,0:T(1,128)} %bitcast.27, s32[384]{0:T(512)} %row0.1, s32[384]{0:T(512)} %row1.1, s32[384]{0:T(512)} %row2.1), custom_call_target="tpu_custom_call" | custom-call | flops 150994944 | bytes 74752 | tf_op jit(solution)/shard_map/pallas_call | solution.py:301
  1.5 21.3 %all_to_all.20 = s32[128,1,128]{2,1,0:T(1,128)} all-to-all(s32[128,1,128]{2,1,0:T(1,128)S(1)} %bitcast.16), channel_id=1, replica_groups=mesh['band'=8,'patch'=16] {'band','patch'}, dimensions={0} | all-to-all | bytes 131072 | tf_op jit(solution)/shard_map/all_to_all | solution.py:368
  22.9 2.4 %shard_map.128 = bf16[3072,128]{1,0:T(8,128)(2,1)} custom-call(s32[128,128]{1,0:T(8,128)} %bitcast.19, bf16[128,512]{1,0:T(8,128)(2,1)} %grid.1), custom_call_target="tpu_custom_call" | custom-call | flops 100663296 | bytes 3342336 | tf_op jit(solution)/shard_map/pallas_call | solution.py:301
  25.3 4.4 %all-to-all-start.1 = ((bf16[128,24,128]{2,1,0:T(8,128)(2,1)}), bf16[128,24,128]{2,1,0:T(8,128)(2,1)S(1)}, u32[]{:S(2)}, u32[]{:S(2)}) async-start(bf16[128,24,128]{2,1,0:T(8,128)(2,1)} %bitcast.18), calls=%async_computation.1 | async-start | bytes 1572864 | tf_op jit(solution)/shard_map/all_to_all | solution.py:316
  29.7 3.6 %shard_map.129 = (bf16[128,512]{1,0:T(8,128)(2,1)}, bf16[256,512]{1,0:T(8,128)(2,1)}, f32[128,512]{1,0:T(8,128)}, bf16[256,512]{1,0:T(8,128)(2,1)}, f32[128,512]{1,0:T(8,128)}, /*index=5*/s32[8,384]{1,0:T(8,128)}) custom-call(bf16[128,512]{1,0:T(8,128)(2,1)} %grid.1, bf16[128,512]{1,0:T(8,128)(2,1)} %mesh.3, s32[1,384]{1,0:T(1,128)} %bitcast.24, ...), custom_call_target="tpu_custom_call" | custom-call | flops 515899392 | bytes 5796352 | tf_op jit(solution)/shard_map/pallas_call | solution.py:301
  33.3 13.1 %all-to-all-done.1 = bf16[128,24,128]{2,1,0:T(8,128)(2,1)S(1)} async-done(((bf16[128,24,128]{2,1,0:T(8,128)(2,1)}), bf16[128,24,128]{2,1,0:T(8,128)(2,1)S(1)}, u32[]{:S(2)}, u32[]{:S(2)}) %all-to-all-start.1) | async-done | bytes 786464 | tf_op jit(solution)/shard_map/all_to_all | solution.py:316
  46.4 4.7 %shard_map.130 = (bf16[128,512]{1,0:T(8,128)(2,1)}, bf16[3072,128]{1,0:T(8,128)(2,1)}) custom-call(bf16[3072,128]{1,0:T(8,128)(2,1)S(1)} %bitcast.15, s32[128,128]{1,0:T(8,128)} %bitcast.20, s32[8,384]{1,0:T(8,128)} %get-tuple-element.16.slots, s32[384]{0:T(512)} %dst.2, bf16[256,512]{1,0:T(8,128)(2,1)} %get-tuple-element.17.ends, ...), custom_call_target="tpu_custom_call" | custom-call | flops 905969664 | bytes 7026176 | tf_op jit(solution)/shard_map/pallas_call | solution.py:301
  51.2 4.3 %all-to-all-start.2 = ((bf16[128,24,128]{2,1,0:T(8,128)(2,1)}), bf16[128,24,128]{2,1,0:T(8,128)(2,1)S(1)}, u32[]{:S(2)}, u32[]{:S(2)}) async-start(bf16[128,24,128]{2,1,0:T(8,128)(2,1)} %bitcast.22), calls=%async_computation.2 | async-start | bytes 1572864 | tf_op jit(solution)/shard_map/all_to_all | solution.py:316
  55.4 3.6 %shard_map.131 = (bf16[256,512]{1,0:T(8,128)(2,1)}, f32[128,512]{1,0:T(8,128)}, f32[128,512]{1,0:T(8,128)}) custom-call(bf16[128,512]{1,0:T(8,128)(2,1)} %get-tuple-element.20.one, s32[256]{0:T(256)} %loc_src.1, s32[256]{0:T(256)} %loc_dst.1, bf16[20,512,512]{2,1,0:T(8,128)(2,1)} %w.9), custom_call_target="tpu_custom_call" | custom-call | flops 469762048 | bytes 3803136 | tf_op jit(solution)/shard_map/pallas_call | solution.py:301
  59.0 13.2 %all-to-all-done.2 = bf16[128,24,128]{2,1,0:T(8,128)(2,1)S(1)} async-done(((bf16[128,24,128]{2,1,0:T(8,128)(2,1)}), bf16[128,24,128]{2,1,0:T(8,128)(2,1)S(1)}, u32[]{:S(2)}, u32[]{:S(2)}) %all-to-all-start.2) | async-done | bytes 786464 | tf_op jit(solution)/shard_map/all_to_all | solution.py:316
  72.1 4.8 %shard_map.132 = bf16[3072,128]{1,0:T(8,128)(2,1)} custom-call(bf16[3072,128]{1,0:T(8,128)(2,1)S(1)} %bitcast.13, s32[128,128]{1,0:T(8,128)} %bitcast.21, s32[8,384]{1,0:T(8,128)} %get-tuple-element.16.slots, s32[384]{0:T(512)} %dst.3, bf16[256,512]{1,0:T(8,128)(2,1)} %get-tuple-element.21.ends, f32[128,512]{1,0:T(8,128)} %get-tuple-element.22.base, ...), custom_call_target="tpu_custom_call" | custom-call | flops 905969664 | bytes 7026176 | tf_op jit(solution)/shard_map/pallas_call | solution.py:301
  77.0 21.2 %all_to_all.21 = bf16[128,24,128]{2,1,0:T(8,128)(2,1)S(1)} all-to-all(bf16[128,24,128]{2,1,0:T(8,128)(2,1)} %bitcast.17), channel_id=1, replica_groups=mesh['band'=8,'patch'=16] {'band','patch'}, dimensions={0} | all-to-all | bytes 1572864 | tf_op jit(solution)/shard_map/all_to_all | solution.py:316
  98.2 4.1 %shard_map.133 = bf16[128,512]{1,0:T(8,128)(2,1)} custom-call(bf16[3072,128]{1,0:T(8,128)(2,1)S(1)} %bitcast.14, s32[8,384]{1,0:T(8,128)} %get-tuple-element.16.slots, bf16[256,512]{1,0:T(8,128)(2,1)} %get-tuple-element.24.ends, f32[128,512]{1,0:T(8,128)} %get-tuple-element.25.base, bf16[128,512]{1,0:T(8,128)(2,1)} %get-tuple-element.26.one, ...), custom_call_target="tpu_custom_call" | custom-call | flops 905969664 | bytes 5255168 | tf_op jit(solution)/shard_map/pallas_call | solution.py:301
Async XLA Ops:
  25.3 21.2 %all-to-all-start.1 = ((bf16[128,24,128]{2,1,0:T(8,128)(2,1)}), bf16[128,24,128]{2,1,0:T(8,128)(2,1)S(1)}, u32[]{:S(2)}, u32[]{:S(2)}) async-start(bf16[128,24,128]{2,1,0:T(8,128)(2,1)} %bitcast.18), calls=%async_computation.1 | async-start | bytes 1572864 | tf_op jit(solution)/shard_map/all_to_all | solution.py:316
  51.2 21.0 %all-to-all-start.2 = ((bf16[128,24,128]{2,1,0:T(8,128)(2,1)}), bf16[128,24,128]{2,1,0:T(8,128)(2,1)S(1)}, u32[]{:S(2)}, u32[]{:S(2)}) async-start(bf16[128,24,128]{2,1,0:T(8,128)(2,1)} %bitcast.22), calls=%async_computation.2 | async-start | bytes 1572864 | tf_op jit(solution)/shard_map/all_to_all | solution.py:316

commit v4 on v3

v4 whole, which is shorter than its diff:
```python
import functools

import jax
import jax.numpy as jnp
from jax import lax
from jax.experimental import pallas as pl
from jax.experimental.pallas import tpu as pltpu
from jax.sharding import PartitionSpec as P

AXES = ("band", "patch")
EPSILON = 1e-05
LANES = 128
BF = jnp.bfloat16
F32 = jnp.float32
I32 = jnp.int32


def dot(a, b):
    return jnp.dot(a, b, preferred_element_type=F32)


def dot_lanes(a, b):
    return lax.dot_general(a, b, (((1,), (1,)), ((), ())), preferred_element_type=F32)


def iota(shape, axis):
    return lax.broadcasted_iota(I32, shape, axis)


def flag(condition):
    return jnp.where(condition, 1.0, 0.0).astype(BF)


def column(row):
    count = row.shape[1]
    same = iota((count, count), 0) == iota((count, count), 1)
    return jnp.sum(jnp.where(same, row.astype(F32), 0.0), axis=1, keepdims=True).astype(I32)


def choose(row, count):
    return flag(iota((row.shape[1], count), 1) == column(row))


def choose_t(row, count):
    return flag(iota((count, row.shape[1]), 0) == row)


def line(ref):
    return ref[...].reshape(1, ref.shape[0])


def silu(v):
    return 0.5 * v * (1.0 + jnp.tanh(0.5 * v))


def finish(summed, second):
    out = dot(silu(summed).astype(BF), second)
    centred = out - jnp.mean(out, axis=-1, keepdims=True)
    spread = jnp.mean(centred * centred, axis=-1, keepdims=True)
    return centred * lax.rsqrt(spread + EPSILON)


def residual(base, update):
    return (base.astype(F32) + update).astype(BF)


def halves(values):
    high = values.astype(BF)
    return jnp.concatenate([high, (values - high.astype(F32)).astype(BF)], axis=0)


def twice(chosen):
    return jnp.concatenate([chosen, chosen], axis=1)


def start(sems, first, *pairs):
    copies = [pltpu.make_async_copy(src, dst, sems.at[first + n]) for n, (src, dst) in enumerate(pairs)]
    for copy in copies:
        copy.start()
    return copies


def wait(*copies):
    for copy in copies:
        copy.wait()


def places(source, devices):
    edges = source.shape[1]
    earlier = flag(iota((edges, edges), 0) < iota((edges, edges), 1))
    hit = iota((devices, edges), 0) == source
    hits = flag(hit)
    return jnp.sum(jnp.where(hit, dot(hits, earlier), 0.0), axis=0, keepdims=True).astype(I32), hits


def fence(ref):
    def step(n, carry):
        ref[pl.ds(pl.multiple_of(n * 8, 8), 8), :] = jnp.zeros((8, ref.shape[1]), ref.dtype)
        return carry

    lax.fori_loop(0, 2, step, 0)


def serve(asked, kind, cap, table, wide, packed, out, sem):
    devices = asked.shape[0]
    blocks = table.shape[1] // LANES
    lanes = iota((devices, table.shape[0]), 1)
    for slot in range(cap):
        lane = kind * cap + slot
        got = dot(flag(asked[:, lane : lane + 1] == lanes), table)
        for block in range(blocks):
            target = pl.ds(slot * blocks + block, devices, stride=cap * blocks)
            wide[target, :] = got[:, block * LANES : (block + 1) * LANES]
    packed[...] = wide[...].astype(BF)
    copy = pltpu.make_async_copy(packed, out, sem)
    copy.start()
    return copy


def take_in(cap, packed, wide, rows):
    blocks = rows.shape[1] // LANES
    devices = rows.shape[0] // cap
    wide[...] = packed[...].astype(F32)
    for slot in range(cap):
        for block in range(blocks):
            source = pl.ds(slot * blocks + block, devices, stride=cap * blocks)
            target = pl.ds(slot * devices, devices)
            rows[target, block * LANES : (block + 1) * LANES] = wide[source, :].astype(BF)


def whole(kept, first, count):
    return kept[first : first + count, :].astype(F32) + kept[first + count : first + 2 * count, :].astype(F32)


def ask_kernel(cap, devices, dev0, dev1, dev2, row0, row1, row2, grid, request, g, *scratch):
    lines, sems = scratch[:6], scratch[6]
    copies = start(sems, 0, *zip((dev0, dev1, dev2, row0, row1, row2), lines), (grid, g))
    wait(*copies[:6])
    total = jnp.zeros(request.shape, F32)
    for kind in range(3):
        place, hits = places(lines[kind][...], devices)
        row = line(lines[3 + kind]).astype(F32)
        mine = iota((request.shape[1], row.shape[1]), 0) == place + kind * cap
        total = total + dot_lanes(hits, jnp.where(mine, row, 0.0).astype(BF))
    request[...] = total.astype(I32)
    wait(copies[6])


def serve_kernel(cap, asked, table, out, wide, packed, sems):
    serve(asked[...], 0, cap, table[...], wide, packed, out, sems.at[0]).wait()


def prepare_kernel(
    devices, grid, mesh, dev0, dev1, dev2, dst0, dst1, w, lines, kept, ws, one,
    g, d0, d1, d2, e0, e1, w6, w7, w1, w3, one_v, sems,
):
    count = g.shape[0]
    m = kept.at[pl.ds(4 * count, count)]
    copies = start(
        sems, 0, (dev0, d0), (dev1, d1), (dev2, d2), (dst0, e0), (dst1, e1), (mesh, m), (w.at[1], w1),
        (w.at[3], w3), (grid, g), (w.at[6], w6), (w.at[7], w7), (w.at[0], ws.at[0]), (w.at[2], ws.at[1]),
    )
    wait(*copies[:5])
    for kind, dev in enumerate((d0, d1, d2)):
        source = dev[...]
        lines[kind : kind + 1, :] = places(source, devices)[0] * devices + source
    lines[3:4, :] = line(e0)
    lines[4:5, :] = line(e1)
    wait(*copies[5:7])
    kept[: 2 * count, :] = halves(dot(m[...], w1[...]))
    wait(copies[7])
    kept[2 * count : 4 * count, :] = halves(dot(m[...], w3[...]))
    wait(*copies[8:11])
    one_v[...] = residual(g[...], finish(dot(g[...], w6[...]), w7[...]))
    wait(*copies[11:], *start(sems, len(copies), (one_v, one)))


def enc_kernel(cap, received, asked, lines, kept, ws, w, one, out, w4, w5, one_v, wide, packed, rows, sems):
    copies = start(sems, 0, (w.at[4], w4), (w.at[5], w5))
    fence(wide)
    count = one_v.shape[0]
    pick = choose(lines[0:1, :], rows.shape[0])
    to = twice(choose(lines[3:4, :], count))
    to_t = choose_t(lines[3:4, :], count)
    take_in(cap, received, wide, rows)
    source = dot(pick, rows[...]).astype(BF)
    summed = dot(source, ws[0]) + dot(to, kept[: 2 * count, :])
    message = finish(summed, ws[1]).astype(BF)
    summed = dot(to_t, message).astype(BF)
    wait(copies[0])
    summed = whole(kept, 2 * count, count) + dot(summed, w4[...])
    wait(copies[1])
    mine = residual(kept[4 * count :, :], finish(summed, w5[...]))
    one_v[...] = mine
    wait(*start(sems, 2, (one_v, one)), serve(asked[...], 1, cap, mine, wide, packed, out, sems.at[3]))


def local_kernel(one, loc_src, loc_dst, w, kept, ws, w9, w11, s, d, sems):
    count = one.shape[0]
    mine = kept.at[pl.ds(6 * count, count)]
    copies = start(
        sems, 0, (one, mine), (w.at[9], w9), (loc_src, s), (loc_dst, d), (w.at[8], ws.at[0]), (w.at[10], ws.at[1]),
        (w.at[11], w11),
    )
    wait(*copies[:2])
    kept[: 2 * count, :] = halves(dot(mine[...], w9[...]))
    wait(*copies[2:5])
    begin = dot(twice(choose(line(s), count)), halves(dot(mine[...], ws[0])))
    stop = line(d)
    wait(copies[5])
    message = finish(begin + dot(twice(choose(stop, count)), kept[: 2 * count, :]), ws[1]).astype(BF)
    kept[4 * count : 6 * count, :] = halves(dot(choose_t(stop, count), message))
    wait(copies[6])
    kept[2 * count : 4 * count, :] = halves(dot(mine[...], w11[...]))


def proc_kernel(cap, received, asked, lines, kept, ws, w, out, w12, w13, wide, packed, rows, sems):
    copies = start(sems, 0, (w.at[12], w12), (w.at[13], w13))
    fence(wide)
    count = kept.shape[0] // 7
    pick = choose(lines[1:2, :], rows.shape[0])
    to = twice(choose(lines[4:5, :], count))
    to_t = choose_t(lines[4:5, :], count)
    take_in(cap, received, wide, rows)
    source = dot(pick, rows[...]).astype(BF)
    summed = dot(source, ws[0]) + dot(to, kept[: 2 * count, :])
    message = finish(summed, ws[1]).astype(BF)
    summed = (whole(kept, 4 * count, count) + dot(to_t, message)).astype(BF)
    wait(copies[0])
    summed = whole(kept, 2 * count, count) + dot(summed, w12[...])
    wait(copies[1])
    two = residual(kept[6 * count :, :], finish(summed, w13[...]))
    serve(asked[...], 2, cap, two, wide, packed, out, sems.at[2]).wait()


def last_kernel(grid_one, w, kept, ws, w15, w17, sems):
    count = grid_one.shape[0]
    one = kept.at[pl.ds(4 * count, count)]
    copies = start(
        sems, 0, (grid_one, one), (w.at[15], w15), (w.at[17], w17), (w.at[14], ws.at[0]), (w.at[16], ws.at[1])
    )
    wait(*copies[:2])
    kept[: 2 * count, :] = halves(dot(one[...], w15[...]))
    wait(copies[2])
    kept[2 * count : 4 * count, :] = halves(dot(one[...], w17[...]))
    wait(*copies[3:])


def dec_kernel(cap, received, lines, kept, ws, w, out, w18, w19, wide, rows, sems):
    copies = start(sems, 0, (w.at[18], w18), (w.at[19], w19))
    fence(wide)
    edges = lines.shape[1]
    count = kept.shape[0] // 5
    pick = choose(lines[2:3, :], rows.shape[0])
    near = iota((edges, count), 0) - 3 * iota((edges, count), 1)
    to = twice(flag((near >= 0) & (near < 3)))
    near = iota((count, edges), 1) - 3 * iota((count, edges), 0)
    to_t = flag((near >= 0) & (near < 3))
    take_in(cap, received, wide, rows)
    source = dot(pick, rows[...]).astype(BF)
    summed = dot(source, ws[0]) + dot(to, kept[: 2 * count, :])
    message = finish(summed, ws[1]).astype(BF)
    summed = dot(to_t, message).astype(BF)
    wait(copies[0])
    summed = whole(kept, 2 * count, count) + dot(summed, w18[...])
    wait(copies[1])
    out[...] = residual(kept[4 * count :, :], finish(summed, w19[...]))


def run(kernel, outs=(), near=(), far=(), held=(), copies=0, macs=0, away=(), last=False):
    inside = pl.BlockSpec(memory_space=pltpu.VMEM)
    outside = pl.BlockSpec(memory_space=pltpu.HBM)
    moved = sum(a.size * a.dtype.itemsize for a in list(held) + list(outs))
    return pl.pallas_call(
        kernel,
        out_shape=(
            *(a if last else pltpu.VMEM(a.shape, a.dtype) for a in outs),
            *(pltpu.HBM(a.shape, a.dtype) for a in away),
        ),
        in_specs=[inside] * len(near) + [outside] * len(far),
        out_specs=(inside,) * len(outs) + (outside,) * len(away),
        scratch_shapes=[pltpu.VMEM(a.shape, a.dtype) for a in held] + [pltpu.SemaphoreType.DMA((copies,))],
        compiler_params=pltpu.CompilerParams(vmem_limit_bytes=16 * 2**20),
        cost_estimate=pl.CostEstimate(flops=2 * macs, bytes_accessed=moved, transcendentals=0),
    )(
        *(pltpu.with_memory_space_constraint(a, pltpu.VMEM) for a in near),
        *(pltpu.with_memory_space_constraint(a, pltpu.HBM) for a in far),
    )


def exchange(rows, devices):
    parts = rows.reshape(devices, rows.shape[0] // devices, LANES)
    moved = lax.all_to_all(parts, AXES, split_axis=0, concat_axis=0, tiled=True)
    return moved.reshape(rows.shape)


def body(
    grid_latent,
    mesh_latent,
    weights,
    enc_dev,
    enc_row,
    enc_dst,
    proc_dev,
    proc_row,
    proc_dst,
    loc_src,
    loc_dst,
    dec_dev,
    dec_row,
):
    devices = lax.axis_size("band") * lax.axis_size("patch")
    edges = enc_dev.shape[0]
    cap = max(2, 2 * edges // devices)
    count, width = mesh_latent.shape
    total = devices * cap

    def arr(shape, dtype):
        return jax.ShapeDtypeStruct(shape, dtype)

    across = arr((1, edges), I32)
    row = arr((edges,), I32)
    loc = arr(loc_src.shape, I32)
    mat = arr((width, width), BF)
    mats = arr((2, width, width), BF)
    nodes = arr((count, width), BF)
    lines = arr((8, edges), I32)
    ask = arr((devices, LANES), I32)
    flat = arr((total * width // LANES, LANES), BF)
    flat32 = arr(flat.shape, F32)
    rows = arr((total, width), BF)
    edge_macs = edges * width * (total + 3 * width)
    devs = tuple(a.reshape(1, edges) for a in (enc_dev, proc_dev, dec_dev))

    def kept(parts):
        return arr((parts * count, width), BF)

    request, grid = run(
        functools.partial(ask_kernel, cap, devices),
        (ask, nodes),
        far=(*devs, enc_row, proc_row, dec_row, grid_latent),
        held=(across, across, across, row, row, row),
        copies=7,
        macs=3 * devices * edges * (edges + LANES),
    )
    asked = request.reshape(devices, 1, LANES)
    wanted = lax.all_to_all(asked, AXES, split_axis=0, concat_axis=0, tiled=True).reshape(devices, LANES)
    (sent,) = run(
        functools.partial(serve_kernel, cap),
        near=(wanted, grid),
        held=(flat32, flat),
        copies=1,
        macs=total * count * width,
        away=(flat,),
    )
    enc_rows = exchange(sent, devices)
    places_of, enc_kept, enc_ws, grid_one = run(
        functools.partial(prepare_kernel, devices),
        (lines, kept(5), mats),
        far=(grid_latent, mesh_latent, *devs, enc_dst, proc_dst, weights),
        held=(nodes, across, across, across, row, row, mat, mat, mat, mat, nodes),
        copies=14,
        macs=6 * count * width * width + 3 * devices * edges * edges,
        away=(nodes,),
    )
    mesh_one, sent = run(
        functools.partial(enc_kernel, cap),
        near=(enc_rows, wanted, places_of, enc_kept, enc_ws),
        far=(weights,),
        held=(mat, mat, nodes, flat32, flat, rows),
        copies=4,
        macs=edge_macs,
        away=(nodes, flat),
    )
    proc_rows = exchange(sent, devices)
    proc_kept, proc_ws = run(
        local_kernel,
        (kept(7), mats),
        far=(mesh_one, loc_src, loc_dst, weights),
        held=(mat, mat, loc, loc),
        copies=7,
        macs=7 * count * width * width,
    )
    (sent,) = run(
        functools.partial(proc_kernel, cap),
        near=(proc_rows, wanted, places_of, proc_kept, proc_ws),
        far=(weights,),
        held=(mat, mat, flat32, flat, rows),
        copies=3,
        macs=edge_macs,
        away=(flat,),
    )
    dec_rows = exchange(sent, devices)
    dec_kept, dec_ws = run(
        last_kernel,
        (kept(5), mats),
        far=(grid_one, weights),
        held=(mat, mat),
        copies=5,
        macs=2 * count * width * width,
    )
    (decoded,) = run(
        functools.partial(dec_kernel, cap),
        (nodes,),
        near=(dec_rows, places_of, dec_kept, dec_ws),
        far=(weights,),
        held=(mat, mat, flat32, rows),
        copies=2,
        macs=edge_macs,
        last=True,
    )
    return decoded


def solution(mesh):
    rows = P(AXES, None)
    edge = P(AXES)
    in_specs = (rows, rows, P(), rows, edge, edge, rows, edge, edge, edge, edge, rows, edge)
    return jax.shard_map(body, mesh=mesh, in_specs=in_specs, out_specs=rows, check_vma=False)
```

time: 103 us -> 97.9 us (0.950)
  blocking collectives: 42.5 us -> 20.9 us
  waiting for transfers between devices: 26.2 us -> 42.5 us
  starting transfers between devices: 8.69 us -> 13 us
  Pallas kernels: 24.7 us -> 21 us
    all_to_all x1 -> x0, blocking collectives: 21.2 us -> none  [exchange(): moved = lax.all_to_all(parts, AXES, split_axis=0, concat_axis=0, tiled=True)]
    all_to_all x2 -> x3, waiting for transfers between devices: 26.2 us -> 42.5 us  [exchange(): moved = lax.all_to_all(parts, AXES, split_axis=0, concat_axis=0, tiled=True)]
    all_to_all x2 -> x3, starting transfers between devices: 8.69 us -> 13 us  [exchange(): moved = lax.all_to_all(parts, AXES, split_axis=0, concat_axis=0, tiled=True)]
    pallas_call x7 -> x8, Pallas kernels: 24.7 us -> 21 us  [run(): pl.pallas_call(kernel, out_shape=(*(a if last else pltpu.VMEM(a.shape, a....]
  transfers between devices with their start and end apart: 2 -> 3, of which waited for: 2 -> 3; matrix products, arithmetic and copies ran while one was open for 0% -> 0% of each run, Pallas kernels for 7% -> 8%
where the time goes in v4:
time: 97.9 us; the launch traced here: 97.5 us
  waiting for transfers between devices  42.5 us (43%)
  Pallas kernels  21 us (21%)
  blocking collectives  20.9 us (21%)
  starting transfers between devices  13 us (13%)
    all_to_all x3, waiting for transfers between devices, exchange(): moved = lax.all_to_all(parts, AXES, split_axis=0, concat_axis=0, tiled=True)  42.5 us
    pallas_call x8, Pallas kernels, run(): pl.pallas_call(kernel, out_shape=(*(a if last else pltpu.VMEM(a.shape, a....  21 us
    all_to_all x1, blocking collectives, body(): lax.all_to_all(asked, AXES, split_axis=0, concat_axis=0, tiled=True)  20.9 us
    all_to_all x3, starting transfers between devices, exchange(): moved = lax.all_to_all(parts, AXES, split_axis=0, concat_axis=0, tiled=True)  13 us
  transfers between devices with their start and end apart: 3, of which 3 were waited for; matrix products, arithmetic and copies ran while one was open for 0% of the time, Pallas kernels for 8%

profile of v4, /device:TPU:1, one launch (start us, length us, event | category | flops | bytes accessed | tf_op | source)
XLA Modules:
  0.0 97.5 jit_solution(15977075226135223344)
XLA Ops:
  0.0 1.5 %shard_map.127 = (s32[128,128]{1,0:T(8,128)S(1)}, bf16[128,512]{1,0:T(8,128)(2,1)S(1)}) custom-call(s32[1,384]{1,0:T(1,128)} %bitcast.23, s32[1,384]{1,0:T(1,128)} %bitcast.25, s32[1,384]{1,0:T(1,128)} %bitcast.27, s32[384]{0:T(512)} %row0.1, s32[384]{0:T(512)} %row1.1, s32[384]{0:T(512)} %row2.1, bf16[128,512]{1,0:T(8,128)(2,1)} %grid.3), custom_call_target="tpu_custom_call" | custom-call | flops 150994944 | bytes 205824 | tf_op jit(solution)/shard_map/pallas_call | solution.py:274
  1.5 20.9 %all_to_all.20 = s32[128,1,128]{2,1,0:T(1,128)S(1)} all-to-all(s32[128,1,128]{2,1,0:T(1,128)S(1)} %bitcast.19), channel_id=1, replica_groups=mesh['band'=8,'patch'=16] {'band','patch'}, dimensions={0} | all-to-all | bytes 131072 | tf_op jit(solution)/shard_map/all_to_all | solution.py:347
  22.4 1.4 %shard_map.128 = bf16[3072,128]{1,0:T(8,128)(2,1)} custom-call(s32[128,128]{1,0:T(8,128)S(1)} %bitcast.16, bf16[128,512]{1,0:T(8,128)(2,1)S(1)} %get-tuple-element.18.table), custom_call_target="tpu_custom_call" | custom-call | flops 100663296 | bytes 2359296 | tf_op jit(solution)/shard_map/pallas_call | solution.py:274
  23.9 4.5 %all-to-all-start.1 = ((bf16[128,24,128]{2,1,0:T(8,128)(2,1)}), bf16[128,24,128]{2,1,0:T(8,128)(2,1)S(1)}, u32[]{:S(2)}, u32[]{:S(2)}) async-start(bf16[128,24,128]{2,1,0:T(8,128)(2,1)} %bitcast.21), calls=%async_computation.1 | async-start | bytes 1572864 | tf_op jit(solution)/shard_map/all_to_all | solution.py:293
  28.4 3.1 %shard_map.129 = (s32[8,384]{1,0:T(8,128)S(1)}, bf16[640,512]{1,0:T(8,128)(2,1)S(1)}, bf16[2,512,512]{2,1,0:T(8,128)(2,1)S(1)}, bf16[128,512]{1,0:T(8,128)(2,1)}) custom-call(bf16[128,512]{1,0:T(8,128)(2,1)} %grid.3, bf16[128,512]{1,0:T(8,128)(2,1)} %mesh.1, s32[1,384]{1,0:T(1,128)} %bitcast.24, s32[1,384]{1,0:T(1,128)} %bitcast.26, s32[1,384]{1,0:T(1,128)} %bitcast.28, ...), custom_call_target="tpu_custom_call" | custom-call | flops 515899392 | bytes 4083200 | tf_op jit(solution)/shard_map/pallas_call | solution.py:274
  31.5 13.5 %all-to-all-done.1 = bf16[128,24,128]{2,1,0:T(8,128)(2,1)S(1)} async-done(((bf16[128,24,128]{2,1,0:T(8,128)(2,1)}), bf16[128,24,128]{2,1,0:T(8,128)(2,1)S(1)}, u32[]{:S(2)}, u32[]{:S(2)}) %all-to-all-start.1) | async-done | bytes 786464 | tf_op jit(solution)/shard_map/all_to_all | solution.py:293
  45.0 3.7 %shard_map.130 = (bf16[128,512]{1,0:T(8,128)(2,1)}, bf16[3072,128]{1,0:T(8,128)(2,1)}) custom-call(bf16[3072,128]{1,0:T(8,128)(2,1)S(1)} %bitcast.14, s32[128,128]{1,0:T(8,128)S(1)} %bitcast.17, s32[8,384]{1,0:T(8,128)S(1)} %get-tuple-element.19.lines, bf16[640,512]{1,0:T(8,128)(2,1)S(1)} %get-tuple-element.20.kept, ...), custom_call_target="tpu_custom_call" | custom-call | flops 905969664 | bytes 4325376 | tf_op jit(solution)/shard_map/pallas_call | solution.py:274
  48.8 4.3 %all-to-all-start.2 = ((bf16[128,24,128]{2,1,0:T(8,128)(2,1)}), bf16[128,24,128]{2,1,0:T(8,128)(2,1)S(1)}, u32[]{:S(2)}, u32[]{:S(2)}) async-start(bf16[128,24,128]{2,1,0:T(8,128)(2,1)} %bitcast.22), calls=%async_computation.2 | async-start | bytes 1572864 | tf_op jit(solution)/shard_map/all_to_all | solution.py:293
  53.0 2.8 %shard_map.131 = (bf16[896,512]{1,0:T(8,128)(2,1)S(1)}, bf16[2,512,512]{2,1,0:T(8,128)(2,1)S(1)}) custom-call(bf16[128,512]{1,0:T(8,128)(2,1)} %get-tuple-element.23.one, s32[256]{0:T(256)} %loc_src.1, s32[256]{0:T(256)} %loc_dst.1, bf16[20,512,512]{2,1,0:T(8,128)(2,1)} %w.11), custom_call_target="tpu_custom_call" | custom-call | flops 469762048 | bytes 3016704 | tf_op jit(solution)/shard_map/pallas_call | solution.py:274
  55.9 13.9 %all-to-all-done.2 = bf16[128,24,128]{2,1,0:T(8,128)(2,1)S(1)} async-done(((bf16[128,24,128]{2,1,0:T(8,128)(2,1)}), bf16[128,24,128]{2,1,0:T(8,128)(2,1)S(1)}, u32[]{:S(2)}, u32[]{:S(2)}) %all-to-all-start.2) | async-done | bytes 786464 | tf_op jit(solution)/shard_map/all_to_all | solution.py:293
  69.7 3.7 %shard_map.132 = bf16[3072,128]{1,0:T(8,128)(2,1)} custom-call(bf16[3072,128]{1,0:T(8,128)(2,1)S(1)} %bitcast.13, s32[128,128]{1,0:T(8,128)S(1)} %bitcast.18, s32[8,384]{1,0:T(8,128)S(1)} %get-tuple-element.19.lines, bf16[896,512]{1,0:T(8,128)(2,1)S(1)} %get-tuple-element.24.kept, bf16[2,512,512]{2,1,0:T(8,128)(2,1)S(1)} %get-tuple-element.25.ws, ...), custom_call_target="tpu_custom_call" | custom-call | flops 905969664 | bytes 4194304 | tf_op jit(solution)/shard_map/pallas_call | solution.py:274
  73.5 4.3 %all-to-all-start.3 = ((bf16[128,24,128]{2,1,0:T(8,128)(2,1)}), bf16[128,24,128]{2,1,0:T(8,128)(2,1)S(1)}, u32[]{:S(2)}, u32[]{:S(2)}) async-start(bf16[128,24,128]{2,1,0:T(8,128)(2,1)} %bitcast.20), calls=%async_computation.3 | async-start | bytes 1572864 | tf_op jit(solution)/shard_map/all_to_all | solution.py:293
  77.7 1.6 %shard_map.133 = (bf16[640,512]{1,0:T(8,128)(2,1)S(1)}, bf16[2,512,512]{2,1,0:T(8,128)(2,1)S(1)}) custom-call(bf16[128,512]{1,0:T(8,128)(2,1)} %get-tuple-element.26.grid_one, bf16[20,512,512]{2,1,0:T(8,128)(2,1)} %w.11), custom_call_target="tpu_custom_call" | custom-call | flops 134217728 | bytes 2752512 | tf_op jit(solution)/shard_map/pallas_call | solution.py:274
  79.4 15.1 %all-to-all-done.3 = bf16[128,24,128]{2,1,0:T(8,128)(2,1)S(1)} async-done(((bf16[128,24,128]{2,1,0:T(8,128)(2,1)}), bf16[128,24,128]{2,1,0:T(8,128)(2,1)S(1)}, u32[]{:S(2)}, u32[]{:S(2)}) %all-to-all-start.3) | async-done | bytes 786464 | tf_op jit(solution)/shard_map/all_to_all | solution.py:293
  94.5 3.0 %shard_map.134 = bf16[128,512]{1,0:T(8,128)(2,1)} custom-call(bf16[3072,128]{1,0:T(8,128)(2,1)S(1)} %bitcast.15, s32[8,384]{1,0:T(8,128)S(1)} %get-tuple-element.19.lines, bf16[640,512]{1,0:T(8,128)(2,1)S(1)} %get-tuple-element.27.kept, bf16[2,512,512]{2,1,0:T(8,128)(2,1)S(1)} %get-tuple-element.28.ws, bf16[20,512,512]{2,1,0:T(8,128)(2,1)} %w.11), custom_call_target="tpu_custom_call" | custom-call | flops 905969664 | bytes 3538944 | tf_op jit(solution)/shard_map/pallas_call | solution.py:274
Async XLA Ops:
  23.9 21.1 %all-to-all-start.1 = ((bf16[128,24,128]{2,1,0:T(8,128)(2,1)}), bf16[128,24,128]{2,1,0:T(8,128)(2,1)S(1)}, u32[]{:S(2)}, u32[]{:S(2)}) async-start(bf16[128,24,128]{2,1,0:T(8,128)(2,1)} %bitcast.21), calls=%async_computation.1 | async-start | bytes 1572864 | tf_op jit(solution)/shard_map/all_to_all | solution.py:293
  48.8 21.0 %all-to-all-start.2 = ((bf16[128,24,128]{2,1,0:T(8,128)(2,1)}), bf16[128,24,128]{2,1,0:T(8,128)(2,1)S(1)}, u32[]{:S(2)}, u32[]{:S(2)}) async-start(bf16[128,24,128]{2,1,0:T(8,128)(2,1)} %bitcast.22), calls=%async_computation.2 | async-start | bytes 1572864 | tf_op jit(solution)/shard_map/all_to_all | solution.py:293
  73.5 21.0 %all-to-all-start.3 = ((bf16[128,24,128]{2,1,0:T(8,128)(2,1)}), bf16[128,24,128]{2,1,0:T(8,128)(2,1)S(1)}, u32[]{:S(2)}, u32[]{:S(2)}) async-start(bf16[128,24,128]{2,1,0:T(8,128)(2,1)} %bitcast.20), calls=%async_computation.3 | async-start | bytes 1572864 | tf_op jit(solution)/shard_map/all_to_all | solution.py:293

commit v5 on v4

v5 whole, which is shorter than its diff:
```python
import functools

import jax
import jax.numpy as jnp
from jax import lax
from jax.experimental import pallas as pl
from jax.experimental.pallas import tpu as pltpu
from jax.sharding import PartitionSpec as P

AXES = ("band", "patch")
EPSILON = 1e-05
LANES = 128
BF = jnp.bfloat16
F32 = jnp.float32
I32 = jnp.int32


def dot(a, b):
    return jnp.dot(a, b, preferred_element_type=F32)


def dot_lanes(a, b):
    return lax.dot_general(a, b, (((1,), (1,)), ((), ())), preferred_element_type=F32)


def iota(shape, axis):
    return lax.broadcasted_iota(I32, shape, axis)


def flag(condition):
    return jnp.where(condition, 1.0, 0.0).astype(BF)


def column(row):
    count = row.shape[1]
    same = iota((count, count), 0) == iota((count, count), 1)
    return jnp.sum(jnp.where(same, row.astype(F32), 0.0), axis=1, keepdims=True).astype(I32)


def choose(row, count):
    return flag(iota((row.shape[1], count), 1) == column(row))


def choose_t(row, count):
    return flag(iota((count, row.shape[1]), 0) == row)


def line(ref):
    return ref[...].reshape(1, ref.shape[0])


def silu(v):
    return 0.5 * v * (1.0 + jnp.tanh(0.5 * v))


def finish(summed, second):
    out = dot(silu(summed).astype(BF), second)
    centred = out - jnp.mean(out, axis=-1, keepdims=True)
    spread = jnp.mean(centred * centred, axis=-1, keepdims=True)
    return centred * lax.rsqrt(spread + EPSILON)


def residual(base, update):
    return (base.astype(F32) + update).astype(BF)


def start(sems, first, *pairs):
    copies = [pltpu.make_async_copy(src, dst, sems.at[first + n]) for n, (src, dst) in enumerate(pairs)]
    for copy in copies:
        copy.start()
    return copies


def wait(*copies):
    for copy in copies:
        copy.wait()


def places(source, devices):
    edges = source.shape[1]
    earlier = flag(iota((edges, edges), 0) < iota((edges, edges), 1))
    hit = iota((devices, edges), 0) == source
    hits = flag(hit)
    return jnp.sum(jnp.where(hit, dot(hits, earlier), 0.0), axis=0, keepdims=True).astype(I32), hits


def fence(ref):
    def step(n, carry):
        ref[pl.ds(pl.multiple_of(n * 8, 8), 8), :] = jnp.zeros((8, ref.shape[1]), ref.dtype)
        return carry

    lax.fori_loop(0, 2, step, 0)


def serve(asked, kind, cap, table, wide, out):
    devices = asked.shape[0]
    blocks = table.shape[1] // LANES
    lanes = iota((devices, table.shape[0]), 1)
    hot = [flag(asked[:, lane : lane + 1] == lanes) for lane in range(kind * cap, kind * cap + cap)]
    got = dot(jnp.concatenate(hot, axis=0), table)
    for slot in range(cap):
        for block in range(blocks):
            target = pl.ds(slot * blocks + block, devices, stride=cap * blocks)
            wide[target, :] = got[slot * devices : (slot + 1) * devices, block * LANES : (block + 1) * LANES]
    out[...] = wide[...].astype(BF)


def take_in(cap, devices, packed, ends, wide, rows):
    blocks = rows.shape[1] // LANES
    rows[cap * devices :, :] = ends
    wide[...] = packed[...].astype(F32)
    for slot in range(cap):
        for block in range(blocks):
            source = pl.ds(slot * blocks + block, devices, stride=cap * blocks)
            target = pl.ds(slot * devices, devices)
            rows[target, block * LANES : (block + 1) * LANES] = wide[source, :].astype(BF)


def ask_kernel(
    cap, devices, dev0, dev1, dev2, row0, row1, row2, dst0, dst1, grid, mesh, w, request, lines, table, kept,
    d0, d1, d2, r0, r1, r2, e0, e1, g, w0, w1, w3, earlier, spare, sems,
):
    count = g.shape[0]
    m = kept.at[pl.ds(2 * count, count)]
    devs, rows = (d0, d1, d2), (r0, r1, r2)
    copies = start(sems, 0, *zip((dev0, dev1, dev2, row0, row1, row2), devs + rows))
    fence(spare)
    later = start(
        sems, 6, (grid, g), (w.at[0], w0), (mesh, m), (w.at[1], w1), (w.at[3], w3), (dst0, e0), (dst1, e1)
    )
    edges = lines.shape[1]
    earlier[...] = flag(iota((edges, edges), 0) < iota((edges, edges), 1))
    fence(spare)
    wait(*copies)
    hits = [iota((devices, edges), 0) == dev[...] for dev in devs]
    before = dot(flag(jnp.concatenate(hits, axis=0)), earlier[...])
    values = []
    for kind in range(3):
        mine = jnp.where(hits[kind], before[kind * devices : (kind + 1) * devices, :], 0.0)
        place = jnp.sum(mine, axis=0, keepdims=True).astype(I32)
        lines[kind : kind + 1, :] = place * devices + devs[kind][...]
        row = line(rows[kind]).astype(F32)
        values.append(jnp.where(iota((LANES, edges), 0) == place + kind * cap, row, 0.0).astype(BF))
    hits = flag(jnp.concatenate(hits, axis=1))
    request[...] = dot_lanes(hits, jnp.concatenate(values, axis=1)).astype(I32)
    wait(*later[:2])
    table[...] = dot(g[...], w0[...]).astype(BF)
    wait(*later[2:4])
    kept[:count, :] = dot(m[...], w1[...]).astype(BF)
    wait(*later[4:])
    kept[count : 2 * count, :] = dot(m[...], w3[...]).astype(BF)
    lines[3:4, :] = line(e0)
    lines[4:5, :] = line(e1)


def serve_kernel(cap, asked, table, out, wide):
    serve(asked[...], 0, cap, table[...], wide, out)


def enc_kernel(cap, received, asked, lines, kept, w, one, out, w2, w4, w5, w8, one_v, wide, packed, rows, sems):
    copies = start(sems, 0, (w.at[2], w2))
    fence(wide)
    copies += start(sems, 1, (w.at[4], w4), (w.at[5], w5), (w.at[8], w8))
    fence(wide)
    count = one_v.shape[0]
    devices = asked.shape[0]
    pick = choose(lines[0:1, :], cap * devices)
    to = choose(lines[3:4, :], count)
    to_t = choose_t(lines[3:4, :], count)
    take_in(cap, devices, received, kept[:count, :], wide, rows)
    summed = dot(jnp.concatenate([pick, to], axis=1), rows[...])
    wait(copies[0])
    message = finish(summed, w2[...]).astype(BF)
    summed = dot(to_t, message).astype(BF)
    wait(copies[1])
    summed = kept[count : 2 * count, :].astype(F32) + dot(summed, w4[...])
    wait(copies[2])
    mine = residual(kept[2 * count :, :], finish(summed, w5[...]))
    one_v[...] = mine
    wait(copies[3])
    serve(asked[...], 1, cap, dot(mine, w8[...]).astype(BF), wide, packed)
    wait(*start(sems, 4, (one_v, one), (packed, out)))


def beside_kernel(
    one, grid, loc_src, loc_dst, w, kept, w10, dec_kept, g, w9, w8, w11, w6, w7, w15, w17, s, d, sems
):
    count = one.shape[0]
    mine = kept.at[pl.ds(3 * count, count)]
    grid_one = dec_kept.at[pl.ds(2 * count, count)]
    copies = start(
        sems, 0, (one, mine), (w.at[9], w9), (loc_src, s), (loc_dst, d), (w.at[8], w8), (w.at[10], w10),
        (w.at[11], w11), (grid, g), (w.at[6], w6), (w.at[7], w7), (w.at[15], w15), (w.at[17], w17),
    )
    wait(*copies[:2])
    kept[:count, :] = dot(mine[...], w9[...]).astype(BF)
    wait(*copies[2:5])
    start_rows = dot(mine[...], w8[...]).astype(BF)
    stop = line(d)
    both = jnp.concatenate([choose(line(s), count), choose(stop, count)], axis=1)
    summed = dot(both, jnp.concatenate([start_rows, kept[:count, :]], axis=0))
    wait(copies[5])
    message = finish(summed, w10[...]).astype(BF)
    kept[2 * count : 3 * count, :] = dot(choose_t(stop, count), message).astype(BF)
    wait(copies[6])
    kept[count : 2 * count, :] = dot(mine[...], w11[...]).astype(BF)
    wait(*copies[7:10])
    grid_one[...] = residual(g[...], finish(dot(g[...], w6[...]), w7[...]))
    wait(copies[10])
    dec_kept[:count, :] = dot(grid_one[...], w15[...]).astype(BF)
    wait(copies[11])
    dec_kept[count : 2 * count, :] = dot(grid_one[...], w17[...]).astype(BF)


def proc_kernel(cap, received, asked, lines, kept, w10, w, out, w12, w13, w14, wide, rows, sems):
    copies = start(sems, 0, (w.at[12], w12), (w.at[13], w13), (w.at[14], w14))
    fence(wide)
    count = kept.shape[0] // 4
    devices = asked.shape[0]
    pick = choose(lines[1:2, :], cap * devices)
    to = choose(lines[4:5, :], count)
    to_t = choose_t(lines[4:5, :], count)
    take_in(cap, devices, received, kept[:count, :], wide, rows)
    summed = dot(jnp.concatenate([pick, to], axis=1), rows[...])
    message = finish(summed, w10[...]).astype(BF)
    summed = (kept[2 * count : 3 * count, :].astype(F32) + dot(to_t, message)).astype(BF)
    wait(copies[0])
    summed = kept[count : 2 * count, :].astype(F32) + dot(summed, w12[...])
    wait(copies[1])
    two = residual(kept[3 * count :, :], finish(summed, w13[...]))
    wait(copies[2])
    serve(asked[...], 2, cap, dot(two, w14[...]).astype(BF), wide, out)


def dec_kernel(cap, devices, received, lines, kept, w, out, w16, w18, w19, wide, rows, sems):
    copies = start(sems, 0, (w.at[16], w16))
    fence(wide)
    copies += start(sems, 1, (w.at[18], w18), (w.at[19], w19))
    fence(wide)
    edges = lines.shape[1]
    count = kept.shape[0] // 3
    pick = choose(lines[2:3, :], cap * devices)
    near = iota((edges, count), 0) - 3 * iota((edges, count), 1)
    to = flag((near >= 0) & (near < 3))
    near = iota((count, edges), 1) - 3 * iota((count, edges), 0)
    to_t = flag((near >= 0) & (near < 3))
    take_in(cap, devices, received, kept[:count, :], wide, rows)
    summed = dot(jnp.concatenate([pick, to], axis=1), rows[...])
    wait(copies[0])
    message = finish(summed, w16[...]).astype(BF)
    summed = dot(to_t, message).astype(BF)
    wait(copies[1])
    summed = kept[count : 2 * count, :].astype(F32) + dot(summed, w18[...])
    wait(copies[2])
    out[...] = residual(kept[2 * count :, :], finish(summed, w19[...]))


def run(kernel, outs=(), near=(), far=(), held=(), copies=0, macs=0, away=(), last=False):
    inside = pl.BlockSpec(memory_space=pltpu.VMEM)
    outside = pl.BlockSpec(memory_space=pltpu.HBM)
    moved = sum(a.size * a.dtype.itemsize for a in list(held) + list(outs))
    return pl.pallas_call(
        kernel,
        out_shape=(
            *(a if last else pltpu.VMEM(a.shape, a.dtype) for a in outs),
            *(pltpu.HBM(a.shape, a.dtype) for a in away),
        ),
        in_specs=[inside] * len(near) + [outside] * len(far),
        out_specs=(inside,) * len(outs) + (outside,) * len(away),
        scratch_shapes=[pltpu.VMEM(a.shape, a.dtype) for a in held]
        + ([pltpu.SemaphoreType.DMA((copies,))] if copies else []),
        compiler_params=pltpu.CompilerParams(vmem_limit_bytes=16 * 2**20),
        cost_estimate=pl.CostEstimate(flops=2 * macs, bytes_accessed=moved, transcendentals=0),
    )(
        *(pltpu.with_memory_space_constraint(a, pltpu.VMEM) for a in near),
        *(pltpu.with_memory_space_constraint(a, pltpu.HBM) for a in far),
    )


def exchange(rows, devices):
    parts = rows.reshape(devices, rows.shape[0] // devices, LANES)
    moved = lax.all_to_all(parts, AXES, split_axis=0, concat_axis=0, tiled=True)
    return moved.reshape(rows.shape)


def body(
    grid_latent,
    mesh_latent,
    weights,
    enc_dev,
    enc_row,
    enc_dst,
    proc_dev,
    proc_row,
    proc_dst,
    loc_src,
    loc_dst,
    dec_dev,
    dec_row,
):
    devices = lax.axis_size("band") * lax.axis_size("patch")
    edges = enc_dev.shape[0]
    cap = max(2, 2 * edges // devices)
    count, width = mesh_latent.shape
    total = devices * cap

    def arr(shape, dtype):
        return jax.ShapeDtypeStruct(shape, dtype)

    across = arr((1, edges), I32)
    row = arr((edges,), I32)
    loc = arr(loc_src.shape, I32)
    mat = arr((width, width), BF)
    square = arr((edges, edges), BF)
    spare = arr((16, LANES), F32)
    nodes = arr((count, width), BF)
    lines = arr((8, edges), I32)
    ask = arr((devices, LANES), I32)
    flat = arr((total * width // LANES, LANES), BF)
    flat32 = arr(flat.shape, F32)
    rows = arr((total + count, width), BF)
    edge_macs = edges * width * (total + 3 * width)
    devs = tuple(a.reshape(1, edges) for a in (enc_dev, proc_dev, dec_dev))

    def kept(parts):
        return arr((parts * count, width), BF)

    request, places_of, table, enc_kept = run(
        functools.partial(ask_kernel, cap, devices),
        (ask, lines, nodes, kept(3)),
        far=(*devs, enc_row, proc_row, dec_row, enc_dst, proc_dst, grid_latent, mesh_latent, weights),
        held=(across,) * 3 + (row,) * 5 + (nodes, mat, mat, mat, square, spare),
        copies=13,
        macs=3 * devices * edges * (edges + LANES) + 3 * count * width * width,
    )
    asked = request.reshape(devices, 1, LANES)
    wanted = lax.all_to_all(asked, AXES, split_axis=0, concat_axis=0, tiled=True).reshape(devices, LANES)
    (sent,) = run(
        functools.partial(serve_kernel, cap),
        (flat,),
        near=(wanted, table),
        held=(flat32,),
        macs=total * count * width,
    )
    enc_rows = exchange(sent, devices)
    mesh_one, sent = run(
        functools.partial(enc_kernel, cap),
        near=(enc_rows, wanted, places_of, enc_kept),
        far=(weights,),
        held=(mat, mat, mat, mat, nodes, flat32, flat, rows),
        copies=6,
        macs=edge_macs,
        away=(nodes, flat),
    )
    proc_rows = exchange(sent, devices)
    proc_kept, w10, dec_kept = run(
        beside_kernel,
        (kept(4), mat, kept(3)),
        far=(mesh_one, grid_latent, loc_src, loc_dst, weights),
        held=(nodes,) + (mat,) * 7 + (loc, loc),
        copies=12,
        macs=11 * count * width * width,
    )
    (sent,) = run(
        functools.partial(proc_kernel, cap),
        (flat,),
        near=(proc_rows, wanted, places_of, proc_kept, w10),
        far=(weights,),
        held=(mat, mat, mat, flat32, rows),
        copies=3,
        macs=edge_macs,
    )
    dec_rows = exchange(sent, devices)
    (decoded,) = run(
        functools.partial(dec_kernel, cap, devices),
        (nodes,),
        near=(dec_rows, places_of, dec_kept),
        far=(weights,),
        held=(mat, mat, mat, flat32, rows),
        copies=3,
        macs=edge_macs,
        last=True,
    )
    return decoded


def solution(mesh):
    rows = P(AXES, None)
    edge = P(AXES)
    in_specs = (rows, rows, P(), rows, edge, edge, rows, edge, edge, edge, edge, rows, edge)
    return jax.shard_map(body, mesh=mesh, in_specs=in_specs, out_specs=rows, check_vma=False)
```

time: 97.9 us -> 96.4 us (0.985)
  blocking collectives: 20.9 us -> 62.2 us
  waiting for transfers between devices: 42.5 us -> 12.8 us
  starting transfers between devices: 13 us -> 4.25 us
  Pallas kernels: 21 us -> 16.8 us
    all_to_all x0 -> x2, blocking collectives: none -> 41.3 us  [exchange(): moved = lax.all_to_all(parts, AXES, split_axis=0, concat_axis=0, tiled=True)]
    all_to_all x3 -> x1, waiting for transfers between devices: 42.5 us -> 12.8 us  [exchange(): moved = lax.all_to_all(parts, AXES, split_axis=0, concat_axis=0, tiled=True)]
    all_to_all x3 -> x1, starting transfers between devices: 13 us -> 4.25 us  [exchange(): moved = lax.all_to_all(parts, AXES, split_axis=0, concat_axis=0, tiled=True)]
    pallas_call x8 -> x6, Pallas kernels: 21 us -> 16.8 us  [run(): pl.pallas_call(kernel, out_shape=(*(a if last else pltpu.VMEM(a.shape, a....]
  transfers between devices with their start and end apart: 3 -> 1, of which waited for: 3 -> 1; matrix products, arithmetic and copies ran while one was open for 0% -> 0% of each run, Pallas kernels for 8% -> 4%
where the time goes in v5:
time: 96.4 us; the launch traced here: 96.1 us
  blocking collectives  62.2 us (65%)
  Pallas kernels  16.8 us (17%)
  waiting for transfers between devices  12.8 us (13%)
  starting transfers between devices  4.25 us (4%)
    all_to_all x2, blocking collectives, exchange(): moved = lax.all_to_all(parts, AXES, split_axis=0, concat_axis=0, tiled=True)  41.3 us
    all_to_all x1, blocking collectives, body(): lax.all_to_all(asked, AXES, split_axis=0, concat_axis=0, tiled=True)  20.9 us
    pallas_call x6, Pallas kernels, run(): pl.pallas_call(kernel, out_shape=(*(a if last else pltpu.VMEM(a.shape, a....  16.8 us
    all_to_all x1, waiting for transfers between devices, exchange(): moved = lax.all_to_all(parts, AXES, split_axis=0, concat_axis=0, tiled=True)  12.8 us
    all_to_all x1, starting transfers between devices, exchange(): moved = lax.all_to_all(parts, AXES, split_axis=0, concat_axis=0, tiled=True)  4.25 us
  transfers between devices with their start and end apart: 1, of which 1 were waited for; matrix products, arithmetic and copies ran while one was open for 0% of the time, Pallas kernels for 4%

profile of v5, /device:TPU:1, one launch (start us, length us, event | category | flops | bytes accessed | tf_op | source)
XLA Modules:
  0.0 96.1 jit_solution(7036552564969474992)
XLA Ops:
  0.0 2.2 %shard_map.127 = (s32[128,128]{1,0:T(8,128)S(1)}, s32[8,384]{1,0:T(8,128)S(1)}, bf16[128,512]{1,0:T(8,128)(2,1)S(1)}, bf16[384,512]{1,0:T(8,128)(2,1)S(1)}) custom-call(s32[1,384]{1,0:T(1,128)} %bitcast.23, s32[1,384]{1,0:T(1,128)} %bitcast.24, s32[1,384]{1,0:T(1,128)} %bitcast.25, s32[384]{0:T(512)} %row0.1, s32[384]{0:T(512)} %row1.1, s32[384]{0:T(512)} %row2.1, ...), custom_call_target="tpu_custom_call" | custom-call | flops 352321536 | bytes 2621440 | tf_op jit(solution)/shard_map/pallas_call | solution.py:262
  2.2 20.9 %all_to_all.20 = s32[128,1,128]{2,1,0:T(1,128)S(1)} all-to-all(s32[128,1,128]{2,1,0:T(1,128)S(1)} %bitcast.21), channel_id=1, replica_groups=mesh['band'=8,'patch'=16] {'band','patch'}, dimensions={0} | all-to-all | bytes 131072 | tf_op jit(solution)/shard_map/all_to_all | solution.py:337
  23.1 0.6 shard_map.128
  23.7 20.9 %all_to_all.21 = bf16[128,24,128]{2,1,0:T(8,128)(2,1)S(1)} all-to-all(bf16[128,24,128]{2,1,0:T(8,128)(2,1)S(1)} %bitcast.15), channel_id=1, replica_groups=mesh['band'=8,'patch'=16] {'band','patch'}, dimensions={0} | all-to-all | bytes 1572864 | tf_op jit(solution)/shard_map/all_to_all | solution.py:282
  44.6 4.1 %shard_map.129 = (bf16[128,512]{1,0:T(8,128)(2,1)}, bf16[3072,128]{1,0:T(8,128)(2,1)}) custom-call(bf16[3072,128]{1,0:T(8,128)(2,1)S(1)} %bitcast.13, s32[128,128]{1,0:T(8,128)S(1)} %bitcast.19, s32[8,384]{1,0:T(8,128)S(1)} %get-tuple-element.16.lines, bf16[384,512]{1,0:T(8,128)(2,1)S(1)} %get-tuple-element.17.kept, bf16[20,512,512]{2,1,0:T(8,128)(2,1)} %w.9), custom_call_target="tpu_custom_call" | custom-call | flops 905969664 | bytes 5505024 | tf_op jit(solution)/shard_map/pallas_call | solution.py:262
  48.6 4.2 %all-to-all-start.2 = ((bf16[128,24,128]{2,1,0:T(8,128)(2,1)}), bf16[128,24,128]{2,1,0:T(8,128)(2,1)S(1)}, u32[]{:S(2)}, u32[]{:S(2)}) async-start(bf16[128,24,128]{2,1,0:T(8,128)(2,1)} %bitcast.22), calls=%async_computation.2 | async-start | bytes 1572864 | tf_op jit(solution)/shard_map/all_to_all | solution.py:282
  52.9 3.9 %shard_map.130 = (bf16[512,512]{1,0:T(8,128)(2,1)S(1)}, bf16[512,512]{1,0:T(8,128)(2,1)S(1)}, bf16[384,512]{1,0:T(8,128)(2,1)S(1)}) custom-call(bf16[128,512]{1,0:T(8,128)(2,1)} %get-tuple-element.19.one, bf16[128,512]{1,0:T(8,128)(2,1)} %grid.3, s32[256]{0:T(256)} %loc_src.1, s32[256]{0:T(256)} %loc_dst.1, bf16[20,512,512]{2,1,0:T(8,128)(2,1)} %w.9), custom_call_target="tpu_custom_call" | custom-call | flops 738197504 | bytes 5244928 | tf_op jit(solution)/shard_map/pallas_call | solution.py:262
  56.8 12.8 %all-to-all-done.2 = bf16[128,24,128]{2,1,0:T(8,128)(2,1)S(1)} async-done(((bf16[128,24,128]{2,1,0:T(8,128)(2,1)}), bf16[128,24,128]{2,1,0:T(8,128)(2,1)S(1)}, u32[]{:S(2)}, u32[]{:S(2)}) %all-to-all-start.2) | async-done | bytes 786464 | tf_op jit(solution)/shard_map/all_to_all | solution.py:282
  69.6 2.9 %shard_map.131 = bf16[3072,128]{1,0:T(8,128)(2,1)S(1)} custom-call(bf16[3072,128]{1,0:T(8,128)(2,1)S(1)} %bitcast.16, s32[128,128]{1,0:T(8,128)S(1)} %bitcast.20, s32[8,384]{1,0:T(8,128)S(1)} %get-tuple-element.16.lines, bf16[512,512]{1,0:T(8,128)(2,1)S(1)} %get-tuple-element.20.kept, bf16[512,512]{1,0:T(8,128)(2,1)S(1)} %get-tuple-element.21.w10, ...), custom_call_target="tpu_custom_call" | custom-call | flops 905969664 | bytes 4849664 | tf_op jit(solution)/shard_map/pallas_call | solution.py:262
  72.5 20.5 %all_to_all.22 = bf16[128,24,128]{2,1,0:T(8,128)(2,1)S(1)} all-to-all(bf16[128,24,128]{2,1,0:T(8,128)(2,1)S(1)} %bitcast.17), channel_id=1, replica_groups=mesh['band'=8,'patch'=16] {'band','patch'}, dimensions={0} | all-to-all | bytes 1572864 | tf_op jit(solution)/shard_map/all_to_all | solution.py:282
  93.0 3.1 %shard_map.132 = bf16[128,512]{1,0:T(8,128)(2,1)} custom-call(bf16[3072,128]{1,0:T(8,128)(2,1)S(1)} %bitcast.14, s32[8,384]{1,0:T(8,128)S(1)} %get-tuple-element.16.lines, bf16[384,512]{1,0:T(8,128)(2,1)S(1)} %get-tuple-element.22.kept, bf16[20,512,512]{2,1,0:T(8,128)(2,1)} %w.9), custom_call_target="tpu_custom_call" | custom-call | flops 905969664 | bytes 4194304 | tf_op jit(solution)/shard_map/pallas_call | solution.py:262
Async XLA Ops:
  48.6 21.0 %all-to-all-start.2 = ((bf16[128,24,128]{2,1,0:T(8,128)(2,1)}), bf16[128,24,128]{2,1,0:T(8,128)(2,1)S(1)}, u32[]{:S(2)}, u32[]{:S(2)}) async-start(bf16[128,24,128]{2,1,0:T(8,128)(2,1)} %bitcast.22), calls=%async_computation.2 | async-start | bytes 1572864 | tf_op jit(solution)/shard_map/all_to_all | solution.py:282

commit v6 on v5

--- a/solution.py
+++ b/solution.py
@@ -117,23 +117,23 @@
 
 
 def ask_kernel(
-    cap, devices, dev0, dev1, dev2, row0, row1, row2, dst0, dst1, grid, mesh, w, request, lines, table, kept,
-    d0, d1, d2, r0, r1, r2, e0, e1, g, w0, w1, w3, earlier, spare, sems,
+    cap, devices, dev0, dev1, dev2, row0, row1, row2, dst0, dst1, grid, mesh, w, request, lines, table, kept, w2,
+    d0, d1, d2, r0, r1, r2, e0, e1, g, w01, earlier, spare, sems,
 ):
     count = g.shape[0]
-    m = kept.at[pl.ds(2 * count, count)]
+    edges = lines.shape[1]
+    m = kept.at[pl.ds(count, count)]
     devs, rows = (d0, d1, d2), (r0, r1, r2)
     copies = start(sems, 0, *zip((dev0, dev1, dev2, row0, row1, row2), devs + rows))
     fence(spare)
-    later = start(
-        sems, 6, (grid, g), (w.at[0], w0), (mesh, m), (w.at[1], w1), (w.at[3], w3), (dst0, e0), (dst1, e1)
-    )
-    edges = lines.shape[1]
+    later = start(sems, 6, (grid, g), (mesh, m), (w.at[pl.ds(0, 2)], w01))
     earlier[...] = flag(iota((edges, edges), 0) < iota((edges, edges), 1))
     fence(spare)
-    wait(*copies)
+    wait(*copies[:3])
     hits = [iota((devices, edges), 0) == dev[...] for dev in devs]
     before = dot(flag(jnp.concatenate(hits, axis=0)), earlier[...])
+    last = start(sems, 9, (dst0, e0), (dst1, e1), (w.at[2], w2))
+    wait(*copies[3:], *later)
     values = []
     for kind in range(3):
         mine = jnp.where(hits[kind], before[kind * devices : (kind + 1) * devices, :], 0.0)
@@ -143,12 +143,9 @@
         values.append(jnp.where(iota((LANES, edges), 0) == place + kind * cap, row, 0.0).astype(BF))
     hits = flag(jnp.concatenate(hits, axis=1))
     request[...] = dot_lanes(hits, jnp.concatenate(values, axis=1)).astype(I32)
-    wait(*later[:2])
-    table[...] = dot(g[...], w0[...]).astype(BF)
-    wait(*later[2:4])
-    kept[:count, :] = dot(m[...], w1[...]).astype(BF)
-    wait(*later[4:])
-    kept[count : 2 * count, :] = dot(m[...], w3[...]).astype(BF)
+    table[...] = dot(g[...], w01[0]).astype(BF)
+    kept[:count, :] = dot(m[...], w01[1]).astype(BF)
+    wait(*last)
     lines[3:4, :] = line(e0)
     lines[4:5, :] = line(e1)
 
@@ -157,10 +154,8 @@
     serve(asked[...], 0, cap, table[...], wide, out)
 
 
-def enc_kernel(cap, received, asked, lines, kept, w, one, out, w2, w4, w5, w8, one_v, wide, packed, rows, sems):
-    copies = start(sems, 0, (w.at[2], w2))
-    fence(wide)
-    copies += start(sems, 1, (w.at[4], w4), (w.at[5], w5), (w.at[8], w8))
+def enc_kernel(cap, received, asked, lines, kept, w2, w, one, out, w345, w8, one_v, wide, packed, rows, sems):
+    copies = start(sems, 0, (w.at[pl.ds(3, 3)], w345), (w.at[8], w8))
     fence(wide)
     count = one_v.shape[0]
     devices = asked.shape[0]
@@ -169,17 +164,15 @@
     to_t = choose_t(lines[3:4, :], count)
     take_in(cap, devices, received, kept[:count, :], wide, rows)
     summed = dot(jnp.concatenate([pick, to], axis=1), rows[...])
-    wait(copies[0])
     message = finish(summed, w2[...]).astype(BF)
     summed = dot(to_t, message).astype(BF)
-    wait(copies[1])
-    summed = kept[count : 2 * count, :].astype(F32) + dot(summed, w4[...])
-    wait(copies[2])
-    mine = residual(kept[2 * count :, :], finish(summed, w5[...]))
+    wait(*copies)
+    m = kept[count:, :]
+    summed = dot(jnp.concatenate([m, summed], axis=1), w345[:2].reshape(2 * m.shape[1], m.shape[1]))
+    mine = residual(m, finish(summed, w345[2]))
     one_v[...] = mine
-    wait(copies[3])
     serve(asked[...], 1, cap, dot(mine, w8[...]).astype(BF), wide, packed)
-    wait(*start(sems, 4, (one_v, one), (packed, out)))
+    wait(*start(sems, 2, (one_v, one), (packed, out)))
 
 
 def beside_kernel(
@@ -212,8 +205,8 @@
     dec_kept[count : 2 * count, :] = dot(grid_one[...], w17[...]).astype(BF)
 
 
-def proc_kernel(cap, received, asked, lines, kept, w10, w, out, w12, w13, w14, wide, rows, sems):
-    copies = start(sems, 0, (w.at[12], w12), (w.at[13], w13), (w.at[14], w14))
+def proc_kernel(cap, received, asked, lines, kept, w10, w, out, ws, wide, rows, sems):
+    copies = start(sems, 0, (w.at[pl.ds(12, 3)], ws))
     fence(wide)
     count = kept.shape[0] // 4
     devices = asked.shape[0]
@@ -224,18 +217,16 @@
     summed = dot(jnp.concatenate([pick, to], axis=1), rows[...])
     message = finish(summed, w10[...]).astype(BF)
     summed = (kept[2 * count : 3 * count, :].astype(F32) + dot(to_t, message)).astype(BF)
-    wait(copies[0])
-    summed = kept[count : 2 * count, :].astype(F32) + dot(summed, w12[...])
-    wait(copies[1])
-    two = residual(kept[3 * count :, :], finish(summed, w13[...]))
-    wait(copies[2])
-    serve(asked[...], 2, cap, dot(two, w14[...]).astype(BF), wide, out)
-
-
-def dec_kernel(cap, devices, received, lines, kept, w, out, w16, w18, w19, wide, rows, sems):
+    wait(*copies)
+    summed = kept[count : 2 * count, :].astype(F32) + dot(summed, ws[0])
+    two = residual(kept[3 * count :, :], finish(summed, ws[1]))
+    serve(asked[...], 2, cap, dot(two, ws[2]).astype(BF), wide, out)
+
+
+def dec_kernel(cap, devices, received, lines, kept, w, out, w16, ws, wide, rows, sems):
     copies = start(sems, 0, (w.at[16], w16))
     fence(wide)
-    copies += start(sems, 1, (w.at[18], w18), (w.at[19], w19))
+    copies += start(sems, 1, (w.at[pl.ds(18, 2)], ws))
     fence(wide)
     edges = lines.shape[1]
     count = kept.shape[0] // 3
@@ -250,9 +241,8 @@
     message = finish(summed, w16[...]).astype(BF)
     summed = dot(to_t, message).astype(BF)
     wait(copies[1])
-    summed = kept[count : 2 * count, :].astype(F32) + dot(summed, w18[...])
-    wait(copies[2])
-    out[...] = residual(kept[2 * count :, :], finish(summed, w19[...]))
+    summed = kept[count : 2 * count, :].astype(F32) + dot(summed, ws[0])
+    out[...] = residual(kept[2 * count :, :], finish(summed, ws[1]))
 
 
 def run(kernel, outs=(), near=(), far=(), held=(), copies=0, macs=0, away=(), last=False):
@@ -322,15 +312,18 @@
     edge_macs = edges * width * (total + 3 * width)
     devs = tuple(a.reshape(1, edges) for a in (enc_dev, proc_dev, dec_dev))
 
+    def mats(number):
+        return arr((number, width, width), BF)
+
     def kept(parts):
         return arr((parts * count, width), BF)
 
-    request, places_of, table, enc_kept = run(
+    request, places_of, table, enc_kept, w2 = run(
         functools.partial(ask_kernel, cap, devices),
-        (ask, lines, nodes, kept(3)),
+        (ask, lines, nodes, kept(2), mat),
         far=(*devs, enc_row, proc_row, dec_row, enc_dst, proc_dst, grid_latent, mesh_latent, weights),
-        held=(across,) * 3 + (row,) * 5 + (nodes, mat, mat, mat, square, spare),
-        copies=13,
+        held=(across,) * 3 + (row,) * 5 + (nodes, mats(2), square, spare),
+        copies=12,
         macs=3 * devices * edges * (edges + LANES) + 3 * count * width * width,
     )
     asked = request.reshape(devices, 1, LANES)
@@ -345,10 +338,10 @@
     enc_rows = exchange(sent, devices)
     mesh_one, sent = run(
         functools.partial(enc_kernel, cap),
-        near=(enc_rows, wanted, places_of, enc_kept),
+        near=(enc_rows, wanted, places_of, enc_kept, w2),
         far=(weights,),
-        held=(mat, mat, mat, mat, nodes, flat32, flat, rows),
-        copies=6,
+        held=(mats(3), mat, nodes, flat32, flat, rows),
+        copies=4,
         macs=edge_macs,
         away=(nodes, flat),
     )
@@ -366,8 +359,8 @@
         (flat,),
         near=(proc_rows, wanted, places_of, proc_kept, w10),
         far=(weights,),
-        held=(mat, mat, mat, flat32, rows),
-        copies=3,
+        held=(mats(3), flat32, rows),
+        copies=1,
         macs=edge_macs,
     )
     dec_rows = exchange(sent, devices)
@@ -376,8 +369,8 @@
         (nodes,),
         near=(dec_rows, places_of, dec_kept),
         far=(weights,),
-        held=(mat, mat, mat, flat32, rows),
-        copies=3,
+        held=(mat, mats(2), flat32, rows),
+        copies=2,
         macs=edge_macs,
         last=True,
     )

time: 96.4 us -> 95.7 us (level)
  no operation moved by 1% of the time
where the time goes in v6:
time: 95.7 us; the launch traced here: 95.4 us
  blocking collectives  62.2 us (65%)
  Pallas kernels  16.1 us (17%)
  waiting for transfers between devices  12.8 us (13%)
  starting transfers between devices  4.25 us (4%)
    all_to_all x2, blocking collectives, exchange(): moved = lax.all_to_all(parts, AXES, split_axis=0, concat_axis=0, tiled=True)  41.3 us
    all_to_all x1, blocking collectives, body(): lax.all_to_all(asked, AXES, split_axis=0, concat_axis=0, tiled=True)  20.9 us
    pallas_call x6, Pallas kernels, run(): pl.pallas_call(kernel, out_shape=(*(a if last else pltpu.VMEM(a.shape, a....  16.1 us
    all_to_all x1, waiting for transfers between devices, exchange(): moved = lax.all_to_all(parts, AXES, split_axis=0, concat_axis=0, tiled=True)  12.8 us
    all_to_all x1, starting transfers between devices, exchange(): moved = lax.all_to_all(parts, AXES, split_axis=0, concat_axis=0, tiled=True)  4.25 us
  transfers between devices with their start and end apart: 1, of which 1 were waited for; matrix products, arithmetic and copies ran while one was open for 0% of the time, Pallas kernels for 4%

profile of v6, /device:TPU:1, one launch (start us, length us, event | category | flops | bytes accessed | tf_op | source)
XLA Modules:
  0.0 95.4 jit_solution(7701881593013058975)
XLA Ops:
  0.0 2.0 %shard_map.127 = (s32[128,128]{1,0:T(8,128)S(1)}, s32[8,384]{1,0:T(8,128)S(1)}, bf16[128,512]{1,0:T(8,128)(2,1)S(1)}, bf16[256,512]{1,0:T(8,128)(2,1)S(1)}, bf16[512,512]{1,0:T(8,128)(2,1)S(1)}) custom-call(s32[1,384]{1,0:T(1,128)} %bitcast.23, s32[1,384]{1,0:T(1,128)} %bitcast.24, s32[1,384]{1,0:T(1,128)} %bitcast.25, s32[384]{0:T(512)} %row0.1, s32[384]{0:T(512)} %row1.1, ...), custom_call_target="tpu_custom_call" | custom-call | flops 352321536 | bytes 2490368 | tf_op jit(solution)/shard_map/pallas_call | solution.py:252
  2.0 20.9 %all_to_all.20 = s32[128,1,128]{2,1,0:T(1,128)S(1)} all-to-all(s32[128,1,128]{2,1,0:T(1,128)S(1)} %bitcast.21), channel_id=1, replica_groups=mesh['band'=8,'patch'=16] {'band','patch'}, dimensions={0} | all-to-all | bytes 131072 | tf_op jit(solution)/shard_map/all_to_all | solution.py:330
  22.9 0.6 shard_map.128
  23.5 20.9 %all_to_all.21 = bf16[128,24,128]{2,1,0:T(8,128)(2,1)S(1)} all-to-all(bf16[128,24,128]{2,1,0:T(8,128)(2,1)S(1)} %bitcast.15), channel_id=1, replica_groups=mesh['band'=8,'patch'=16] {'band','patch'}, dimensions={0} | all-to-all | bytes 1572864 | tf_op jit(solution)/shard_map/all_to_all | solution.py:272
  44.3 3.8 %shard_map.129 = (bf16[128,512]{1,0:T(8,128)(2,1)}, bf16[3072,128]{1,0:T(8,128)(2,1)}) custom-call(bf16[3072,128]{1,0:T(8,128)(2,1)S(1)} %bitcast.13, s32[128,128]{1,0:T(8,128)S(1)} %bitcast.19, s32[8,384]{1,0:T(8,128)S(1)} %get-tuple-element.17.lines, bf16[256,512]{1,0:T(8,128)(2,1)S(1)} %get-tuple-element.18.kept, ...), custom_call_target="tpu_custom_call" | custom-call | flops 905969664 | bytes 5505024 | tf_op jit(solution)/shard_map/pallas_call | solution.py:252
  48.1 4.3 %all-to-all-start.2 = ((bf16[128,24,128]{2,1,0:T(8,128)(2,1)}), bf16[128,24,128]{2,1,0:T(8,128)(2,1)S(1)}, u32[]{:S(2)}, u32[]{:S(2)}) async-start(bf16[128,24,128]{2,1,0:T(8,128)(2,1)} %bitcast.22), calls=%async_computation.2 | async-start | bytes 1572864 | tf_op jit(solution)/shard_map/all_to_all | solution.py:272
  52.4 3.9 %shard_map.130 = (bf16[512,512]{1,0:T(8,128)(2,1)S(1)}, bf16[512,512]{1,0:T(8,128)(2,1)S(1)}, bf16[384,512]{1,0:T(8,128)(2,1)S(1)}) custom-call(bf16[128,512]{1,0:T(8,128)(2,1)} %get-tuple-element.21.one, bf16[128,512]{1,0:T(8,128)(2,1)} %grid.3, s32[256]{0:T(256)} %loc_src.1, s32[256]{0:T(256)} %loc_dst.1, bf16[20,512,512]{2,1,0:T(8,128)(2,1)} %w.9), custom_call_target="tpu_custom_call" | custom-call | flops 738197504 | bytes 5244928 | tf_op jit(solution)/shard_map/pallas_call | solution.py:252
  56.3 12.8 %all-to-all-done.2 = bf16[128,24,128]{2,1,0:T(8,128)(2,1)S(1)} async-done(((bf16[128,24,128]{2,1,0:T(8,128)(2,1)}), bf16[128,24,128]{2,1,0:T(8,128)(2,1)S(1)}, u32[]{:S(2)}, u32[]{:S(2)}) %all-to-all-start.2) | async-done | bytes 786464 | tf_op jit(solution)/shard_map/all_to_all | solution.py:272
  69.1 2.8 %shard_map.131 = bf16[3072,128]{1,0:T(8,128)(2,1)S(1)} custom-call(bf16[3072,128]{1,0:T(8,128)(2,1)S(1)} %bitcast.16, s32[128,128]{1,0:T(8,128)S(1)} %bitcast.20, s32[8,384]{1,0:T(8,128)S(1)} %get-tuple-element.17.lines, bf16[512,512]{1,0:T(8,128)(2,1)S(1)} %get-tuple-element.22.kept, bf16[512,512]{1,0:T(8,128)(2,1)S(1)} %get-tuple-element.23.w10, ...), custom_call_target="tpu_custom_call" | custom-call | flops 905969664 | bytes 4849664 | tf_op jit(solution)/shard_map/pallas_call | solution.py:252
  71.9 20.5 %all_to_all.22 = bf16[128,24,128]{2,1,0:T(8,128)(2,1)S(1)} all-to-all(bf16[128,24,128]{2,1,0:T(8,128)(2,1)S(1)} %bitcast.17), channel_id=1, replica_groups=mesh['band'=8,'patch'=16] {'band','patch'}, dimensions={0} | all-to-all | bytes 1572864 | tf_op jit(solution)/shard_map/all_to_all | solution.py:272
  92.4 3.0 %shard_map.132 = bf16[128,512]{1,0:T(8,128)(2,1)} custom-call(bf16[3072,128]{1,0:T(8,128)(2,1)S(1)} %bitcast.14, s32[8,384]{1,0:T(8,128)S(1)} %get-tuple-element.17.lines, bf16[384,512]{1,0:T(8,128)(2,1)S(1)} %get-tuple-element.24.kept, bf16[20,512,512]{2,1,0:T(8,128)(2,1)} %w.9), custom_call_target="tpu_custom_call" | custom-call | flops 905969664 | bytes 4194304 | tf_op jit(solution)/shard_map/pallas_call | solution.py:252
Async XLA Ops:
  48.1 21.0 %all-to-all-start.2 = ((bf16[128,24,128]{2,1,0:T(8,128)(2,1)}), bf16[128,24,128]{2,1,0:T(8,128)(2,1)S(1)}, u32[]{:S(2)}, u32[]{:S(2)}) async-start(bf16[128,24,128]{2,1,0:T(8,128)(2,1)} %bitcast.22), calls=%async_computation.2 | async-start | bytes 1572864 | tf_op jit(solution)/shard_map/all_to_all | solution.py:272

commit v7 on v6

--- a/solution.py
+++ b/solution.py
@@ -53,11 +53,16 @@
     return 0.5 * v * (1.0 + jnp.tanh(0.5 * v))
 
 
-def finish(summed, second):
+def centred(matrix):
+    wide = matrix.astype(F32)
+    return (wide - jnp.mean(wide, axis=-1, keepdims=True)).astype(BF)
+
+
+def finish(summed, second, zero_mean=False):
     out = dot(silu(summed).astype(BF), second)
-    centred = out - jnp.mean(out, axis=-1, keepdims=True)
-    spread = jnp.mean(centred * centred, axis=-1, keepdims=True)
-    return centred * lax.rsqrt(spread + EPSILON)
+    if not zero_mean:
+        out = out - jnp.mean(out, axis=-1, keepdims=True)
+    return out * lax.rsqrt(jnp.mean(out * out, axis=-1, keepdims=True) + EPSILON)
 
 
 def residual(base, update):
@@ -117,23 +122,17 @@
 
 
 def ask_kernel(
-    cap, devices, dev0, dev1, dev2, row0, row1, row2, dst0, dst1, grid, mesh, w, request, lines, table, kept, w2,
-    d0, d1, d2, r0, r1, r2, e0, e1, g, w01, earlier, spare, sems,
-):
-    count = g.shape[0]
+    cap, devices, dev0, dev1, dev2, row0, row1, row2, lines, request,
+    d0, d1, d2, r0, r1, r2, asking, earlier, spare, sems,
+):
     edges = lines.shape[1]
-    m = kept.at[pl.ds(count, count)]
     devs, rows = (d0, d1, d2), (r0, r1, r2)
     copies = start(sems, 0, *zip((dev0, dev1, dev2, row0, row1, row2), devs + rows))
-    fence(spare)
-    later = start(sems, 6, (grid, g), (mesh, m), (w.at[pl.ds(0, 2)], w01))
     earlier[...] = flag(iota((edges, edges), 0) < iota((edges, edges), 1))
     fence(spare)
-    wait(*copies[:3])
+    wait(*copies)
     hits = [iota((devices, edges), 0) == dev[...] for dev in devs]
     before = dot(flag(jnp.concatenate(hits, axis=0)), earlier[...])
-    last = start(sems, 9, (dst0, e0), (dst1, e1), (w.at[2], w2))
-    wait(*copies[3:], *later)
     values = []
     for kind in range(3):
         mine = jnp.where(hits[kind], before[kind * devices : (kind + 1) * devices, :], 0.0)
@@ -142,105 +141,117 @@
         row = line(rows[kind]).astype(F32)
         values.append(jnp.where(iota((LANES, edges), 0) == place + kind * cap, row, 0.0).astype(BF))
     hits = flag(jnp.concatenate(hits, axis=1))
-    request[...] = dot_lanes(hits, jnp.concatenate(values, axis=1)).astype(I32)
+    asking[...] = dot_lanes(hits, jnp.concatenate(values, axis=1)).astype(I32)
+    wait(*start(sems, 6, (asking, request)))
+
+
+def prepare_kernel(
+    grid, mesh, dst0, dst1, src2, dst2, w, table, kept, w2, w10, ends, w16, dec_kept,
+    g, e0, e1, e2, e3, w01, w67, w16_v, w15, w17, dec_kept_v, sems,
+):
+    count = g.shape[0]
+    m = kept.at[pl.ds(count, count)]
+    one = dec_kept_v.at[pl.ds(2 * count, count)]
+    copies = start(
+        sems, 0, (grid, g), (w.at[pl.ds(0, 2)], w01), (mesh, m), (w.at[16], w16_v), (w.at[pl.ds(6, 2)], w67),
+        (w.at[15], w15), (w.at[17], w17), (w.at[2], w2), (w.at[10], w10), (dst0, e0), (dst1, e1), (src2, e2), (dst2, e3),
+    )
+    wait(*copies[:3])
     table[...] = dot(g[...], w01[0]).astype(BF)
     kept[:count, :] = dot(m[...], w01[1]).astype(BF)
-    wait(*last)
-    lines[3:4, :] = line(e0)
-    lines[4:5, :] = line(e1)
+    wait(copies[3])
+    w16_v[...] = centred(w16_v[...])
+    out = start(sems, len(copies), (w16_v, w16))
+    wait(*copies[4:7])
+    one[...] = residual(g[...], finish(dot(g[...], w67[0]), w67[1]))
+    dec_kept_v[:count, :] = dot(one[...], w15[...]).astype(BF)
+    dec_kept_v[count : 2 * count, :] = dot(one[...], w17[...]).astype(BF)
+    out += start(sems, len(copies) + 1, (dec_kept_v, dec_kept))
+    wait(*copies[7:])
+    w2[...] = centred(w2[...])
+    w10[...] = centred(w10[...])
+    for n, row in enumerate((e0, e1, e2, e3)):
+        ends[n : n + 1, : row.shape[0]] = line(row)
+    wait(*out)
 
 
 def serve_kernel(cap, asked, table, out, wide):
     serve(asked[...], 0, cap, table[...], wide, out)
 
 
-def enc_kernel(cap, received, asked, lines, kept, w2, w, one, out, w345, w8, one_v, wide, packed, rows, sems):
-    copies = start(sems, 0, (w.at[pl.ds(3, 3)], w345), (w.at[8], w8))
-    fence(wide)
-    count = one_v.shape[0]
-    devices = asked.shape[0]
-    pick = choose(lines[0:1, :], cap * devices)
-    to = choose(lines[3:4, :], count)
-    to_t = choose_t(lines[3:4, :], count)
-    take_in(cap, devices, received, kept[:count, :], wide, rows)
+def enc_kernel(
+    cap, received, asked, lines, ends, kept, w2, w, out, proc_kept, w34, w5, w89, w11, wide, rows, sems
+):
+    copies = start(sems, 0, (w.at[pl.ds(3, 2)], w34), (w.at[5], w5))
+    fence(wide)
+    copies += start(sems, 2, (w.at[pl.ds(8, 2)], w89), (w.at[11], w11))
+    fence(wide)
+    count = kept.shape[0] // 2
+    others = asked.shape[0]
+    pick = choose(lines[0:1, :], cap * others)
+    to = choose(ends[0:1, :], count)
+    to_t = choose_t(ends[0:1, :], count)
+    take_in(cap, others, received, kept[:count, :], wide, rows)
     summed = dot(jnp.concatenate([pick, to], axis=1), rows[...])
-    message = finish(summed, w2[...]).astype(BF)
+    message = finish(summed, w2[...], True).astype(BF)
     summed = dot(to_t, message).astype(BF)
-    wait(*copies)
+    wait(copies[0])
     m = kept[count:, :]
-    summed = dot(jnp.concatenate([m, summed], axis=1), w345[:2].reshape(2 * m.shape[1], m.shape[1]))
-    mine = residual(m, finish(summed, w345[2]))
-    one_v[...] = mine
-    serve(asked[...], 1, cap, dot(mine, w8[...]).astype(BF), wide, packed)
-    wait(*start(sems, 2, (one_v, one), (packed, out)))
-
-
-def beside_kernel(
-    one, grid, loc_src, loc_dst, w, kept, w10, dec_kept, g, w9, w8, w11, w6, w7, w15, w17, s, d, sems
-):
-    count = one.shape[0]
-    mine = kept.at[pl.ds(3 * count, count)]
-    grid_one = dec_kept.at[pl.ds(2 * count, count)]
-    copies = start(
-        sems, 0, (one, mine), (w.at[9], w9), (loc_src, s), (loc_dst, d), (w.at[8], w8), (w.at[10], w10),
-        (w.at[11], w11), (grid, g), (w.at[6], w6), (w.at[7], w7), (w.at[15], w15), (w.at[17], w17),
-    )
-    wait(*copies[:2])
-    kept[:count, :] = dot(mine[...], w9[...]).astype(BF)
-    wait(*copies[2:5])
-    start_rows = dot(mine[...], w8[...]).astype(BF)
-    stop = line(d)
-    both = jnp.concatenate([choose(line(s), count), choose(stop, count)], axis=1)
-    summed = dot(both, jnp.concatenate([start_rows, kept[:count, :]], axis=0))
-    wait(copies[5])
-    message = finish(summed, w10[...]).astype(BF)
-    kept[2 * count : 3 * count, :] = dot(choose_t(stop, count), message).astype(BF)
-    wait(copies[6])
-    kept[count : 2 * count, :] = dot(mine[...], w11[...]).astype(BF)
-    wait(*copies[7:10])
-    grid_one[...] = residual(g[...], finish(dot(g[...], w6[...]), w7[...]))
-    wait(copies[10])
-    dec_kept[:count, :] = dot(grid_one[...], w15[...]).astype(BF)
-    wait(copies[11])
-    dec_kept[count : 2 * count, :] = dot(grid_one[...], w17[...]).astype(BF)
-
-
-def proc_kernel(cap, received, asked, lines, kept, w10, w, out, ws, wide, rows, sems):
+    summed = dot(jnp.concatenate([m, summed], axis=1), w34[...].reshape(2 * m.shape[1], m.shape[1]))
+    wait(copies[1])
+    mine = residual(m, finish(summed, w5[...]))
+    wait(*copies[2:])
+    table = dot(mine, w89[0]).astype(BF)
+    serve(asked[...], 1, cap, table, wide, out)
+    proc_kept[:count, :] = dot(mine, w89[1]).astype(BF)
+    proc_kept[count : 2 * count, :] = table
+    proc_kept[2 * count : 3 * count, :] = dot(mine, w11[...]).astype(BF)
+    proc_kept[3 * count :, :] = mine
+
+
+def proc_kernel(
+    cap, local, received, asked, lines, ends, kept, w10, w, dec_far, out, dec_kept, ws, wide, rows, sems
+):
     copies = start(sems, 0, (w.at[pl.ds(12, 3)], ws))
     fence(wide)
+    copies += start(sems, 1, (dec_far, dec_kept))
+    fence(wide)
     count = kept.shape[0] // 4
-    devices = asked.shape[0]
-    pick = choose(lines[1:2, :], cap * devices)
-    to = choose(lines[4:5, :], count)
-    to_t = choose_t(lines[4:5, :], count)
-    take_in(cap, devices, received, kept[:count, :], wide, rows)
-    summed = dot(jnp.concatenate([pick, to], axis=1), rows[...])
-    message = finish(summed, w10[...]).astype(BF)
-    summed = (kept[2 * count : 3 * count, :].astype(F32) + dot(to_t, message)).astype(BF)
-    wait(*copies)
-    summed = kept[count : 2 * count, :].astype(F32) + dot(summed, ws[0])
+    others = asked.shape[0]
+    pick = choose(lines[1:2, :], cap * others)
+    to, near_to = choose(ends[1:2, :], count), choose(ends[3:4, :local], count)
+    near_from = choose(ends[2:3, :local], count)
+    to_t = jnp.concatenate([choose_t(ends[1:2, :], count), choose_t(ends[3:4, :local], count)], axis=1)
+    near = dot(jnp.concatenate([near_to, near_from], axis=1), kept[: 2 * count, :])
+    take_in(cap, others, received, kept[:count, :], wide, rows)
+    far = dot(jnp.concatenate([pick, to], axis=1), rows[...])
+    message = finish(jnp.concatenate([far, near], axis=0), w10[...], True).astype(BF)
+    summed = dot(to_t, message).astype(BF)
+    wait(copies[0])
+    summed = kept[2 * count : 3 * count, :].astype(F32) + dot(summed, ws[0])
     two = residual(kept[3 * count :, :], finish(summed, ws[1]))
     serve(asked[...], 2, cap, dot(two, ws[2]).astype(BF), wide, out)
-
-
-def dec_kernel(cap, devices, received, lines, kept, w, out, w16, ws, wide, rows, sems):
-    copies = start(sems, 0, (w.at[16], w16))
+    wait(copies[1])
+
+
+def dec_kernel(cap, others, received, lines, kept, w, late, out, w16, ws, wide, rows, sems):
+    copies = start(sems, 0, (late, w16))
     fence(wide)
     copies += start(sems, 1, (w.at[pl.ds(18, 2)], ws))
     fence(wide)
     edges = lines.shape[1]
     count = kept.shape[0] // 3
-    pick = choose(lines[2:3, :], cap * devices)
+    pick = choose(lines[2:3, :], cap * others)
     near = iota((edges, count), 0) - 3 * iota((edges, count), 1)
     to = flag((near >= 0) & (near < 3))
     near = iota((count, edges), 1) - 3 * iota((count, edges), 0)
     to_t = flag((near >= 0) & (near < 3))
-    take_in(cap, devices, received, kept[:count, :], wide, rows)
+    take_in(cap, others, received, kept[:count, :], wide, rows)
     summed = dot(jnp.concatenate([pick, to], axis=1), rows[...])
     wait(copies[0])
-    message = finish(summed, w16[...]).astype(BF)
+    message = finish(summed, w16[...], True).astype(BF)
     summed = dot(to_t, message).astype(BF)
-    wait(copies[1])
+    wait(*copies[1:])
     summed = kept[count : 2 * count, :].astype(F32) + dot(summed, ws[0])
     out[...] = residual(kept[2 * count :, :], finish(summed, ws[1]))
 
@@ -318,16 +329,26 @@
     def kept(parts):
         return arr((parts * count, width), BF)
 
-    request, places_of, table, enc_kept, w2 = run(
+    places_of, request = run(
         functools.partial(ask_kernel, cap, devices),
-        (ask, lines, nodes, kept(2), mat),
-        far=(*devs, enc_row, proc_row, dec_row, enc_dst, proc_dst, grid_latent, mesh_latent, weights),
-        held=(across,) * 3 + (row,) * 5 + (nodes, mats(2), square, spare),
-        copies=12,
-        macs=3 * devices * edges * (edges + LANES) + 3 * count * width * width,
+        (lines,),
+        far=(*devs, enc_row, proc_row, dec_row),
+        held=(across,) * 3 + (row,) * 3 + (ask, square, spare),
+        copies=7,
+        macs=3 * devices * edges * (edges + LANES),
+        away=(ask,),
     )
     asked = request.reshape(devices, 1, LANES)
     wanted = lax.all_to_all(asked, AXES, split_axis=0, concat_axis=0, tiled=True).reshape(devices, LANES)
+    table, enc_kept, w2, w10, ends, w16, dec_far = run(
+        prepare_kernel,
+        (nodes, kept(2), mat, mat, lines),
+        far=(grid_latent, mesh_latent, enc_dst, proc_dst, loc_src, loc_dst, weights),
+        held=(nodes, row, row, loc, loc, mats(2), mats(2), mat, mat, mat, kept(3)),
+        copies=15,
+        macs=6 * count * width * width,
+        away=(mat, kept(3)),
+    )
     (sent,) = run(
         functools.partial(serve_kernel, cap),
         (flat,),
@@ -336,31 +357,23 @@
         macs=total * count * width,
     )
     enc_rows = exchange(sent, devices)
-    mesh_one, sent = run(
+    sent, proc_kept = run(
         functools.partial(enc_kernel, cap),
-        near=(enc_rows, wanted, places_of, enc_kept, w2),
+        (flat, kept(4)),
+        near=(enc_rows, wanted, places_of, ends, enc_kept, w2),
         far=(weights,),
-        held=(mats(3), mat, nodes, flat32, flat, rows),
+        held=(mats(2), mat, mats(2), mat, flat32, rows),
         copies=4,
         macs=edge_macs,
-        away=(nodes, flat),
     )
     proc_rows = exchange(sent, devices)
-    proc_kept, w10, dec_kept = run(
-        beside_kernel,
-        (kept(4), mat, kept(3)),
-        far=(mesh_one, grid_latent, loc_src, loc_dst, weights),
-        held=(nodes,) + (mat,) * 7 + (loc, loc),
-        copies=12,
-        macs=11 * count * width * width,
-    )
-    (sent,) = run(
-        functools.partial(proc_kernel, cap),
-        (flat,),
-        near=(proc_rows, wanted, places_of, proc_kept, w10),
-        far=(weights,),
+    sent, dec_kept = run(
+        functools.partial(proc_kernel, cap, loc_src.shape[0]),
+        (flat, kept(3)),
+        near=(proc_rows, wanted, places_of, ends, proc_kept, w10),
+        far=(weights, dec_far),
         held=(mats(3), flat32, rows),
-        copies=1,
+        copies=2,
         macs=edge_macs,
     )
     dec_rows = exchange(sent, devices)
@@ -368,7 +381,7 @@
         functools.partial(dec_kernel, cap, devices),
         (nodes,),
         near=(dec_rows, places_of, dec_kept),
-        far=(weights,),
+        far=(weights, w16),
         held=(mat, mats(2), flat32, rows),
         copies=2,
         macs=edge_macs,

time: 95.7 us -> 94.7 us (0.990)
  starting transfers between devices: 4.25 us -> 11.5 us
  waiting for transfers between devices: 12.8 us -> 5.67 us
    all_to_all x1 -> x0, blocking collectives: 20.9 us -> none  [body(): lax.all_to_all(asked, AXES, split_axis=0, concat_axis=0, tiled=True)]
    all_to_all x2 -> x3, blocking collectives: 41.3 us -> 61.8 us  [exchange(): moved = lax.all_to_all(parts, AXES, split_axis=0, concat_axis=0, tiled=True)]
    all_to_all x1, starting transfers between devices: 4.25 us -> 11.5 us  [body(): lax.all_to_all(asked, AXES, split_axis=0, concat_axis=0, tiled=True)]
    all_to_all x1, waiting for transfers between devices: 12.8 us -> 5.67 us  [body(): lax.all_to_all(asked, AXES, split_axis=0, concat_axis=0, tiled=True)]
where the time goes in v7:
time: 94.7 us; the launch traced here: 94.5 us
  blocking collectives  61.8 us (65%)
  Pallas kernels  15.4 us (16%)
  starting transfers between devices  11.5 us (12%)
  waiting for transfers between devices  5.67 us (6%)
    all_to_all x3, blocking collectives, exchange(): moved = lax.all_to_all(parts, AXES, split_axis=0, concat_axis=0, tiled=True)  61.8 us
    pallas_call x6, Pallas kernels, run(): pl.pallas_call(kernel, out_shape=(*(a if last else pltpu.VMEM(a.shape, a....  15.4 us
    all_to_all x1, starting transfers between devices, body(): lax.all_to_all(asked, AXES, split_axis=0, concat_axis=0, tiled=True)  11.5 us
    all_to_all x1, waiting for transfers between devices, body(): lax.all_to_all(asked, AXES, split_axis=0, concat_axis=0, tiled=True)  5.67 us
  transfers between devices with their start and end apart: 1, of which 1 were waited for; matrix products, arithmetic and copies ran while one was open for 0% of the time, Pallas kernels for 4%

profile of v7, /device:TPU:1, one launch (start us, length us, event | category | flops | bytes accessed | tf_op | source)
XLA Modules:
  0.0 94.5 jit_solution(7701995350243493285)
XLA Ops:
  0.0 2.1 %shard_map.127 = (s32[8,384]{1,0:T(8,128)S(1)}, s32[128,128]{1,0:T(8,128)}) custom-call(s32[1,384]{1,0:T(1,128)} %bitcast.23, s32[1,384]{1,0:T(1,128)} %bitcast.24, s32[1,384]{1,0:T(1,128)} %bitcast.25, s32[384]{0:T(512)} %row0.1, s32[384]{0:T(512)} %row1.1, s32[384]{0:T(512)} %row2.1), custom_call_target="tpu_custom_call" | custom-call | flops 150994944 | bytes 390144 | tf_op jit(solution)/shard_map/pallas_call | solution.py:263
  2.1 11.5 %all-to-all-start = ((s32[128,1,128]{2,1,0:T(1,128)}), s32[128,1,128]{2,1,0:T(1,128)S(1)}, u32[]{:S(2)}, u32[]{:S(2)}) async-start(s32[128,1,128]{2,1,0:T(1,128)} %bitcast.22), calls=%async_computation | async-start | bytes 131072 | tf_op jit(solution)/shard_map/all_to_all | solution.py:342
  13.6 3.8 %shard_map.128 = (bf16[128,512]{1,0:T(8,128)(2,1)S(1)}, bf16[256,512]{1,0:T(8,128)(2,1)S(1)}, bf16[512,512]{1,0:T(8,128)(2,1)S(1)}, bf16[512,512]{1,0:T(8,128)(2...) custom-call(bf16[128,512]{1,0:T(8,128)(2,1)} %grid.1, bf16[128,512]{1,0:T(8,128)(2,1)} %mesh.1, ...), custom_call_target="tpu_custom_call" | custom-call | flops 402653184 | bytes 5653504 | tf_op jit(solution)/shard_map/pallas_call | solution.py:263
  17.5 5.7 %all-to-all-done = s32[128,1,128]{2,1,0:T(1,128)S(1)} async-done(((s32[128,1,128]{2,1,0:T(1,128)}), s32[128,1,128]{2,1,0:T(1,128)S(1)}, u32[]{:S(2)}, u32[]{:S(2)}) %all-to-all-start) | async-done | bytes 65568 | tf_op jit(solution)/shard_map/all_to_all | solution.py:342
  23.2 0.6 shard_map.129
  23.7 20.9 %all_to_all.20 = bf16[128,24,128]{2,1,0:T(8,128)(2,1)S(1)} all-to-all(bf16[128,24,128]{2,1,0:T(8,128)(2,1)S(1)} %bitcast.14), channel_id=1, replica_groups=mesh['band'=8,'patch'=16] {'band','patch'}, dimensions={0} | all-to-all | bytes 1572864 | tf_op jit(solution)/shard_map/all_to_all | solution.py:283
  44.6 3.0 %shard_map.130 = (bf16[3072,128]{1,0:T(8,128)(2,1)S(1)}, bf16[512,512]{1,0:T(8,128)(2,1)S(1)}) custom-call(bf16[3072,128]{1,0:T(8,128)(2,1)S(1)} %bitcast.16, s32[128,128]{1,0:T(8,128)S(1)} %bitcast.18, s32[8,384]{1,0:T(8,128)S(1)} %get-tuple-element.20.lines, s32[8,384]{1,0:T(8,128)S(1)} %get-tuple-element.21.ends, ...), custom_call_target="tpu_custom_call" | custom-call | flops 905969664 | bytes 6946816 | tf_op jit(solution)/shard_map/pallas_call | solution.py:263
  47.6 20.5 %all_to_all.21 = bf16[128,24,128]{2,1,0:T(8,128)(2,1)S(1)} all-to-all(bf16[128,24,128]{2,1,0:T(8,128)(2,1)S(1)} %bitcast.21), channel_id=1, replica_groups=mesh['band'=8,'patch'=16] {'band','patch'}, dimensions={0} | all-to-all | bytes 1572864 | tf_op jit(solution)/shard_map/all_to_all | solution.py:283
  68.1 2.9 %shard_map.131 = (bf16[3072,128]{1,0:T(8,128)(2,1)S(1)}, bf16[384,512]{1,0:T(8,128)(2,1)S(1)}) custom-call(bf16[3072,128]{1,0:T(8,128)(2,1)S(1)} %bitcast.15, s32[128,128]{1,0:T(8,128)S(1)} %bitcast.19, s32[8,384]{1,0:T(8,128)S(1)} %get-tuple-element.20.lines, s32[8,384]{1,0:T(8,128)S(1)} %get-tuple-element.21.ends, ...), custom_call_target="tpu_custom_call" | custom-call | flops 905969664 | bytes 5242880 | tf_op jit(solution)/shard_map/pallas_call | solution.py:263
  71.0 20.5 %all_to_all.22 = bf16[128,24,128]{2,1,0:T(8,128)(2,1)S(1)} all-to-all(bf16[128,24,128]{2,1,0:T(8,128)(2,1)S(1)} %bitcast.20), channel_id=1, replica_groups=mesh['band'=8,'patch'=16] {'band','patch'}, dimensions={0} | all-to-all | bytes 1572864 | tf_op jit(solution)/shard_map/all_to_all | solution.py:283
  91.5 3.0 %shard_map.132 = bf16[128,512]{1,0:T(8,128)(2,1)} custom-call(bf16[3072,128]{1,0:T(8,128)(2,1)S(1)} %bitcast.13, s32[8,384]{1,0:T(8,128)S(1)} %get-tuple-element.20.lines, bf16[384,512]{1,0:T(8,128)(2,1)S(1)} %get-tuple-element.29.kept, bf16[20,512,512]{2,1,0:T(8,128)(2,1)} %w.7, bf16[512,512]{1,0:T(8,128)(2,1)} %get-tuple-element.30.late), custom_call_target="tpu_custom_call" | custom-call | flops 905969664 | bytes 4194304 | tf_op jit(solution)/shard_map/pallas_call | solution.py:263
Async XLA Ops:
  2.1 21.0 %all-to-all-start = ((s32[128,1,128]{2,1,0:T(1,128)}), s32[128,1,128]{2,1,0:T(1,128)S(1)}, u32[]{:S(2)}, u32[]{:S(2)}) async-start(s32[128,1,128]{2,1,0:T(1,128)} %bitcast.22), calls=%async_computation | async-start | bytes 131072 | tf_op jit(solution)/shard_map/all_to_all | solution.py:342

commit v8 on v7

--- a/solution.py
+++ b/solution.py
@@ -100,23 +100,30 @@
 def serve(asked, kind, cap, table, wide, out):
     devices = asked.shape[0]
     blocks = table.shape[1] // LANES
+    each, pitch = cap * blocks, wide.shape[0] // devices
     lanes = iota((devices, table.shape[0]), 1)
     hot = [flag(asked[:, lane : lane + 1] == lanes) for lane in range(kind * cap, kind * cap + cap)]
     got = dot(jnp.concatenate(hot, axis=0), table)
     for slot in range(cap):
         for block in range(blocks):
-            target = pl.ds(slot * blocks + block, devices, stride=cap * blocks)
+            target = pl.ds(slot * blocks + block, devices, stride=pitch)
             wide[target, :] = got[slot * devices : (slot + 1) * devices, block * LANES : (block + 1) * LANES]
-    out[...] = wide[...].astype(BF)
+    for first in range(0, devices, 2):
+        pair = [wide[pitch * n : pitch * n + each, :] for n in (first, first + 1)]
+        out[each * first : each * (first + 2), :] = jnp.concatenate(pair, axis=0).astype(BF)
 
 
 def take_in(cap, devices, packed, ends, wide, rows):
     blocks = rows.shape[1] // LANES
+    each, pitch = cap * blocks, wide.shape[0] // devices
     rows[cap * devices :, :] = ends
-    wide[...] = packed[...].astype(F32)
+    for first in range(0, devices, 2):
+        pair = packed[each * first : each * (first + 2), :].astype(F32)
+        wide[pitch * first : pitch * first + each, :] = pair[:each]
+        wide[pitch * (first + 1) : pitch * (first + 1) + each, :] = pair[each:]
     for slot in range(cap):
         for block in range(blocks):
-            source = pl.ds(slot * blocks + block, devices, stride=cap * blocks)
+            source = pl.ds(slot * blocks + block, devices, stride=pitch)
             target = pl.ds(slot * devices, devices)
             rows[target, block * LANES : (block + 1) * LANES] = wide[source, :].astype(BF)
 
@@ -130,44 +137,51 @@
     copies = start(sems, 0, *zip((dev0, dev1, dev2, row0, row1, row2), devs + rows))
     earlier[...] = flag(iota((edges, edges), 0) < iota((edges, edges), 1))
     fence(spare)
-    wait(*copies)
+    wait(*copies[:3])
     hits = [iota((devices, edges), 0) == dev[...] for dev in devs]
     before = dot(flag(jnp.concatenate(hits, axis=0)), earlier[...])
+    wait(*copies[3:])
+    few = -(-3 * cap // 16) * 16
     values = []
     for kind in range(3):
         mine = jnp.where(hits[kind], before[kind * devices : (kind + 1) * devices, :], 0.0)
         place = jnp.sum(mine, axis=0, keepdims=True).astype(I32)
         lines[kind : kind + 1, :] = place * devices + devs[kind][...]
         row = line(rows[kind]).astype(F32)
-        values.append(jnp.where(iota((LANES, edges), 0) == place + kind * cap, row, 0.0).astype(BF))
+        values.append(jnp.where(iota((few, edges), 0) == place + kind * cap, row, 0.0).astype(BF))
     hits = flag(jnp.concatenate(hits, axis=1))
-    asking[...] = dot_lanes(hits, jnp.concatenate(values, axis=1)).astype(I32)
+    asking[:, :few] = dot_lanes(hits, jnp.concatenate(values, axis=1)).astype(I32)
+    asking[:, few:] = jnp.zeros((devices, LANES - few), I32)
     wait(*start(sems, 6, (asking, request)))
 
 
 def prepare_kernel(
     grid, mesh, dst0, dst1, src2, dst2, w, table, kept, w2, w10, ends, w16, dec_kept,
-    g, e0, e1, e2, e3, w01, w67, w16_v, w15, w17, dec_kept_v, sems,
+    g, e0, e1, e2, e3, w01, w67, w16_v, w15, w17, dec_kept_v, spare, sems,
 ):
     count = g.shape[0]
     m = kept.at[pl.ds(count, count)]
     one = dec_kept_v.at[pl.ds(2 * count, count)]
-    copies = start(
-        sems, 0, (grid, g), (w.at[pl.ds(0, 2)], w01), (mesh, m), (w.at[16], w16_v), (w.at[pl.ds(6, 2)], w67),
-        (w.at[15], w15), (w.at[17], w17), (w.at[2], w2), (w.at[10], w10), (dst0, e0), (dst1, e1), (src2, e2), (dst2, e3),
-    )
-    wait(*copies[:3])
+    copies = start(sems, 0, (grid, g), (w.at[pl.ds(6, 2)], w67))
+    fence(spare)
+    copies += start(sems, 2, (w.at[15], w15), (w.at[17], w17), (w.at[16], w16_v))
+    fence(spare)
+    copies += start(
+        sems, 5, (mesh, m), (w.at[pl.ds(0, 2)], w01), (w.at[2], w2), (w.at[10], w10), (dst0, e0), (dst1, e1),
+        (src2, e2), (dst2, e3),
+    )
+    fence(spare)
+    wait(*copies[:2])
+    one[...] = residual(g[...], finish(dot(g[...], w67[0]), w67[1]))
+    wait(*copies[2:5])
+    dec_kept_v[:count, :] = dot(one[...], w15[...]).astype(BF)
+    dec_kept_v[count : 2 * count, :] = dot(one[...], w17[...]).astype(BF)
+    w16_v[...] = centred(w16_v[...])
+    out = start(sems, len(copies), (w16_v, w16), (dec_kept_v, dec_kept))
+    fence(spare)
+    wait(*copies[5:])
     table[...] = dot(g[...], w01[0]).astype(BF)
     kept[:count, :] = dot(m[...], w01[1]).astype(BF)
-    wait(copies[3])
-    w16_v[...] = centred(w16_v[...])
-    out = start(sems, len(copies), (w16_v, w16))
-    wait(*copies[4:7])
-    one[...] = residual(g[...], finish(dot(g[...], w67[0]), w67[1]))
-    dec_kept_v[:count, :] = dot(one[...], w15[...]).astype(BF)
-    dec_kept_v[count : 2 * count, :] = dot(one[...], w17[...]).astype(BF)
-    out += start(sems, len(copies) + 1, (dec_kept_v, dec_kept))
-    wait(*copies[7:])
     w2[...] = centred(w2[...])
     w10[...] = centred(w10[...])
     for n, row in enumerate((e0, e1, e2, e3)):
@@ -210,11 +224,11 @@
 
 
 def proc_kernel(
-    cap, local, received, asked, lines, ends, kept, w10, w, dec_far, out, dec_kept, ws, wide, rows, sems
+    cap, local, received, asked, lines, ends, kept, w10, w, dec_far, w16_far, out, dec_kept, w16, ws, wide, rows, sems
 ):
     copies = start(sems, 0, (w.at[pl.ds(12, 3)], ws))
     fence(wide)
-    copies += start(sems, 1, (dec_far, dec_kept))
+    copies += start(sems, 1, (dec_far, dec_kept), (w16_far, w16))
     fence(wide)
     count = kept.shape[0] // 4
     others = asked.shape[0]
@@ -231,13 +245,11 @@
     summed = kept[2 * count : 3 * count, :].astype(F32) + dot(summed, ws[0])
     two = residual(kept[3 * count :, :], finish(summed, ws[1]))
     serve(asked[...], 2, cap, dot(two, ws[2]).astype(BF), wide, out)
-    wait(copies[1])
-
-
-def dec_kernel(cap, others, received, lines, kept, w, late, out, w16, ws, wide, rows, sems):
-    copies = start(sems, 0, (late, w16))
-    fence(wide)
-    copies += start(sems, 1, (w.at[pl.ds(18, 2)], ws))
+    wait(*copies[1:])
+
+
+def dec_kernel(cap, others, received, lines, kept, w16, w, out, ws, wide, rows, sems):
+    copies = start(sems, 0, (w.at[pl.ds(18, 2)], ws))
     fence(wide)
     edges = lines.shape[1]
     count = kept.shape[0] // 3
@@ -248,10 +260,9 @@
     to_t = flag((near >= 0) & (near < 3))
     take_in(cap, others, received, kept[:count, :], wide, rows)
     summed = dot(jnp.concatenate([pick, to], axis=1), rows[...])
-    wait(copies[0])
     message = finish(summed, w16[...], True).astype(BF)
     summed = dot(to_t, message).astype(BF)
-    wait(*copies[1:])
+    wait(*copies)
     summed = kept[count : 2 * count, :].astype(F32) + dot(summed, ws[0])
     out[...] = residual(kept[2 * count :, :], finish(summed, ws[1]))
 
@@ -318,7 +329,7 @@
     lines = arr((8, edges), I32)
     ask = arr((devices, LANES), I32)
     flat = arr((total * width // LANES, LANES), BF)
-    flat32 = arr(flat.shape, F32)
+    flat32 = arr((devices * (cap * width // LANES + 1), LANES), F32)
     rows = arr((total + count, width), BF)
     edge_macs = edges * width * (total + 3 * width)
     devs = tuple(a.reshape(1, edges) for a in (enc_dev, proc_dev, dec_dev))
@@ -340,11 +351,11 @@
     )
     asked = request.reshape(devices, 1, LANES)
     wanted = lax.all_to_all(asked, AXES, split_axis=0, concat_axis=0, tiled=True).reshape(devices, LANES)
-    table, enc_kept, w2, w10, ends, w16, dec_far = run(
+    table, enc_kept, w2, w10, ends, w16_far, dec_far = run(
         prepare_kernel,
         (nodes, kept(2), mat, mat, lines),
         far=(grid_latent, mesh_latent, enc_dst, proc_dst, loc_src, loc_dst, weights),
-        held=(nodes, row, row, loc, loc, mats(2), mats(2), mat, mat, mat, kept(3)),
+        held=(nodes, row, row, loc, loc, mats(2), mats(2), mat, mat, mat, kept(3), spare),
         copies=15,
         macs=6 * count * width * width,
         away=(mat, kept(3)),
@@ -367,23 +378,23 @@
         macs=edge_macs,
     )
     proc_rows = exchange(sent, devices)
-    sent, dec_kept = run(
+    sent, dec_kept, w16 = run(
         functools.partial(proc_kernel, cap, loc_src.shape[0]),
-        (flat, kept(3)),
+        (flat, kept(3), mat),
         near=(proc_rows, wanted, places_of, ends, proc_kept, w10),
-        far=(weights, dec_far),
+        far=(weights, dec_far, w16_far),
         held=(mats(3), flat32, rows),
-        copies=2,
+        copies=3,
         macs=edge_macs,
     )
     dec_rows = exchange(sent, devices)
     (decoded,) = run(
         functools.partial(dec_kernel, cap, devices),
         (nodes,),
-        near=(dec_rows, places_of, dec_kept),
-        far=(weights, w16),
-        held=(mat, mats(2), flat32, rows),
-        copies=2,
+        near=(dec_rows, places_of, dec_kept, w16),
+        far=(weights,),
+        held=(mats(2), flat32, rows),
+        copies=1,
         macs=edge_macs,
         last=True,
     )

time: 94.7 us -> 93.8 us (level)
  Pallas kernels: 15.4 us -> 14 us
    pallas_call x6, Pallas kernels: 15.4 us -> 14 us  [run(): pl.pallas_call(kernel, out_shape=(*(a if last else pltpu.VMEM(a.shape, a....]
where the time goes in v8:
time: 93.8 us; the launch traced here: 93.6 us
  blocking collectives  61.8 us (66%)
  Pallas kernels  14 us (15%)
  starting transfers between devices  11.5 us (12%)
  waiting for transfers between devices  6.2 us (7%)
    all_to_all x3, blocking collectives, exchange(): moved = lax.all_to_all(parts, AXES, split_axis=0, concat_axis=0, tiled=True)  61.8 us
    pallas_call x6, Pallas kernels, run(): pl.pallas_call(kernel, out_shape=(*(a if last else pltpu.VMEM(a.shape, a....  14 us
    all_to_all x1, starting transfers between devices, body(): lax.all_to_all(asked, AXES, split_axis=0, concat_axis=0, tiled=True)  11.5 us
    all_to_all x1, waiting for transfers between devices, body(): lax.all_to_all(asked, AXES, split_axis=0, concat_axis=0, tiled=True)  6.2 us
  transfers between devices with their start and end apart: 1, of which 1 were waited for; matrix products, arithmetic and copies ran while one was open for 0% of the time, Pallas kernels for 4%

profile of v8, /device:TPU:1, one launch (start us, length us, event | category | flops | bytes accessed | tf_op | source)
XLA Modules:
  0.0 93.6 jit_solution(15495152331860994530)
XLA Ops:
  0.0 2.1 %shard_map.127 = (s32[8,384]{1,0:T(8,128)S(1)}, s32[128,128]{1,0:T(8,128)}) custom-call(s32[1,384]{1,0:T(1,128)} %bitcast.23, s32[1,384]{1,0:T(1,128)} %bitcast.24, s32[1,384]{1,0:T(1,128)} %bitcast.25, s32[384]{0:T(512)} %row0.1, s32[384]{0:T(512)} %row1.1, s32[384]{0:T(512)} %row2.1), custom_call_target="tpu_custom_call" | custom-call | flops 150994944 | bytes 390144 | tf_op jit(solution)/shard_map/pallas_call | solution.py:274
  2.1 11.5 %all-to-all-start = ((s32[128,1,128]{2,1,0:T(1,128)}), s32[128,1,128]{2,1,0:T(1,128)S(1)}, u32[]{:S(2)}, u32[]{:S(2)}) async-start(s32[128,1,128]{2,1,0:T(1,128)} %bitcast.22), calls=%async_computation | async-start | bytes 131072 | tf_op jit(solution)/shard_map/all_to_all | solution.py:353
  13.6 3.3 %shard_map.128 = (bf16[128,512]{1,0:T(8,128)(2,1)S(1)}, bf16[256,512]{1,0:T(8,128)(2,1)S(1)}, bf16[512,512]{1,0:T(8,128)(2,1)S(1)}, bf16[512,512]{1,0:T(8,128)(2...) custom-call(bf16[128,512]{1,0:T(8,128)(2,1)} %grid.1, bf16[128,512]{1,0:T(8,128)(2,1)} %mesh.1, ...), custom_call_target="tpu_custom_call" | custom-call | flops 402653184 | bytes 5661696 | tf_op jit(solution)/shard_map/pallas_call | solution.py:274
  16.9 6.2 %all-to-all-done = s32[128,1,128]{2,1,0:T(1,128)S(1)} async-done(((s32[128,1,128]{2,1,0:T(1,128)}), s32[128,1,128]{2,1,0:T(1,128)S(1)}, u32[]{:S(2)}, u32[]{:S(2)}) %all-to-all-start) | async-done | bytes 65568 | tf_op jit(solution)/shard_map/all_to_all | solution.py:353
  23.1 0.5 shard_map.129
  23.6 20.9 %all_to_all.20 = bf16[128,24,128]{2,1,0:T(8,128)(2,1)S(1)} all-to-all(bf16[128,24,128]{2,1,0:T(8,128)(2,1)S(1)} %bitcast.15), channel_id=1, replica_groups=mesh['band'=8,'patch'=16] {'band','patch'}, dimensions={0} | all-to-all | bytes 1572864 | tf_op jit(solution)/shard_map/all_to_all | solution.py:294
  44.5 2.8 %shard_map.130 = (bf16[3072,128]{1,0:T(8,128)(2,1)S(1)}, bf16[512,512]{1,0:T(8,128)(2,1)S(1)}) custom-call(bf16[3072,128]{1,0:T(8,128)(2,1)S(1)} %bitcast.16, s32[128,128]{1,0:T(8,128)S(1)} %bitcast.18, s32[8,384]{1,0:T(8,128)S(1)} %get-tuple-element.21.lines, s32[8,384]{1,0:T(8,128)S(1)} %get-tuple-element.22.ends, ...), custom_call_target="tpu_custom_call" | custom-call | flops 905969664 | bytes 7012352 | tf_op jit(solution)/shard_map/pallas_call | solution.py:274
  47.3 20.5 %all_to_all.21 = bf16[128,24,128]{2,1,0:T(8,128)(2,1)S(1)} all-to-all(bf16[128,24,128]{2,1,0:T(8,128)(2,1)S(1)} %bitcast.21), channel_id=1, replica_groups=mesh['band'=8,'patch'=16] {'band','patch'}, dimensions={0} | all-to-all | bytes 1572864 | tf_op jit(solution)/shard_map/all_to_all | solution.py:294
  67.8 2.7 %shard_map.131 = (bf16[3072,128]{1,0:T(8,128)(2,1)S(1)}, bf16[384,512]{1,0:T(8,128)(2,1)S(1)}, bf16[512,512]{1,0:T(8,128)(2,1)S(1)}) custom-call(bf16[3072,128]{1,0:T(8,128)(2,1)S(1)} %bitcast.13, s32[128,128]{1,0:T(8,128)S(1)} %bitcast.19, s32[8,384]{1,0:T(8,128)S(1)} %get-tuple-element.21.lines, s32[8,384]{1,0:T(8,128)S(1)} %get-tuple-element.22.ends, ...), custom_call_target="tpu_custom_call" | custom-call | flops 905969664 | bytes 5832704 | tf_op jit(solution)/shard_map/pallas_call | solution.py:274
  70.5 20.5 %all_to_all.22 = bf16[128,24,128]{2,1,0:T(8,128)(2,1)S(1)} all-to-all(bf16[128,24,128]{2,1,0:T(8,128)(2,1)S(1)} %bitcast.20), channel_id=1, replica_groups=mesh['band'=8,'patch'=16] {'band','patch'}, dimensions={0} | all-to-all | bytes 1572864 | tf_op jit(solution)/shard_map/all_to_all | solution.py:294
  91.0 2.6 %shard_map.132 = bf16[128,512]{1,0:T(8,128)(2,1)} custom-call(bf16[3072,128]{1,0:T(8,128)(2,1)S(1)} %bitcast.14, s32[8,384]{1,0:T(8,128)S(1)} %get-tuple-element.21.lines, bf16[384,512]{1,0:T(8,128)(2,1)S(1)} %get-tuple-element.31.kept, bf16[512,512]{1,0:T(8,128)(2,1)S(1)} %get-tuple-element.32.w16, bf16[20,512,512]{2,1,0:T(8,128)(2,1)} %w.7), custom_call_target="tpu_custom_call" | custom-call | flops 905969664 | bytes 3735552 | tf_op jit(solution)/shard_map/pallas_call | solution.py:274
Async XLA Ops:
  2.1 21.0 %all-to-all-start = ((s32[128,1,128]{2,1,0:T(1,128)}), s32[128,1,128]{2,1,0:T(1,128)S(1)}, u32[]{:S(2)}, u32[]{:S(2)}) async-start(s32[128,1,128]{2,1,0:T(1,128)} %bitcast.22), calls=%async_computation | async-start | bytes 131072 | tf_op jit(solution)/shard_map/all_to_all | solution.py:353

commit v9 on v8

--- a/solution.py
+++ b/solution.py
@@ -157,7 +157,7 @@
 
 def prepare_kernel(
     grid, mesh, dst0, dst1, src2, dst2, w, table, kept, w2, w10, ends, w16, dec_kept,
-    g, e0, e1, e2, e3, w01, w67, w16_v, w15, w17, dec_kept_v, spare, sems,
+    g, e0, e1, e2, e3, w01, w3, w67, w16_v, w15, w17, dec_kept_v, spare, sems,
 ):
     count = g.shape[0]
     m = kept.at[pl.ds(count, count)]
@@ -167,7 +167,7 @@
     copies += start(sems, 2, (w.at[15], w15), (w.at[17], w17), (w.at[16], w16_v))
     fence(spare)
     copies += start(
-        sems, 5, (mesh, m), (w.at[pl.ds(0, 2)], w01), (w.at[2], w2), (w.at[10], w10), (dst0, e0), (dst1, e1),
+        sems, 5, (mesh, m), (w.at[pl.ds(0, 2)], w01), (w.at[3], w3), (w.at[2], w2), (w.at[10], w10), (dst0, e0), (dst1, e1),
         (src2, e2), (dst2, e3),
     )
     fence(spare)
@@ -182,6 +182,7 @@
     wait(*copies[5:])
     table[...] = dot(g[...], w01[0]).astype(BF)
     kept[:count, :] = dot(m[...], w01[1]).astype(BF)
+    kept[2 * count :, :] = dot(m[...], w3[...]).astype(BF)
     w2[...] = centred(w2[...])
     w10[...] = centred(w10[...])
     for n, row in enumerate((e0, e1, e2, e3)):
@@ -194,13 +195,13 @@
 
 
 def enc_kernel(
-    cap, received, asked, lines, ends, kept, w2, w, out, proc_kept, w34, w5, w89, w11, wide, rows, sems
+    cap, received, asked, lines, ends, kept, w2, w, out, proc_kept, w45, w89, w11, wide, rows, sems
 ):
-    copies = start(sems, 0, (w.at[pl.ds(3, 2)], w34), (w.at[5], w5))
+    copies = start(sems, 0, (w.at[pl.ds(4, 2)], w45))
     fence(wide)
-    copies += start(sems, 2, (w.at[pl.ds(8, 2)], w89), (w.at[11], w11))
+    copies += start(sems, 1, (w.at[pl.ds(8, 2)], w89), (w.at[11], w11))
     fence(wide)
-    count = kept.shape[0] // 2
+    count = kept.shape[0] // 3
     others = asked.shape[0]
     pick = choose(lines[0:1, :], cap * others)
     to = choose(ends[0:1, :], count)
@@ -210,11 +211,9 @@
     message = finish(summed, w2[...], True).astype(BF)
     summed = dot(to_t, message).astype(BF)
     wait(copies[0])
-    m = kept[count:, :]
-    summed = dot(jnp.concatenate([m, summed], axis=1), w34[...].reshape(2 * m.shape[1], m.shape[1]))
-    wait(copies[1])
-    mine = residual(m, finish(summed, w5[...]))
-    wait(*copies[2:])
+    summed = kept[2 * count :, :].astype(F32) + dot(summed, w45[0])
+    mine = residual(kept[count : 2 * count, :], finish(summed, w45[1]))
+    wait(*copies[1:])
     table = dot(mine, w89[0]).astype(BF)
     serve(asked[...], 1, cap, table, wide, out)
     proc_kept[:count, :] = dot(mine, w89[1]).astype(BF)
@@ -329,7 +328,8 @@
     lines = arr((8, edges), I32)
     ask = arr((devices, LANES), I32)
     flat = arr((total * width // LANES, LANES), BF)
-    flat32 = arr((devices * (cap * width // LANES + 1), LANES), F32)
+    spread = devices * (cap * width // LANES + 1)
+    flat32 = arr((spread + 32, LANES), F32)
     rows = arr((total + count, width), BF)
     edge_macs = edges * width * (total + 3 * width)
     devs = tuple(a.reshape(1, edges) for a in (enc_dev, proc_dev, dec_dev))
@@ -353,10 +353,10 @@
     wanted = lax.all_to_all(asked, AXES, split_axis=0, concat_axis=0, tiled=True).reshape(devices, LANES)
     table, enc_kept, w2, w10, ends, w16_far, dec_far = run(
         prepare_kernel,
-        (nodes, kept(2), mat, mat, lines),
+        (nodes, kept(3), mat, mat, lines),
         far=(grid_latent, mesh_latent, enc_dst, proc_dst, loc_src, loc_dst, weights),
-        held=(nodes, row, row, loc, loc, mats(2), mats(2), mat, mat, mat, kept(3), spare),
-        copies=15,
+        held=(nodes, row, row, loc, loc, mats(2), mat, mats(2), mat, mat, mat, kept(3), spare),
+        copies=16,
         macs=6 * count * width * width,
         away=(mat, kept(3)),
     )
@@ -373,8 +373,8 @@
         (flat, kept(4)),
         near=(enc_rows, wanted, places_of, ends, enc_kept, w2),
         far=(weights,),
-        held=(mats(2), mat, mats(2), mat, flat32, rows),
-        copies=4,
+        held=(mats(2), mats(2), mat, flat32, rows),
+        copies=3,
         macs=edge_macs,
     )
     proc_rows = exchange(sent, devices)

time: 93.8 us -> 93.7 us (level)
  no operation moved by 1% of the time
where the time goes in v9:
time: 93.7 us; the launch traced here: 93.5 us
  blocking collectives  61.8 us (66%)
  Pallas kernels  13.9 us (15%)
  starting transfers between devices  11.5 us (12%)
  waiting for transfers between devices  6.19 us (7%)
    all_to_all x3, blocking collectives, exchange(): moved = lax.all_to_all(parts, AXES, split_axis=0, concat_axis=0, tiled=True)  61.8 us
    pallas_call x6, Pallas kernels, run(): pl.pallas_call(kernel, out_shape=(*(a if last else pltpu.VMEM(a.shape, a....  13.9 us
    all_to_all x1, starting transfers between devices, body(): lax.all_to_all(asked, AXES, split_axis=0, concat_axis=0, tiled=True)  11.5 us
    all_to_all x1, waiting for transfers between devices, body(): lax.all_to_all(asked, AXES, split_axis=0, concat_axis=0, tiled=True)  6.19 us
  transfers between devices with their start and end apart: 1, of which 1 were waited for; matrix products, arithmetic and copies ran while one was open for 0% of the time, Pallas kernels for 4%

profile of v9, /device:TPU:1, one launch (start us, length us, event | category | flops | bytes accessed | tf_op | source)
XLA Modules:
  0.0 93.5 jit_solution(17748486045500834595)
XLA Ops:
  0.0 2.1 %shard_map.127 = (s32[8,384]{1,0:T(8,128)S(1)}, s32[128,128]{1,0:T(8,128)}) custom-call(s32[1,384]{1,0:T(1,128)} %bitcast.23, s32[1,384]{1,0:T(1,128)} %bitcast.24, s32[1,384]{1,0:T(1,128)} %bitcast.25, s32[384]{0:T(512)} %row0.1, s32[384]{0:T(512)} %row1.1, s32[384]{0:T(512)} %row2.1), custom_call_target="tpu_custom_call" | custom-call | flops 150994944 | bytes 390144 | tf_op jit(solution)/shard_map/pallas_call | solution.py:273
  2.1 11.5 %all-to-all-start = ((s32[128,1,128]{2,1,0:T(1,128)}), s32[128,1,128]{2,1,0:T(1,128)S(1)}, u32[]{:S(2)}, u32[]{:S(2)}) async-start(s32[128,1,128]{2,1,0:T(1,128)} %bitcast.22), calls=%async_computation | async-start | bytes 131072 | tf_op jit(solution)/shard_map/all_to_all | solution.py:353
  13.6 3.3 %shard_map.128 = (bf16[128,512]{1,0:T(8,128)(2,1)S(1)}, bf16[384,512]{1,0:T(8,128)(2,1)S(1)}, bf16[512,512]{1,0:T(8,128)(2,1)S(1)}, bf16[512,512]{1,0:T(8,128)(2...) custom-call(bf16[128,512]{1,0:T(8,128)(2,1)} %grid.1, bf16[128,512]{1,0:T(8,128)(2,1)} %mesh.1, ...), custom_call_target="tpu_custom_call" | custom-call | flops 402653184 | bytes 6317056 | tf_op jit(solution)/shard_map/pallas_call | solution.py:273
  17.0 6.2 %all-to-all-done = s32[128,1,128]{2,1,0:T(1,128)S(1)} async-done(((s32[128,1,128]{2,1,0:T(1,128)}), s32[128,1,128]{2,1,0:T(1,128)S(1)}, u32[]{:S(2)}, u32[]{:S(2)}) %all-to-all-start) | async-done | bytes 65568 | tf_op jit(solution)/shard_map/all_to_all | solution.py:353
  23.1 0.5 shard_map.129
  23.6 20.9 %all_to_all.20 = bf16[128,24,128]{2,1,0:T(8,128)(2,1)S(1)} all-to-all(bf16[128,24,128]{2,1,0:T(8,128)(2,1)S(1)} %bitcast.15), channel_id=1, replica_groups=mesh['band'=8,'patch'=16] {'band','patch'}, dimensions={0} | all-to-all | bytes 1572864 | tf_op jit(solution)/shard_map/all_to_all | solution.py:293
  44.5 2.7 %shard_map.130 = (bf16[3072,128]{1,0:T(8,128)(2,1)S(1)}, bf16[512,512]{1,0:T(8,128)(2,1)S(1)}) custom-call(bf16[3072,128]{1,0:T(8,128)(2,1)S(1)} %bitcast.16, s32[128,128]{1,0:T(8,128)S(1)} %bitcast.18, s32[8,384]{1,0:T(8,128)S(1)} %get-tuple-element.21.lines, s32[8,384]{1,0:T(8,128)S(1)} %get-tuple-element.22.ends, ...), custom_call_target="tpu_custom_call" | custom-call | flops 905969664 | bytes 6504448 | tf_op jit(solution)/shard_map/pallas_call | solution.py:273
  47.2 20.5 %all_to_all.21 = bf16[128,24,128]{2,1,0:T(8,128)(2,1)S(1)} all-to-all(bf16[128,24,128]{2,1,0:T(8,128)(2,1)S(1)} %bitcast.21), channel_id=1, replica_groups=mesh['band'=8,'patch'=16] {'band','patch'}, dimensions={0} | all-to-all | bytes 1572864 | tf_op jit(solution)/shard_map/all_to_all | solution.py:293
  67.7 2.7 %shard_map.131 = (bf16[3072,128]{1,0:T(8,128)(2,1)S(1)}, bf16[384,512]{1,0:T(8,128)(2,1)S(1)}, bf16[512,512]{1,0:T(8,128)(2,1)S(1)}) custom-call(bf16[3072,128]{1,0:T(8,128)(2,1)S(1)} %bitcast.13, s32[128,128]{1,0:T(8,128)S(1)} %bitcast.19, s32[8,384]{1,0:T(8,128)S(1)} %get-tuple-element.21.lines, s32[8,384]{1,0:T(8,128)S(1)} %get-tuple-element.22.ends, ...), custom_call_target="tpu_custom_call" | custom-call | flops 905969664 | bytes 5849088 | tf_op jit(solution)/shard_map/pallas_call | solution.py:273
  70.4 20.5 %all_to_all.22 = bf16[128,24,128]{2,1,0:T(8,128)(2,1)S(1)} all-to-all(bf16[128,24,128]{2,1,0:T(8,128)(2,1)S(1)} %bitcast.20), channel_id=1, replica_groups=mesh['band'=8,'patch'=16] {'band','patch'}, dimensions={0} | all-to-all | bytes 1572864 | tf_op jit(solution)/shard_map/all_to_all | solution.py:293
  90.9 2.6 %shard_map.132 = bf16[128,512]{1,0:T(8,128)(2,1)} custom-call(bf16[3072,128]{1,0:T(8,128)(2,1)S(1)} %bitcast.14, s32[8,384]{1,0:T(8,128)S(1)} %get-tuple-element.21.lines, bf16[384,512]{1,0:T(8,128)(2,1)S(1)} %get-tuple-element.31.kept, bf16[512,512]{1,0:T(8,128)(2,1)S(1)} %get-tuple-element.32.w16, bf16[20,512,512]{2,1,0:T(8,128)(2,1)} %w.7), custom_call_target="tpu_custom_call" | custom-call | flops 905969664 | bytes 3751936 | tf_op jit(solution)/shard_map/pallas_call | solution.py:273
Async XLA Ops:
  2.1 21.0 %all-to-all-start = ((s32[128,1,128]{2,1,0:T(1,128)}), s32[128,1,128]{2,1,0:T(1,128)S(1)}, u32[]{:S(2)}, u32[]{:S(2)}) async-start(s32[128,1,128]{2,1,0:T(1,128)} %bitcast.22), calls=%async_computation | async-start | bytes 131072 | tf_op jit(solution)/shard_map/all_to_all | solution.py:353

commit v10 on v8

--- a/solution.py
+++ b/solution.py
@@ -329,7 +329,8 @@
     lines = arr((8, edges), I32)
     ask = arr((devices, LANES), I32)
     flat = arr((total * width // LANES, LANES), BF)
-    flat32 = arr((devices * (cap * width // LANES + 1), LANES), F32)
+    spread = devices * (cap * width // LANES + 1)
+    flat32 = arr((spread + 32, LANES), F32)
     rows = arr((total + count, width), BF)
     edge_macs = edges * width * (total + 3 * width)
     devs = tuple(a.reshape(1, edges) for a in (enc_dev, proc_dev, dec_dev))

time: 93.8 us -> 93.8 us (level)
  no operation moved by 1% of the time
where the time goes in v10:
time: 93.8 us; the launch traced here: 93.6 us
  blocking collectives  61.8 us (66%)
  Pallas kernels  14 us (15%)
  starting transfers between devices  11.5 us (12%)
  waiting for transfers between devices  6.2 us (7%)
    all_to_all x3, blocking collectives, exchange(): moved = lax.all_to_all(parts, AXES, split_axis=0, concat_axis=0, tiled=True)  61.8 us
    pallas_call x6, Pallas kernels, run(): pl.pallas_call(kernel, out_shape=(*(a if last else pltpu.VMEM(a.shape, a....  14 us
    all_to_all x1, starting transfers between devices, body(): lax.all_to_all(asked, AXES, split_axis=0, concat_axis=0, tiled=True)  11.5 us
    all_to_all x1, waiting for transfers between devices, body(): lax.all_to_all(asked, AXES, split_axis=0, concat_axis=0, tiled=True)  6.2 us
  transfers between devices with their start and end apart: 1, of which 1 were waited for; matrix products, arithmetic and copies ran while one was open for 0% of the time, Pallas kernels for 4%

profile of v10, /device:TPU:1, one launch (start us, length us, event | category | flops | bytes accessed | tf_op | source)
XLA Modules:
  0.0 93.6 jit_solution(12923754969812600557)
XLA Ops:
  0.0 2.1 %shard_map.127 = (s32[8,384]{1,0:T(8,128)S(1)}, s32[128,128]{1,0:T(8,128)}) custom-call(s32[1,384]{1,0:T(1,128)} %bitcast.23, s32[1,384]{1,0:T(1,128)} %bitcast.24, s32[1,384]{1,0:T(1,128)} %bitcast.25, s32[384]{0:T(512)} %row0.1, s32[384]{0:T(512)} %row1.1, s32[384]{0:T(512)} %row2.1), custom_call_target="tpu_custom_call" | custom-call | flops 150994944 | bytes 390144 | tf_op jit(solution)/shard_map/pallas_call | solution.py:274
  2.1 11.5 %all-to-all-start = ((s32[128,1,128]{2,1,0:T(1,128)}), s32[128,1,128]{2,1,0:T(1,128)S(1)}, u32[]{:S(2)}, u32[]{:S(2)}) async-start(s32[128,1,128]{2,1,0:T(1,128)} %bitcast.22), calls=%async_computation | async-start | bytes 131072 | tf_op jit(solution)/shard_map/all_to_all | solution.py:354
  13.6 3.3 %shard_map.128 = (bf16[128,512]{1,0:T(8,128)(2,1)S(1)}, bf16[256,512]{1,0:T(8,128)(2,1)S(1)}, bf16[512,512]{1,0:T(8,128)(2,1)S(1)}, bf16[512,512]{1,0:T(8,128)(2...) custom-call(bf16[128,512]{1,0:T(8,128)(2,1)} %grid.1, bf16[128,512]{1,0:T(8,128)(2,1)} %mesh.1, ...), custom_call_target="tpu_custom_call" | custom-call | flops 402653184 | bytes 5661696 | tf_op jit(solution)/shard_map/pallas_call | solution.py:274
  16.9 6.2 %all-to-all-done = s32[128,1,128]{2,1,0:T(1,128)S(1)} async-done(((s32[128,1,128]{2,1,0:T(1,128)}), s32[128,1,128]{2,1,0:T(1,128)S(1)}, u32[]{:S(2)}, u32[]{:S(2)}) %all-to-all-start) | async-done | bytes 65568 | tf_op jit(solution)/shard_map/all_to_all | solution.py:354
  23.1 0.5 shard_map.129
  23.6 20.9 %all_to_all.20 = bf16[128,24,128]{2,1,0:T(8,128)(2,1)S(1)} all-to-all(bf16[128,24,128]{2,1,0:T(8,128)(2,1)S(1)} %bitcast.15), channel_id=1, replica_groups=mesh['band'=8,'patch'=16] {'band','patch'}, dimensions={0} | all-to-all | bytes 1572864 | tf_op jit(solution)/shard_map/all_to_all | solution.py:294
  44.5 2.8 %shard_map.130 = (bf16[3072,128]{1,0:T(8,128)(2,1)S(1)}, bf16[512,512]{1,0:T(8,128)(2,1)S(1)}) custom-call(bf16[3072,128]{1,0:T(8,128)(2,1)S(1)} %bitcast.16, s32[128,128]{1,0:T(8,128)S(1)} %bitcast.18, s32[8,384]{1,0:T(8,128)S(1)} %get-tuple-element.21.lines, s32[8,384]{1,0:T(8,128)S(1)} %get-tuple-element.22.ends, ...), custom_call_target="tpu_custom_call" | custom-call | flops 905969664 | bytes 7028736 | tf_op jit(solution)/shard_map/pallas_call | solution.py:274
  47.3 20.5 %all_to_all.21 = bf16[128,24,128]{2,1,0:T(8,128)(2,1)S(1)} all-to-all(bf16[128,24,128]{2,1,0:T(8,128)(2,1)S(1)} %bitcast.21), channel_id=1, replica_groups=mesh['band'=8,'patch'=16] {'band','patch'}, dimensions={0} | all-to-all | bytes 1572864 | tf_op jit(solution)/shard_map/all_to_all | solution.py:294
  67.8 2.7 %shard_map.131 = (bf16[3072,128]{1,0:T(8,128)(2,1)S(1)}, bf16[384,512]{1,0:T(8,128)(2,1)S(1)}, bf16[512,512]{1,0:T(8,128)(2,1)S(1)}) custom-call(bf16[3072,128]{1,0:T(8,128)(2,1)S(1)} %bitcast.13, s32[128,128]{1,0:T(8,128)S(1)} %bitcast.19, s32[8,384]{1,0:T(8,128)S(1)} %get-tuple-element.21.lines, s32[8,384]{1,0:T(8,128)S(1)} %get-tuple-element.22.ends, ...), custom_call_target="tpu_custom_call" | custom-call | flops 905969664 | bytes 5849088 | tf_op jit(solution)/shard_map/pallas_call | solution.py:274
  70.5 20.5 %all_to_all.22 = bf16[128,24,128]{2,1,0:T(8,128)(2,1)S(1)} all-to-all(bf16[128,24,128]{2,1,0:T(8,128)(2,1)S(1)} %bitcast.20), channel_id=1, replica_groups=mesh['band'=8,'patch'=16] {'band','patch'}, dimensions={0} | all-to-all | bytes 1572864 | tf_op jit(solution)/shard_map/all_to_all | solution.py:294
  91.0 2.6 %shard_map.132 = bf16[128,512]{1,0:T(8,128)(2,1)} custom-call(bf16[3072,128]{1,0:T(8,128)(2,1)S(1)} %bitcast.14, s32[8,384]{1,0:T(8,128)S(1)} %get-tuple-element.21.lines, bf16[384,512]{1,0:T(8,128)(2,1)S(1)} %get-tuple-element.31.kept, bf16[512,512]{1,0:T(8,128)(2,1)S(1)} %get-tuple-element.32.w16, bf16[20,512,512]{2,1,0:T(8,128)(2,1)} %w.7), custom_call_target="tpu_custom_call" | custom-call | flops 905969664 | bytes 3751936 | tf_op jit(solution)/shard_map/pallas_call | solution.py:274
Async XLA Ops:
  2.1 21.0 %all-to-all-start = ((s32[128,1,128]{2,1,0:T(1,128)}), s32[128,1,128]{2,1,0:T(1,128)S(1)}, u32[]{:S(2)}, u32[]{:S(2)}) async-start(s32[128,1,128]{2,1,0:T(1,128)} %bitcast.22), calls=%async_computation | async-start | bytes 131072 | tf_op jit(solution)/shard_map/all_to_all | solution.py:354

commit v11 on v10

--- a/solution.py
+++ b/solution.py
@@ -157,32 +157,31 @@
 
 def prepare_kernel(
     grid, mesh, dst0, dst1, src2, dst2, w, table, kept, w2, w10, ends, w16, dec_kept,
-    g, e0, e1, e2, e3, w01, w67, w16_v, w15, w17, dec_kept_v, spare, sems,
+    g, e0, e1, e2, e3, first, w67, mid, dec_kept_v, spare, sems,
 ):
     count = g.shape[0]
     m = kept.at[pl.ds(count, count)]
     one = dec_kept_v.at[pl.ds(2 * count, count)]
     copies = start(sems, 0, (grid, g), (w.at[pl.ds(6, 2)], w67))
     fence(spare)
-    copies += start(sems, 2, (w.at[15], w15), (w.at[17], w17), (w.at[16], w16_v))
+    copies += start(sems, 2, (w.at[pl.ds(15, 3)], mid))
     fence(spare)
     copies += start(
-        sems, 5, (mesh, m), (w.at[pl.ds(0, 2)], w01), (w.at[2], w2), (w.at[10], w10), (dst0, e0), (dst1, e1),
-        (src2, e2), (dst2, e3),
+        sems, 3, (mesh, m), (w.at[pl.ds(0, 3)], first), (w.at[10], w10), (dst0, e0), (dst1, e1), (src2, e2), (dst2, e3)
     )
     fence(spare)
     wait(*copies[:2])
     one[...] = residual(g[...], finish(dot(g[...], w67[0]), w67[1]))
-    wait(*copies[2:5])
-    dec_kept_v[:count, :] = dot(one[...], w15[...]).astype(BF)
-    dec_kept_v[count : 2 * count, :] = dot(one[...], w17[...]).astype(BF)
-    w16_v[...] = centred(w16_v[...])
-    out = start(sems, len(copies), (w16_v, w16), (dec_kept_v, dec_kept))
+    wait(copies[2])
+    dec_kept_v[:count, :] = dot(one[...], mid[0]).astype(BF)
+    dec_kept_v[count : 2 * count, :] = dot(one[...], mid[2]).astype(BF)
+    mid[1] = centred(mid[1])
+    out = start(sems, len(copies), (mid.at[1], w16), (dec_kept_v, dec_kept))
     fence(spare)
-    wait(*copies[5:])
-    table[...] = dot(g[...], w01[0]).astype(BF)
-    kept[:count, :] = dot(m[...], w01[1]).astype(BF)
-    w2[...] = centred(w2[...])
+    wait(*copies[3:])
+    table[...] = dot(g[...], first[0]).astype(BF)
+    kept[:count, :] = dot(m[...], first[1]).astype(BF)
+    w2[...] = centred(first[2])
     w10[...] = centred(w10[...])
     for n, row in enumerate((e0, e1, e2, e3)):
         ends[n : n + 1, : row.shape[0]] = line(row)
@@ -356,8 +355,8 @@
         prepare_kernel,
         (nodes, kept(2), mat, mat, lines),
         far=(grid_latent, mesh_latent, enc_dst, proc_dst, loc_src, loc_dst, weights),
-        held=(nodes, row, row, loc, loc, mats(2), mats(2), mat, mat, mat, kept(3), spare),
-        copies=15,
+        held=(nodes, row, row, loc, loc, mats(3), mats(2), mats(3), kept(3), spare),
+        copies=12,
         macs=6 * count * width * width,
         away=(mat, kept(3)),
     )

time: 93.8 us -> 93.8 us (level)
  transfers between devices with their start and end apart: 1 -> 1, of which waited for: 1 -> 1; matrix products, arithmetic and copies ran while one was open for 0% -> 0% of each run, Pallas kernels for 4% -> 3%
where the time goes in v11:
time: 93.8 us; the launch traced here: 93.6 us
  blocking collectives  61.8 us (66%)
  Pallas kernels  14 us (15%)
  starting transfers between devices  11.5 us (12%)
  waiting for transfers between devices  6.24 us (7%)
    all_to_all x3, blocking collectives, exchange(): moved = lax.all_to_all(parts, AXES, split_axis=0, concat_axis=0, tiled=True)  61.8 us
    pallas_call x6, Pallas kernels, run(): pl.pallas_call(kernel, out_shape=(*(a if last else pltpu.VMEM(a.shape, a....  14 us
    all_to_all x1, starting transfers between devices, body(): lax.all_to_all(asked, AXES, split_axis=0, concat_axis=0, tiled=True)  11.5 us
    all_to_all x1, waiting for transfers between devices, body(): lax.all_to_all(asked, AXES, split_axis=0, concat_axis=0, tiled=True)  6.24 us
  transfers between devices with their start and end apart: 1, of which 1 were waited for; matrix products, arithmetic and copies ran while one was open for 0% of the time, Pallas kernels for 3%

profile of v11, /device:TPU:1, one launch (start us, length us, event | category | flops | bytes accessed | tf_op | source)
XLA Modules:
  0.0 93.6 jit_solution(2510262389768979615)
XLA Ops:
  0.0 2.1 %shard_map.127 = (s32[8,384]{1,0:T(8,128)S(1)}, s32[128,128]{1,0:T(8,128)}) custom-call(s32[1,384]{1,0:T(1,128)} %bitcast.23, s32[1,384]{1,0:T(1,128)} %bitcast.24, s32[1,384]{1,0:T(1,128)} %bitcast.25, s32[384]{0:T(512)} %row0.1, s32[384]{0:T(512)} %row1.1, s32[384]{0:T(512)} %row2.1), custom_call_target="tpu_custom_call" | custom-call | flops 150994944 | bytes 390144 | tf_op jit(solution)/shard_map/pallas_call | solution.py:273
  2.1 11.5 %all-to-all-start = ((s32[128,1,128]{2,1,0:T(1,128)}), s32[128,1,128]{2,1,0:T(1,128)S(1)}, u32[]{:S(2)}, u32[]{:S(2)}) async-start(s32[128,1,128]{2,1,0:T(1,128)} %bitcast.22), calls=%async_computation | async-start | bytes 131072 | tf_op jit(solution)/shard_map/all_to_all | solution.py:353
  13.6 3.3 %shard_map.128 = (bf16[128,512]{1,0:T(8,128)(2,1)S(1)}, bf16[256,512]{1,0:T(8,128)(2,1)S(1)}, bf16[512,512]{1,0:T(8,128)(2,1)S(1)}, bf16[512,512]{1,0:T(8,128)(2...) custom-call(bf16[128,512]{1,0:T(8,128)(2,1)} %grid.1, bf16[128,512]{1,0:T(8,128)(2,1)} %mesh.1, ...), custom_call_target="tpu_custom_call" | custom-call | flops 402653184 | bytes 6185984 | tf_op jit(solution)/shard_map/pallas_call | solution.py:273
  16.9 6.2 %all-to-all-done = s32[128,1,128]{2,1,0:T(1,128)S(1)} async-done(((s32[128,1,128]{2,1,0:T(1,128)}), s32[128,1,128]{2,1,0:T(1,128)S(1)}, u32[]{:S(2)}, u32[]{:S(2)}) %all-to-all-start) | async-done | bytes 65568 | tf_op jit(solution)/shard_map/all_to_all | solution.py:353
  23.1 0.5 shard_map.129
  23.6 20.9 %all_to_all.20 = bf16[128,24,128]{2,1,0:T(8,128)(2,1)S(1)} all-to-all(bf16[128,24,128]{2,1,0:T(8,128)(2,1)S(1)} %bitcast.15), channel_id=1, replica_groups=mesh['band'=8,'patch'=16] {'band','patch'}, dimensions={0} | all-to-all | bytes 1572864 | tf_op jit(solution)/shard_map/all_to_all | solution.py:293
  44.5 2.8 %shard_map.130 = (bf16[3072,128]{1,0:T(8,128)(2,1)S(1)}, bf16[512,512]{1,0:T(8,128)(2,1)S(1)}) custom-call(bf16[3072,128]{1,0:T(8,128)(2,1)S(1)} %bitcast.16, s32[128,128]{1,0:T(8,128)S(1)} %bitcast.18, s32[8,384]{1,0:T(8,128)S(1)} %get-tuple-element.21.lines, s32[8,384]{1,0:T(8,128)S(1)} %get-tuple-element.22.ends, ...), custom_call_target="tpu_custom_call" | custom-call | flops 905969664 | bytes 7028736 | tf_op jit(solution)/shard_map/pallas_call | solution.py:273
  47.3 20.5 %all_to_all.21 = bf16[128,24,128]{2,1,0:T(8,128)(2,1)S(1)} all-to-all(bf16[128,24,128]{2,1,0:T(8,128)(2,1)S(1)} %bitcast.21), channel_id=1, replica_groups=mesh['band'=8,'patch'=16] {'band','patch'}, dimensions={0} | all-to-all | bytes 1572864 | tf_op jit(solution)/shard_map/all_to_all | solution.py:293
  67.8 2.7 %shard_map.131 = (bf16[3072,128]{1,0:T(8,128)(2,1)S(1)}, bf16[384,512]{1,0:T(8,128)(2,1)S(1)}, bf16[512,512]{1,0:T(8,128)(2,1)S(1)}) custom-call(bf16[3072,128]{1,0:T(8,128)(2,1)S(1)} %bitcast.13, s32[128,128]{1,0:T(8,128)S(1)} %bitcast.19, s32[8,384]{1,0:T(8,128)S(1)} %get-tuple-element.21.lines, s32[8,384]{1,0:T(8,128)S(1)} %get-tuple-element.22.ends, ...), custom_call_target="tpu_custom_call" | custom-call | flops 905969664 | bytes 5849088 | tf_op jit(solution)/shard_map/pallas_call | solution.py:273
  70.5 20.5 %all_to_all.22 = bf16[128,24,128]{2,1,0:T(8,128)(2,1)S(1)} all-to-all(bf16[128,24,128]{2,1,0:T(8,128)(2,1)S(1)} %bitcast.20), channel_id=1, replica_groups=mesh['band'=8,'patch'=16] {'band','patch'}, dimensions={0} | all-to-all | bytes 1572864 | tf_op jit(solution)/shard_map/all_to_all | solution.py:293
  91.0 2.6 %shard_map.132 = bf16[128,512]{1,0:T(8,128)(2,1)} custom-call(bf16[3072,128]{1,0:T(8,128)(2,1)S(1)} %bitcast.14, s32[8,384]{1,0:T(8,128)S(1)} %get-tuple-element.21.lines, bf16[384,512]{1,0:T(8,128)(2,1)S(1)} %get-tuple-element.31.kept, bf16[512,512]{1,0:T(8,128)(2,1)S(1)} %get-tuple-element.32.w16, bf16[20,512,512]{2,1,0:T(8,128)(2,1)} %w.7), custom_call_target="tpu_custom_call" | custom-call | flops 905969664 | bytes 3751936 | tf_op jit(solution)/shard_map/pallas_call | solution.py:273
Async XLA Ops:
  2.1 21.0 %all-to-all-start = ((s32[128,1,128]{2,1,0:T(1,128)}), s32[128,1,128]{2,1,0:T(1,128)S(1)}, u32[]{:S(2)}, u32[]{:S(2)}) async-start(s32[128,1,128]{2,1,0:T(1,128)} %bitcast.22), calls=%async_computation | async-start | bytes 131072 | tf_op jit(solution)/shard_map/all_to_all | solution.py:353

commit v12 on v11

--- a/solution.py
+++ b/solution.py
@@ -167,7 +167,7 @@
     copies += start(sems, 2, (w.at[pl.ds(15, 3)], mid))
     fence(spare)
     copies += start(
-        sems, 3, (mesh, m), (w.at[pl.ds(0, 3)], first), (w.at[10], w10), (dst0, e0), (dst1, e1), (src2, e2), (dst2, e3)
+        sems, 3, (mesh, m), (w.at[pl.ds(0, 4)], first), (w.at[10], w10), (dst0, e0), (dst1, e1), (src2, e2), (dst2, e3)
     )
     fence(spare)
     wait(*copies[:2])
@@ -181,6 +181,7 @@
     wait(*copies[3:])
     table[...] = dot(g[...], first[0]).astype(BF)
     kept[:count, :] = dot(m[...], first[1]).astype(BF)
+    kept[2 * count :, :] = dot(m[...], first[3]).astype(BF)
     w2[...] = centred(first[2])
     w10[...] = centred(w10[...])
     for n, row in enumerate((e0, e1, e2, e3)):
@@ -193,13 +194,13 @@
 
 
 def enc_kernel(
-    cap, received, asked, lines, ends, kept, w2, w, out, proc_kept, w34, w5, w89, w11, wide, rows, sems
+    cap, received, asked, lines, ends, kept, w2, w, out, proc_kept, w45, w89, w11, wide, rows, sems
 ):
-    copies = start(sems, 0, (w.at[pl.ds(3, 2)], w34), (w.at[5], w5))
+    copies = start(sems, 0, (w.at[pl.ds(4, 2)], w45))
     fence(wide)
-    copies += start(sems, 2, (w.at[pl.ds(8, 2)], w89), (w.at[11], w11))
+    copies += start(sems, 1, (w.at[pl.ds(8, 2)], w89), (w.at[11], w11))
     fence(wide)
-    count = kept.shape[0] // 2
+    count = kept.shape[0] // 3
     others = asked.shape[0]
     pick = choose(lines[0:1, :], cap * others)
     to = choose(ends[0:1, :], count)
@@ -209,11 +210,9 @@
     message = finish(summed, w2[...], True).astype(BF)
     summed = dot(to_t, message).astype(BF)
     wait(copies[0])
-    m = kept[count:, :]
-    summed = dot(jnp.concatenate([m, summed], axis=1), w34[...].reshape(2 * m.shape[1], m.shape[1]))
-    wait(copies[1])
-    mine = residual(m, finish(summed, w5[...]))
-    wait(*copies[2:])
+    summed = kept[2 * count :, :].astype(F32) + dot(summed, w45[0])
+    mine = residual(kept[count : 2 * count, :], finish(summed, w45[1]))
+    wait(*copies[1:])
     table = dot(mine, w89[0]).astype(BF)
     serve(asked[...], 1, cap, table, wide, out)
     proc_kept[:count, :] = dot(mine, w89[1]).astype(BF)
@@ -353,9 +352,9 @@
     wanted = lax.all_to_all(asked, AXES, split_axis=0, concat_axis=0, tiled=True).reshape(devices, LANES)
     table, enc_kept, w2, w10, ends, w16_far, dec_far = run(
         prepare_kernel,
-        (nodes, kept(2), mat, mat, lines),
+        (nodes, kept(3), mat, mat, lines),
         far=(grid_latent, mesh_latent, enc_dst, proc_dst, loc_src, loc_dst, weights),
-        held=(nodes, row, row, loc, loc, mats(3), mats(2), mats(3), kept(3), spare),
+        held=(nodes, row, row, loc, loc, mats(4), mats(2), mats(3), kept(3), spare),
         copies=12,
         macs=6 * count * width * width,
         away=(mat, kept(3)),
@@ -373,8 +372,8 @@
         (flat, kept(4)),
         near=(enc_rows, wanted, places_of, ends, enc_kept, w2),
         far=(weights,),
-        held=(mats(2), mat, mats(2), mat, flat32, rows),
-        copies=4,
+        held=(mats(2), mats(2), mat, flat32, rows),
+        copies=3,
         macs=edge_macs,
     )
     proc_rows = exchange(sent, devices)

time: 93.8 us -> 93.7 us (level)
  no operation moved by 1% of the time
where the time goes in v12:
time: 93.7 us; the launch traced here: 93.5 us
  blocking collectives  61.8 us (66%)
  Pallas kernels  13.9 us (15%)
  starting transfers between devices  11.5 us (12%)
  waiting for transfers between devices  6.24 us (7%)
    all_to_all x3, blocking collectives, exchange(): moved = lax.all_to_all(parts, AXES, split_axis=0, concat_axis=0, tiled=True)  61.8 us
    pallas_call x6, Pallas kernels, run(): pl.pallas_call(kernel, out_shape=(*(a if last else pltpu.VMEM(a.shape, a....  13.9 us
    all_to_all x1, starting transfers between devices, body(): lax.all_to_all(asked, AXES, split_axis=0, concat_axis=0, tiled=True)  11.5 us
    all_to_all x1, waiting for transfers between devices, body(): lax.all_to_all(asked, AXES, split_axis=0, concat_axis=0, tiled=True)  6.24 us
  transfers between devices with their start and end apart: 1, of which 1 were waited for; matrix products, arithmetic and copies ran while one was open for 0% of the time, Pallas kernels for 3%

profile of v12, /device:TPU:1, one launch (start us, length us, event | category | flops | bytes accessed | tf_op | source)
XLA Modules:
  0.0 93.5 jit_solution(4579106268611219446)
XLA Ops:
  0.0 2.1 %shard_map.127 = (s32[8,384]{1,0:T(8,128)S(1)}, s32[128,128]{1,0:T(8,128)}) custom-call(s32[1,384]{1,0:T(1,128)} %bitcast.23, s32[1,384]{1,0:T(1,128)} %bitcast.24, s32[1,384]{1,0:T(1,128)} %bitcast.25, s32[384]{0:T(512)} %row0.1, s32[384]{0:T(512)} %row1.1, s32[384]{0:T(512)} %row2.1), custom_call_target="tpu_custom_call" | custom-call | flops 150994944 | bytes 390144 | tf_op jit(solution)/shard_map/pallas_call | solution.py:272
  2.1 11.5 %all-to-all-start = ((s32[128,1,128]{2,1,0:T(1,128)}), s32[128,1,128]{2,1,0:T(1,128)S(1)}, u32[]{:S(2)}, u32[]{:S(2)}) async-start(s32[128,1,128]{2,1,0:T(1,128)} %bitcast.22), calls=%async_computation | async-start | bytes 131072 | tf_op jit(solution)/shard_map/all_to_all | solution.py:352
  13.6 3.3 %shard_map.128 = (bf16[128,512]{1,0:T(8,128)(2,1)S(1)}, bf16[384,512]{1,0:T(8,128)(2,1)S(1)}, bf16[512,512]{1,0:T(8,128)(2,1)S(1)}, bf16[512,512]{1,0:T(8,128)(2...) custom-call(bf16[128,512]{1,0:T(8,128)(2,1)} %grid.1, bf16[128,512]{1,0:T(8,128)(2,1)} %mesh.1, ...), custom_call_target="tpu_custom_call" | custom-call | flops 402653184 | bytes 6841344 | tf_op jit(solution)/shard_map/pallas_call | solution.py:272
  16.9 6.2 %all-to-all-done = s32[128,1,128]{2,1,0:T(1,128)S(1)} async-done(((s32[128,1,128]{2,1,0:T(1,128)}), s32[128,1,128]{2,1,0:T(1,128)S(1)}, u32[]{:S(2)}, u32[]{:S(2)}) %all-to-all-start) | async-done | bytes 65568 | tf_op jit(solution)/shard_map/all_to_all | solution.py:352
  23.1 0.5 shard_map.129
  23.6 20.9 %all_to_all.20 = bf16[128,24,128]{2,1,0:T(8,128)(2,1)S(1)} all-to-all(bf16[128,24,128]{2,1,0:T(8,128)(2,1)S(1)} %bitcast.15), channel_id=1, replica_groups=mesh['band'=8,'patch'=16] {'band','patch'}, dimensions={0} | all-to-all | bytes 1572864 | tf_op jit(solution)/shard_map/all_to_all | solution.py:292
  44.5 2.7 %shard_map.130 = (bf16[3072,128]{1,0:T(8,128)(2,1)S(1)}, bf16[512,512]{1,0:T(8,128)(2,1)S(1)}) custom-call(bf16[3072,128]{1,0:T(8,128)(2,1)S(1)} %bitcast.16, s32[128,128]{1,0:T(8,128)S(1)} %bitcast.18, s32[8,384]{1,0:T(8,128)S(1)} %get-tuple-element.21.lines, s32[8,384]{1,0:T(8,128)S(1)} %get-tuple-element.22.ends, ...), custom_call_target="tpu_custom_call" | custom-call | flops 905969664 | bytes 6504448 | tf_op jit(solution)/shard_map/pallas_call | solution.py:272
  47.2 20.5 %all_to_all.21 = bf16[128,24,128]{2,1,0:T(8,128)(2,1)S(1)} all-to-all(bf16[128,24,128]{2,1,0:T(8,128)(2,1)S(1)} %bitcast.21), channel_id=1, replica_groups=mesh['band'=8,'patch'=16] {'band','patch'}, dimensions={0} | all-to-all | bytes 1572864 | tf_op jit(solution)/shard_map/all_to_all | solution.py:292
  67.7 2.7 %shard_map.131 = (bf16[3072,128]{1,0:T(8,128)(2,1)S(1)}, bf16[384,512]{1,0:T(8,128)(2,1)S(1)}, bf16[512,512]{1,0:T(8,128)(2,1)S(1)}) custom-call(bf16[3072,128]{1,0:T(8,128)(2,1)S(1)} %bitcast.13, s32[128,128]{1,0:T(8,128)S(1)} %bitcast.19, s32[8,384]{1,0:T(8,128)S(1)} %get-tuple-element.21.lines, s32[8,384]{1,0:T(8,128)S(1)} %get-tuple-element.22.ends, ...), custom_call_target="tpu_custom_call" | custom-call | flops 905969664 | bytes 5849088 | tf_op jit(solution)/shard_map/pallas_call | solution.py:272
  70.4 20.5 %all_to_all.22 = bf16[128,24,128]{2,1,0:T(8,128)(2,1)S(1)} all-to-all(bf16[128,24,128]{2,1,0:T(8,128)(2,1)S(1)} %bitcast.20), channel_id=1, replica_groups=mesh['band'=8,'patch'=16] {'band','patch'}, dimensions={0} | all-to-all | bytes 1572864 | tf_op jit(solution)/shard_map/all_to_all | solution.py:292
  90.9 2.6 %shard_map.132 = bf16[128,512]{1,0:T(8,128)(2,1)} custom-call(bf16[3072,128]{1,0:T(8,128)(2,1)S(1)} %bitcast.14, s32[8,384]{1,0:T(8,128)S(1)} %get-tuple-element.21.lines, bf16[384,512]{1,0:T(8,128)(2,1)S(1)} %get-tuple-element.31.kept, bf16[512,512]{1,0:T(8,128)(2,1)S(1)} %get-tuple-element.32.w16, bf16[20,512,512]{2,1,0:T(8,128)(2,1)} %w.7), custom_call_target="tpu_custom_call" | custom-call | flops 905969664 | bytes 3751936 | tf_op jit(solution)/shard_map/pallas_call | solution.py:272
Async XLA Ops:
  2.1 21.0 %all-to-all-start = ((s32[128,1,128]{2,1,0:T(1,128)}), s32[128,1,128]{2,1,0:T(1,128)S(1)}, u32[]{:S(2)}, u32[]{:S(2)}) async-start(s32[128,1,128]{2,1,0:T(1,128)} %bitcast.22), calls=%async_computation | async-start | bytes 131072 | tf_op jit(solution)/shard_map/all_to_all | solution.py:352

commit v13 on v12

--- a/solution.py
+++ b/solution.py
@@ -197,9 +197,7 @@
     cap, received, asked, lines, ends, kept, w2, w, out, proc_kept, w45, w89, w11, wide, rows, sems
 ):
     copies = start(sems, 0, (w.at[pl.ds(4, 2)], w45))
-    fence(wide)
     copies += start(sems, 1, (w.at[pl.ds(8, 2)], w89), (w.at[11], w11))
-    fence(wide)
     count = kept.shape[0] // 3
     others = asked.shape[0]
     pick = choose(lines[0:1, :], cap * others)
@@ -225,9 +223,7 @@
     cap, local, received, asked, lines, ends, kept, w10, w, dec_far, w16_far, out, dec_kept, w16, ws, wide, rows, sems
 ):
     copies = start(sems, 0, (w.at[pl.ds(12, 3)], ws))
-    fence(wide)
     copies += start(sems, 1, (dec_far, dec_kept), (w16_far, w16))
-    fence(wide)
     count = kept.shape[0] // 4
     others = asked.shape[0]
     pick = choose(lines[1:2, :], cap * others)

time: 93.7 us -> 93.7 us (level)
  no operation moved by 1% of the time
where the time goes in v13:
time: 93.7 us; the launch traced here: 93.5 us
  blocking collectives  61.8 us (66%)
  Pallas kernels  13.9 us (15%)
  starting transfers between devices  11.5 us (12%)
  waiting for transfers between devices  6.24 us (7%)
    all_to_all x3, blocking collectives, exchange(): moved = lax.all_to_all(parts, AXES, split_axis=0, concat_axis=0, tiled=True)  61.8 us
    pallas_call x6, Pallas kernels, run(): pl.pallas_call(kernel, out_shape=(*(a if last else pltpu.VMEM(a.shape, a....  13.9 us
    all_to_all x1, starting transfers between devices, body(): lax.all_to_all(asked, AXES, split_axis=0, concat_axis=0, tiled=True)  11.5 us
    all_to_all x1, waiting for transfers between devices, body(): lax.all_to_all(asked, AXES, split_axis=0, concat_axis=0, tiled=True)  6.24 us
  transfers between devices with their start and end apart: 1, of which 1 were waited for; matrix products, arithmetic and copies ran while one was open for 0% of the time, Pallas kernels for 3%

profile of v13, /device:TPU:1, one launch (start us, length us, event | category | flops | bytes accessed | tf_op | source)
XLA Modules:
  0.0 93.5 jit_solution(1269081235514926189)
XLA Ops:
  0.0 2.1 %shard_map.127 = (s32[8,384]{1,0:T(8,128)S(1)}, s32[128,128]{1,0:T(8,128)}) custom-call(s32[1,384]{1,0:T(1,128)} %bitcast.23, s32[1,384]{1,0:T(1,128)} %bitcast.24, s32[1,384]{1,0:T(1,128)} %bitcast.25, s32[384]{0:T(512)} %row0.1, s32[384]{0:T(512)} %row1.1, s32[384]{0:T(512)} %row2.1), custom_call_target="tpu_custom_call" | custom-call | flops 150994944 | bytes 390144 | tf_op jit(solution)/shard_map/pallas_call | solution.py:268
  2.1 11.5 %all-to-all-start = ((s32[128,1,128]{2,1,0:T(1,128)}), s32[128,1,128]{2,1,0:T(1,128)S(1)}, u32[]{:S(2)}, u32[]{:S(2)}) async-start(s32[128,1,128]{2,1,0:T(1,128)} %bitcast.22), calls=%async_computation | async-start | bytes 131072 | tf_op jit(solution)/shard_map/all_to_all | solution.py:348
  13.6 3.3 %shard_map.128 = (bf16[128,512]{1,0:T(8,128)(2,1)S(1)}, bf16[384,512]{1,0:T(8,128)(2,1)S(1)}, bf16[512,512]{1,0:T(8,128)(2,1)S(1)}, bf16[512,512]{1,0:T(8,128)(2...) custom-call(bf16[128,512]{1,0:T(8,128)(2,1)} %grid.1, bf16[128,512]{1,0:T(8,128)(2,1)} %mesh.1, ...), custom_call_target="tpu_custom_call" | custom-call | flops 402653184 | bytes 6841344 | tf_op jit(solution)/shard_map/pallas_call | solution.py:268
  16.9 6.2 %all-to-all-done = s32[128,1,128]{2,1,0:T(1,128)S(1)} async-done(((s32[128,1,128]{2,1,0:T(1,128)}), s32[128,1,128]{2,1,0:T(1,128)S(1)}, u32[]{:S(2)}, u32[]{:S(2)}) %all-to-all-start) | async-done | bytes 65568 | tf_op jit(solution)/shard_map/all_to_all | solution.py:348
  23.1 0.5 shard_map.129
  23.6 20.9 %all_to_all.20 = bf16[128,24,128]{2,1,0:T(8,128)(2,1)S(1)} all-to-all(bf16[128,24,128]{2,1,0:T(8,128)(2,1)S(1)} %bitcast.15), channel_id=1, replica_groups=mesh['band'=8,'patch'=16] {'band','patch'}, dimensions={0} | all-to-all | bytes 1572864 | tf_op jit(solution)/shard_map/all_to_all | solution.py:288
  44.5 2.7 %shard_map.130 = (bf16[3072,128]{1,0:T(8,128)(2,1)S(1)}, bf16[512,512]{1,0:T(8,128)(2,1)S(1)}) custom-call(bf16[3072,128]{1,0:T(8,128)(2,1)S(1)} %bitcast.16, s32[128,128]{1,0:T(8,128)S(1)} %bitcast.18, s32[8,384]{1,0:T(8,128)S(1)} %get-tuple-element.21.lines, s32[8,384]{1,0:T(8,128)S(1)} %get-tuple-element.22.ends, ...), custom_call_target="tpu_custom_call" | custom-call | flops 905969664 | bytes 6504448 | tf_op jit(solution)/shard_map/pallas_call | solution.py:268
  47.2 20.5 %all_to_all.21 = bf16[128,24,128]{2,1,0:T(8,128)(2,1)S(1)} all-to-all(bf16[128,24,128]{2,1,0:T(8,128)(2,1)S(1)} %bitcast.21), channel_id=1, replica_groups=mesh['band'=8,'patch'=16] {'band','patch'}, dimensions={0} | all-to-all | bytes 1572864 | tf_op jit(solution)/shard_map/all_to_all | solution.py:288
  67.7 2.7 %shard_map.131 = (bf16[3072,128]{1,0:T(8,128)(2,1)S(1)}, bf16[384,512]{1,0:T(8,128)(2,1)S(1)}, bf16[512,512]{1,0:T(8,128)(2,1)S(1)}) custom-call(bf16[3072,128]{1,0:T(8,128)(2,1)S(1)} %bitcast.13, s32[128,128]{1,0:T(8,128)S(1)} %bitcast.19, s32[8,384]{1,0:T(8,128)S(1)} %get-tuple-element.21.lines, s32[8,384]{1,0:T(8,128)S(1)} %get-tuple-element.22.ends, ...), custom_call_target="tpu_custom_call" | custom-call | flops 905969664 | bytes 5849088 | tf_op jit(solution)/shard_map/pallas_call | solution.py:268
  70.4 20.5 %all_to_all.22 = bf16[128,24,128]{2,1,0:T(8,128)(2,1)S(1)} all-to-all(bf16[128,24,128]{2,1,0:T(8,128)(2,1)S(1)} %bitcast.20), channel_id=1, replica_groups=mesh['band'=8,'patch'=16] {'band','patch'}, dimensions={0} | all-to-all | bytes 1572864 | tf_op jit(solution)/shard_map/all_to_all | solution.py:288
  90.9 2.6 %shard_map.132 = bf16[128,512]{1,0:T(8,128)(2,1)} custom-call(bf16[3072,128]{1,0:T(8,128)(2,1)S(1)} %bitcast.14, s32[8,384]{1,0:T(8,128)S(1)} %get-tuple-element.21.lines, bf16[384,512]{1,0:T(8,128)(2,1)S(1)} %get-tuple-element.31.kept, bf16[512,512]{1,0:T(8,128)(2,1)S(1)} %get-tuple-element.32.w16, bf16[20,512,512]{2,1,0:T(8,128)(2,1)} %w.7), custom_call_target="tpu_custom_call" | custom-call | flops 905969664 | bytes 3751936 | tf_op jit(solution)/shard_map/pallas_call | solution.py:268
Async XLA Ops:
  2.1 21.0 %all-to-all-start = ((s32[128,1,128]{2,1,0:T(1,128)}), s32[128,1,128]{2,1,0:T(1,128)S(1)}, u32[]{:S(2)}, u32[]{:S(2)}) async-start(s32[128,1,128]{2,1,0:T(1,128)} %bitcast.22), calls=%async_computation | async-start | bytes 131072 | tf_op jit(solution)/shard_map/all_to_all | solution.py:348
